TPU v7x, 128 devices: a whole 4x4x4 slice. The times are simulated.
128 devices in a mesh: ctx: 16 (over y, z_lo, core), fsdp: 8 (over z_hi, x).
Axes of the slice: x: 4, y: 4, z: 4 (z_hi: 2, z_lo: 2; z = z_hi * 2 + z_lo), core: 2. Of those that a mesh axis runs over, the one named last changes fastest.
Arguments:
- tokens: bfloat16 [8, 4096, 576], P('fsdp', 'ctx'), may hold values from -6 to 6
- block_order: int32 [32], replicated, may hold values from 0 to 31, as said below
- doc_ids: int32 [8, 4096], P('fsdp'), may hold values from 0 to 4, as said below
- norm_gains: bfloat16 [2, 2, 576], P(None, None, 'fsdp'), may hold values from 0.5 to 1.5
- w_qkv: bfloat16 [2, 576, 960], P(None, 'fsdp'), may hold values from -0.25 to 0.25
- w_out: bfloat16 [2, 576, 576], P(None, 'fsdp'), may hold values from -3 to 3
- w_gate_up: bfloat16 [2, 576, 3072], P(None, 'fsdp'), may hold values from -0.25 to 0.25
- w_down: bfloat16 [2, 1536, 576], P(None, 'fsdp'), may hold values from -0.15625 to 0.15625
- cotangent: bfloat16 [8, 4096, 576], P('fsdp', 'ctx'), may hold values from -6 to 6
Outputs:
- output: bfloat16 [8, 4096, 576], P('fsdp', 'ctx')
- input_grad: float32 [8, 4096, 576], P('fsdp', 'ctx')
- gain_grad: float32 [2, 2, 576], P(None, None, 'fsdp')
- qkv_grad: float32 [2, 576, 960], P(None, 'fsdp')
- out_proj_grad: float32 [2, 576, 576], P(None, 'fsdp')
- gate_up_grad: float32 [2, 576, 3072], P(None, 'fsdp')
- down_grad: float32 [2, 1536, 576], P(None, 'fsdp')
Inputs may be any that keep to these rules, and one draw needn't show every extreme that they name: `block_order`: entries 2 c and 2 c + 1 add up to 31, and every block number appears once. `doc_ids`: non-decreasing along each sequence; document 0 covers at least the first 2176 positions; the last position has id 4.
All inputs are finite; a program needn't handle non-finite values.
Results may differ from a plain program's by a relative error of at most 0.025.
Values may be sent and summed in bfloat16 or wider, within the bound.
No kernel may reach another device: no remote copies, remote signals or barrier semaphores. Data moves between devices by JAX's collectives and lax.ppermute only.
A program may use at most 192 MiB of HBM per device.

v0:
```python
import jax
import jax.numpy as jnp
from jax import lax
from jax.sharding import PartitionSpec as P

D = 576
HEADS = 9
KV_HEADS = 3
HEAD_DIM = 64
FF = 1536
LAYERS = 2
BLK = 128


EPS = 1e-05
THETA = 100000.0
NEG = -1e30


def side_by_side(arrays, axis, dim, along):
    ends, at = ([], 0)
    for a in arrays[:-1]:
        at += a.shape[along]
        ends.append(at)
    both = jnp.concatenate(arrays, axis=along)
    return tuple(jnp.split(lax.all_gather(both, axis, axis=dim, tiled=True), ends, axis=along))


def sent_together(arrays, axis, dim, along):
    ends, at = ([], 0)
    for a in arrays[:-1]:
        at += a.shape[along]
        ends.append(at)
    both = jnp.concatenate(arrays, axis=along)
    return tuple(
        jnp.split(lax.psum_scatter(both, axis, scatter_dimension=dim, tiled=True), ends, axis=along)
    )


def rope_tables(positions):
    half_dim = HEAD_DIM // 2
    freq_idx = jnp.arange(half_dim, dtype=jnp.float32)
    inv_freq = THETA ** (-freq_idx / half_dim)
    angles = positions.astype(jnp.float32)[:, None] * inv_freq[None, :]
    return (jnp.cos(angles), jnp.sin(angles))


def rotate(vectors, cosine, sine_t):
    half_dim = HEAD_DIM // 2
    lower_half = vectors[..., :half_dim]
    second = vectors[..., half_dim:]
    cos_b = cosine[:, None, :]
    sin_b = sine_t[:, None, :]
    return jnp.concatenate(
        [lower_half * cos_b - second * sin_b, second * cos_b + lower_half * sin_b], -1
    )


def normed(hidden):
    inv_rms = lax.rsqrt(jnp.mean(hidden * hidden, -1, keepdims=True) + EPS)
    return (hidden * inv_rms, inv_rms)


def norm_back(d_unit, unit_val, inv_rms):
    return inv_rms * (d_unit - unit_val * jnp.mean(d_unit * unit_val, -1, keepdims=True))


def local(tokens, block_order, doc_ids, norm_gains, w_qkv, w_out, w_gate_up, w_down, cotangent):
    tok_rows = tokens.shape[1]
    seq_len = tok_rows * lax.axis_size("ctx")
    key_rows = min(512, seq_len)
    key_steps = seq_len // key_rows
    groups = HEADS // KV_HEADS
    q_width = HEADS * HEAD_DIM
    kv_width = KV_HEADS * HEAD_DIM
    factor = HEAD_DIM ** (-0.5)
    places = jnp.arange(seq_len, dtype=jnp.int32)
    pos_all = block_order[places // BLK] * BLK + places % BLK
    doc_all = doc_ids[0][pos_all]
    row_start = lax.axis_index("ctx") * tok_rows
    pos_mine = lax.dynamic_slice_in_dim(pos_all, row_start, tok_rows)
    doc_mine = lax.dynamic_slice_in_dim(doc_all, row_start, tok_rows)
    cosine, sine_t = rope_tables(pos_mine)
    pos_blocks = pos_all.reshape(key_steps, key_rows)
    doc_blocks = doc_all.reshape(key_steps, key_rows)

    def allowed_mask(pos_keys, doc_keys):
        return (doc_mine[:, None] == doc_keys[None, :]) & (pos_keys[None, :] <= pos_mine[:, None])

    def block_scores(queries, key_part, allowed):
        scores = (
            jnp.einsum("qkgd,nkd->kgqn", queries, key_part, preferred_element_type=jnp.float32)
            * factor
        )
        return jnp.where(allowed[None, None], scores, NEG)

    def split_kv(kv_all):
        key_all = kv_all[:, :kv_width].reshape(key_steps, key_rows, KV_HEADS, HEAD_DIM)
        val_all = kv_all[:, kv_width:].reshape(key_steps, key_rows, KV_HEADS, HEAD_DIM)
        return (key_all, val_all)

    def attention_back(queries, kv_all, log_total, d_out4, row_delta):
        key_all, val_all = split_kv(kv_all)

        def back_step(dq_in, pieces):
            key_part, val_part, pos_keys, doc_keys = pieces
            allowed = allowed_mask(pos_keys, doc_keys)
            prob_f = jnp.exp(block_scores(queries, key_part, allowed) - log_total[..., None])
            d_prob = jnp.einsum(
                "qkgd,nkd->kgqn", d_out4, val_part, preferred_element_type=jnp.float32
            )
            d_score = (prob_f * (d_prob - row_delta[..., None])).astype(jnp.bfloat16)
            dq_next = dq_in + jnp.einsum(
                "kgqn,nkd->qkgd", d_score, key_part, preferred_element_type=jnp.float32
            )
            d_key = (
                jnp.einsum("kgqn,qkgd->nkd", d_score, queries, preferred_element_type=jnp.float32)
                * factor
            )
            d_val = jnp.einsum(
                "kgqn,qkgd->nkd",
                prob_f.astype(jnp.bfloat16),
                d_out4,
                preferred_element_type=jnp.float32,
            )
            return (
                dq_next,
                jnp.concatenate(
                    [d_key.reshape(key_rows, kv_width), d_val.reshape(key_rows, kv_width)], 1
                ),
            )

        start_dq = jnp.zeros((tok_rows, KV_HEADS, groups, HEAD_DIM), jnp.float32)
        dq_sum, dkv_blocks = lax.scan(
            back_step, start_dq, (key_all, val_all, pos_blocks, doc_blocks)
        )
        return (dq_sum * factor, dkv_blocks.reshape(seq_len, 2 * kv_width))

    hidden = tokens[0].astype(jnp.float32)
    saved = []
    for layer_idx in range(LAYERS):
        wqkv, wout, wgu, wdown, gain_pair = (
            *side_by_side((w_qkv[layer_idx], w_out[layer_idx], w_gate_up[layer_idx]), "fsdp", 0, 1),
            lax.all_gather(w_down[layer_idx], "fsdp", axis=0, tiled=True),
            lax.all_gather(norm_gains[layer_idx], "fsdp", axis=1, tiled=True),
        )
        gain_pair = gain_pair.astype(jnp.float32)
        unit_a, rms_a = normed(hidden)
        attn_in = (unit_a * gain_pair[0]).astype(jnp.bfloat16)
        qkv = jnp.dot(attn_in, wqkv, preferred_element_type=jnp.float32)
        queries = rotate(qkv[:, :q_width].reshape(tok_rows, HEADS, HEAD_DIM), cosine, sine_t)
        queries = queries.astype(jnp.bfloat16).reshape(tok_rows, KV_HEADS, groups, HEAD_DIM)
        key_mine = rotate(
            qkv[:, q_width : q_width + kv_width].reshape(tok_rows, KV_HEADS, HEAD_DIM),
            cosine,
            sine_t,
        )
        kv_local = jnp.concatenate(
            [
                key_mine.reshape(tok_rows, kv_width).astype(jnp.bfloat16),
                qkv[:, q_width + kv_width :].astype(jnp.bfloat16),
            ],
            1,
        )
        kv_all = lax.all_gather(kv_local, "ctx", axis=0, tiled=True)
        attention_key_all, attention_val_all = split_kv(kv_all)

        def stat_step(carry_in, pieces):
            key_part, pos_keys, doc_keys = pieces
            allowed = allowed_mask(pos_keys, doc_keys)
            scores = block_scores(queries, key_part, allowed)
            new_top = jnp.maximum(carry_in[0], jnp.max(scores, -1))
            new_sum = carry_in[1] * jnp.exp(carry_in[0] - new_top) + jnp.sum(
                jnp.exp(scores - new_top[..., None]), -1
            )
            return ((new_top, new_sum), None)

        start_top = jnp.full((KV_HEADS, groups, tok_rows), NEG, jnp.float32)
        start_sum = jnp.zeros((KV_HEADS, groups, tok_rows), jnp.float32)
        (row_top, row_sum), unused = lax.scan(
            stat_step, (start_top, start_sum), (attention_key_all, pos_blocks, doc_blocks)
        )
        attention_log_total = row_top + jnp.log(row_sum)

        def out_step(acc_in, pieces):
            key_part, val_part, pos_keys, doc_keys = pieces
            allowed = allowed_mask(pos_keys, doc_keys)
            prob_b = jnp.exp(
                block_scores(queries, key_part, allowed) - attention_log_total[..., None]
            ).astype(jnp.bfloat16)
            return (
                acc_in
                + jnp.einsum(
                    "kgqn,nkd->qkgd", prob_b, val_part, preferred_element_type=jnp.float32
                ),
                None,
            )

        start_acc = jnp.zeros((tok_rows, KV_HEADS, groups, HEAD_DIM), jnp.float32)
        mixed, unused = lax.scan(
            out_step, start_acc, (attention_key_all, attention_val_all, pos_blocks, doc_blocks)
        )
        log_total = attention_log_total
        mixed_f = mixed.reshape(tok_rows, q_width)
        attn_out = mixed_f.astype(jnp.bfloat16)
        mid_h = hidden + jnp.dot(attn_out, wout, preferred_element_type=jnp.float32)
        unit_m, rms_m = normed(mid_h)
        mlp_in = (unit_m * gain_pair[1]).astype(jnp.bfloat16)
        gate_up = jnp.dot(mlp_in, wgu, preferred_element_type=jnp.float32)
        inner_act = (jax.nn.silu(gate_up[:, :FF]) * gate_up[:, FF:]).astype(jnp.bfloat16)
        kv_saved = kv_local
        saved.append(
            (
                wqkv,
                wout,
                wgu,
                wdown,
                gain_pair,
                unit_a,
                rms_a,
                attn_in,
                queries,
                kv_saved,
                log_total,
                mixed_f,
                attn_out,
                unit_m,
                rms_m,
                mlp_in,
                gate_up,
                inner_act,
            )
        )
        hidden = mid_h + jnp.dot(inner_act, wdown, preferred_element_type=jnp.float32)
    output = hidden.astype(jnp.bfloat16).reshape(1, tok_rows, D)
    d_hidden = cotangent[0].astype(jnp.float32)
    grads_rev = []
    for layer_idx in reversed(range(LAYERS)):
        (
            wqkv,
            wout,
            wgu,
            wdown,
            gain_pair,
            unit_a,
            rms_a,
            attn_in,
            queries,
            kv_saved,
            log_total,
            mixed_f,
            attn_out,
            unit_m,
            rms_m,
            mlp_in,
            gate_up,
            inner_act,
        ) = saved[layer_idx]
        grad_b = d_hidden.astype(jnp.bfloat16)
        d_wdown = jnp.einsum("tf,td->fd", inner_act, grad_b, preferred_element_type=jnp.float32)
        d_inner = jnp.einsum("td,fd->tf", grad_b, wdown, preferred_element_type=jnp.float32)
        gate_part = gate_up[:, :FF]
        up_part = gate_up[:, FF:]
        sigmoid_g = jax.nn.sigmoid(gate_part)
        d_gate = d_inner * up_part * sigmoid_g * (1.0 + gate_part * (1.0 - sigmoid_g))
        d_up = d_inner * (gate_part * sigmoid_g)
        d_gu = jnp.concatenate([d_gate, d_up], 1).astype(jnp.bfloat16)
        d_wgu = jnp.einsum("td,tf->df", mlp_in, d_gu, preferred_element_type=jnp.float32)
        d_norm = jnp.einsum("tf,df->td", d_gu, wgu, preferred_element_type=jnp.float32)
        d_gain_m = jnp.sum(d_norm * unit_m, 0)
        d_hidden = d_hidden + norm_back(d_norm * gain_pair[1], unit_m, rms_m)
        grad_b = d_hidden.astype(jnp.bfloat16)
        d_wout = jnp.einsum("ta,td->ad", attn_out, grad_b, preferred_element_type=jnp.float32)
        d_out = jnp.einsum("td,ad->ta", grad_b, wout, preferred_element_type=jnp.float32).astype(
            jnp.bfloat16
        )
        d_out4 = d_out.reshape(tok_rows, KV_HEADS, groups, HEAD_DIM)
        row_delta = jnp.sum(
            d_out4.astype(jnp.float32) * mixed_f.reshape(tok_rows, KV_HEADS, groups, HEAD_DIM), -1
        )
        row_delta = jnp.transpose(row_delta, (1, 2, 0))
        kv_back = lax.all_gather(kv_saved, "ctx", axis=0, tiled=True)
        d_query, dkv_all = attention_back(queries, kv_back, log_total, d_out4, row_delta)
        dkv_mine = lax.psum_scatter(
            dkv_all.astype(jnp.bfloat16), "ctx", scatter_dimension=0, tiled=True
        ).astype(jnp.float32)
        dq_pre = rotate(d_query.reshape(tok_rows, HEADS, HEAD_DIM), cosine, -sine_t)
        dk_pre = rotate(
            dkv_mine[:, :kv_width].reshape(tok_rows, KV_HEADS, HEAD_DIM), cosine, -sine_t
        )
        d_qkv = jnp.concatenate(
            [
                dq_pre.reshape(tok_rows, q_width),
                dk_pre.reshape(tok_rows, kv_width),
                dkv_mine[:, kv_width:],
            ],
            1,
        ).astype(jnp.bfloat16)
        d_wqkv = jnp.einsum("td,te->de", attn_in, d_qkv, preferred_element_type=jnp.float32)
        d_norm = jnp.einsum("te,de->td", d_qkv, wqkv, preferred_element_type=jnp.float32)
        d_gain_a = jnp.sum(d_norm * unit_a, 0)
        d_hidden = d_hidden + norm_back(d_norm * gain_pair[0], unit_a, rms_a)
        d_gains = jnp.stack([d_gain_a, d_gain_m])
        shares = (
            *tuple(
                (
                    part.astype(jnp.float32)
                    for part in sent_together(
                        (
                            d_wqkv.astype(jnp.bfloat16),
                            d_wout.astype(jnp.bfloat16),
                            d_wgu.astype(jnp.bfloat16),
                        ),
                        "fsdp",
                        0,
                        1,
                    )
                )
            ),
            lax.psum_scatter(
                d_wdown.astype(jnp.bfloat16), "fsdp", scatter_dimension=0, tiled=True
            ).astype(jnp.float32),
            lax.psum_scatter(
                d_gains.astype(jnp.bfloat16), "fsdp", scatter_dimension=1, tiled=True
            ).astype(jnp.float32),
        )
        shares = (
            lax.psum(shares[0].astype(jnp.bfloat16), "ctx").astype(jnp.float32),
            lax.psum(shares[1].astype(jnp.bfloat16), "ctx").astype(jnp.float32),
            lax.psum(shares[2].astype(jnp.bfloat16), "ctx").astype(jnp.float32),
            lax.psum(shares[3].astype(jnp.bfloat16), "ctx").astype(jnp.float32),
            lax.psum(shares[4].astype(jnp.bfloat16), "ctx").astype(jnp.float32),
        )
        grads_rev.append(shares)
    grads_fwd = grads_rev[::-1]
    gain_grad = jnp.stack([item[4] for item in grads_fwd])
    qkv_grad = jnp.stack([item[0] for item in grads_fwd])
    out_proj_grad = jnp.stack([item[1] for item in grads_fwd])
    gate_up_grad = jnp.stack([item[2] for item in grads_fwd])
    down_grad = jnp.stack([item[3] for item in grads_fwd])
    input_grad = d_hidden.reshape(1, tok_rows, D)
    return (output, input_grad, gain_grad, qkv_grad, out_proj_grad, gate_up_grad, down_grad)


def solution(mesh):
    in_specs = (
        P("fsdp", "ctx", None),
        P(),
        P("fsdp", None),
        P(None, None, "fsdp"),
        P(None, "fsdp", None),
        P(None, "fsdp", None),
        P(None, "fsdp", None),
        P(None, "fsdp", None),
        P("fsdp", "ctx", None),
    )
    out_specs = (
        P("fsdp", "ctx", None),
        P("fsdp", "ctx", None),
        P(None, None, "fsdp"),
        P(None, "fsdp", None),
        P(None, "fsdp", None),
        P(None, "fsdp", None),
        P(None, "fsdp", None),
    )
    return jax.shard_map(local, mesh=mesh, in_specs=in_specs, out_specs=out_specs, check_vma=False)
```

profile of v0, /device:TPU:1, one launch (start us, length us, event | category | flops | bytes accessed | tf_op | source)
XLA Modules:
  0.0 1311.8 jit_solution(9222217486396801556)
XLA Ops:
  11.9 30.7 %all-gather = bf16[1,2,576]{1,0,2:T(2,128)(2,1)S(1)} all-gather(bf16[1,2,72]{1,0,2:T(2,128)(2,1)S(1)} %copy.190), channel_id=2, replica_groups=mesh['ctx'=16,'fsdp'=8] {'fsdp'}, dimensions={2}, use_global_device_ids=true | all-gather | bytes 2592 | tf_op jit(solution)/shard_map/all_gather | solution.py:145
  45.8 4.5 compare_select_fusion.2
  50.4 15.6 %select_multiply_fusion.2 = s32[4096]{0:T(1024)S(1)} fusion(pred[4096]{0:T(1024)(128)(4,1)S(1)} %compare_reduce_fusion, pred[4096]{0:T(1024)(128)(4,1)S(1)} %compare_reduce_fusion.1, pred[4096]{0:T(1024)(128)(4,1)S(1)} %compare_reduce_fusion.2, pred[4096]{0:T(1024)(128)(4,1)S(1)} %compare_reduce_fusion.3, pred[4096]{0:T(1024)(128)(4,1)S(1)} %compare_reduce_fusion.4, ...), kind=kLoop, calls=%fused_computation.318 | loop fusion | flops 106496 | bytes 135268 | tf_op jit(solution)/shard_map/mul | solution.py:78
  70.8 25.7 %all-gather.11.cloned.1.call-done = bf16[576,4608]{1,0:T(8,128)(2,1)} async-done(((bf16[72,4608]{1,0:T(8,128)(2,1)}), bf16[576,4608]{1,0:T(8,128)(2,1)}) %all-gather.11.cloned.1.call-update) | async-done | bytes 5308432 | tf_op jit(solution)/shard_map/all_gather | solution.py:26
  101.9 23.0 %gather_fusion = s32[4096]{0:T(1024)S(1)} fusion(s32[4096]{0:T(1024)S(1)} %bitcast.519, s32[4096]{0:T(1024)S(1)} %broadcast_clamp_fusion), kind=kCustom, calls=%fused_computation | custom fusion | bytes 49152 | tf_op jit(solution)/shard_map/gather | solution.py:79
  126.4 28.4 %all-gather.2 = bf16[1,2,576]{1,0,2:T(2,128)(2,1)S(1)} all-gather(bf16[1,2,72]{1,0,2:T(2,128)(2,1)S(1)} %copy.191), channel_id=4, replica_groups=mesh['ctx'=16,'fsdp'=8] {'fsdp'}, dimensions={2}, use_global_device_ids=true | all-gather | bytes 2592 | tf_op jit(solution)/shard_map/all_gather | solution.py:145
  163.0 73.6 %while.74 = (s32[]{:T(128)}, f32[3,3,256]{2,1,0:T(4,128)S(1)}, f32[3,3,256]{2,1,0:T(4,128)S(1)}, s32[256]{0:T(256)S(1)}, s32[8,512]{1,0:T(8,128)}, /*index=5*/s3...) while((s32[]{:T(128)}, f32[3,3,256]{2,1,0:T(4,128)S(1)}, ...), condition=%wide.region_4.5_spmd.clone, body=%wide.region_1.4_spmd.clone.sunk | while | flops 159657216 | bytes 10456200 | solution.py:180
  165.1 4.0 fusion.264
  174.2 4.0 fusion.264
  183.2 4.0 fusion.264
  192.3 4.0 fusion.264
  201.3 4.0 fusion.264
  210.7 4.0 fusion.264
  219.8 4.0 fusion.264
  228.8 4.0 fusion.264
  232.9 3.7 exponential_reduce_fusion.4
  237.8 34.7 %while.75 = (s32[]{:T(128)}, f32[256,3,3,64]{0,3,2,1:T(8,128)S(1)}, bf16[8,512,3,64]{1,3,2,0:T(8,128)(2,1)S(1)}, s32[256]{0:T(256)S(1)}, s32[8,512]{1,0:T(8,128)...) while((s32[]{:T(128)}, f32[256,3,3,64]{0,3,2,1:T(8,128)S(1)}, ...), condition=%wide.region_6.7_spmd.clone, body=%wide.region_5.6_spmd.clone.sunk | while | flops 307396608 | bytes 2158218 | solution.py:200
  276.0 3.7 fusion.110
  288.7 44.0 %all-gather.17.cloned.1.call-done = bf16[4096,384]{0,1:T(8,128)(2,1)} async-done(((bf16[256,384]{0,1:T(8,128)(2,1)}), bf16[4096,384]{0,1:T(8,128)(2,1)}) %all-gather.17.cloned.1.call-update) | async-done | bytes 3145744 | tf_op jit(solution)/shard_map/all_gather | solution.py:165
  339.6 72.5 %while.76 = (s32[]{:T(128)}, f32[3,3,256]{2,1,0:T(4,128)S(1)}, f32[3,3,256]{2,1,0:T(4,128)S(1)}, s32[256]{0:T(256)S(1)}, s32[8,512]{1,0:T(8,128)}, /*index=5*/s3...) while((s32[]{:T(128)}, f32[3,3,256]{2,1,0:T(4,128)S(1)}, ...), condition=%wide.region_12.13_spmd.clone, body=%wide.region_9.12_spmd.clone.sunk | while | flops 159657216 | bytes 10456200 | solution.py:180
  341.3 4.0 fusion.272
  350.4 4.0 fusion.272
  359.5 4.0 fusion.272
  368.5 4.0 fusion.272
  377.6 4.0 fusion.272
  386.7 4.0 fusion.272
  395.7 4.0 fusion.272
  404.7 4.0 fusion.272
  412.1 35.4 %while.77 = (s32[]{:T(128)}, f32[256,3,3,64]{0,3,2,1:T(8,128)S(1)}, bf16[8,512,3,64]{1,3,2,0:T(8,128)(2,1)}, s32[256]{0:T(256)S(1)}, s32[8,512]{1,0:T(8,128)}, /...) while((s32[]{:T(128)}, f32[256,3,3,64]{0,3,2,1:T(8,128)S(1)}, ...), condition=%wide.region_14.15_spmd.clone, body=%wide.region_13.14_spmd.clone.sunk | while | flops 307396608 | bytes 2155146 | solution.py:200
  450.5 5.5 fusion.106
  455.9 4.6 multiply_convert_fusion.3
  460.5 4.4 multiply_reduce_fusion
  471.8 102.2 %while.78 = (s32[]{:T(128)}, f32[256,3,3,64]{0,3,2,1:T(8,128)S(1)}, bf16[8,512,384]{2,1,0:T(8,128)(2,1)}, bf16[8,512,3,64]{1,3,2,0:T(8,128)(2,1)}, s32[256]{0:T(...) while((s32[]{:T(128)}, f32[256,3,3,64]{0,3,2,1:T(8,128)S(1)}, ...), condition=%wide.region_19.20_spmd.clone, body=%wide.region_18.19_spmd.clone.sunk | while | flops 768442368 | bytes 66278772 | solution.py:134
  574.0 4.7 copy.155
  579.7 61.3 %reduce-scatter.9.cloned.1.call-done = bf16[256,384]{0,1:T(8,128)(2,1)} async-done(((bf16[4096,384]{0,1:T(8,128)(2,1)}), bf16[256,384]{0,1:T(8,128)(2,1)}) %reduce-scatter.9.cloned.1.call-update) | async-done | bytes 196624 | tf_op jit(solution)/shard_map/reduce_scatter | solution.py:284
  653.3 101.1 %while.79 = (s32[]{:T(128)}, f32[256,3,3,64]{0,3,2,1:T(8,128)S(1)}, bf16[8,512,384]{2,1,0:T(8,128)(2,1)}, bf16[8,512,3,64]{1,3,2,0:T(8,128)(2,1)}, s32[256]{0:T(...) while((s32[]{:T(128)}, f32[256,3,3,64]{0,3,2,1:T(8,128)S(1)}, ...), condition=%wide.region_25.26_spmd.clone, body=%wide.region_24.25_spmd.clone.sunk | while | flops 768442368 | bytes 66409820 | solution.py:134
  754.4 4.8 copy.159
  760.8 4.5 convolution_convert_fusion
  765.8 8.4 concatenate.103
  777.9 45.7 %reduce-scatter.11.cloned.1.call-done = bf16[256,384]{0,1:T(8,128)(2,1)} async-done(((bf16[4096,384]{0,1:T(8,128)(2,1)}), bf16[256,384]{0,1:T(8,128)(2,1)}) %reduce-scatter.11.cloned.1.call-update) | async-done | bytes 196624 | tf_op jit(solution)/shard_map/reduce_scatter | solution.py:284
  828.7 7.9 concatenate.102
  842.5 79.0 %reduce-scatter.15.cloned.1.call-done = bf16[72,4608]{1,0:T(8,128)(2,1)} async-done(((bf16[576,4608]{1,0:T(8,128)(2,1)}), bf16[72,4608]{1,0:T(8,128)(2,1)}) %reduce-scatter.15.cloned.1.call-update) | async-done | bytes 663568 | tf_op jit(solution)/shard_map/reduce_scatter | solution.py:36
  926.5 89.7 %reduce-scatter.13.cloned.1.call-done = bf16[72,4608]{1,0:T(8,128)(2,1)} async-done(((bf16[576,4608]{1,0:T(8,128)(2,1)}), bf16[72,4608]{1,0:T(8,128)(2,1)}) %reduce-scatter.13.cloned.1.call-update) | async-done | bytes 663568 | tf_op jit(solution)/shard_map/reduce_scatter | solution.py:36
  1021.4 71.9 %reduce-scatter.19.cloned.1.call-done = bf16[192,576]{1,0:T(8,128)(2,1)} async-done(((bf16[1536,576]{1,0:T(8,128)(2,1)}), bf16[192,576]{1,0:T(8,128)(2,1)}) %reduce-scatter.19.cloned.1.call-update) | async-done | bytes 221200 | tf_op jit(solution)/shard_map/reduce_scatter | solution.py:320
  1093.3 77.7 %reduce-scatter.17.cloned.1.call-done = bf16[192,576]{1,0:T(8,128)(2,1)} async-done(((bf16[1536,576]{1,0:T(8,128)(2,1)}), bf16[192,576]{1,0:T(8,128)(2,1)}) %reduce-scatter.17.cloned.1.call-update) | async-done | bytes 221200 | tf_op jit(solution)/shard_map/reduce_scatter | solution.py:320
  1177.5 18.1 %all-reduce.4 = (bf16[2,576]{1,0:T(2,128)(2,1)S(1)}, bf16[2,576]{1,0:T(2,128)(2,1)S(1)}) all-reduce(bf16[2,576]{1,0:T(2,128)(2,1)S(1)} %pad_maximum_fusion.23, bf16[2,576]{1,0:T(2,128)(2,1)S(1)} %pad_maximum_fusion.22), channel_id=9, replica_groups=mesh['ctx'=16,'fsdp'=8] {'fsdp'}, use_global_device_ids=true, to_apply=%region_34.35.clone | all-reduce | flops 2304 | bytes 9216
  1195.7 32.2 %all-reduce.2 = (bf16[1,2,72]{2,1,0:T(2,128)(2,1)S(1)}, bf16[1,2,72]{2,1,0:T(2,128)(2,1)S(1)}) all-reduce(bf16[1,2,72]{2,1,0:T(2,128)(2,1)S(1)} %get-tuple-element.1202, bf16[1,2,72]{2,1,0:T(2,128)(2,1)S(1)} %get-tuple-element.1201), channel_id=1, replica_groups=mesh['ctx'=16,'fsdp'=8] {'ctx'}, use_global_device_ids=true, to_apply=%region_35.36 | all-reduce | flops 288 | bytes 1152 | tf_op jit(solution)/shard_map/psum | solution.py:332
  1229.5 68.2 %all-reduce.7.cloned.1.call-done = (bf16[1,72,960]{2,1,0:T(8,128)(2,1)}, bf16[1,72,960]{2,1,0:T(8,128)(2,1)}, bf16[1,72,576]{2,1,0:T(8,128)(2,1)}, bf16[1,72,576...) async-done(((bf16[1,72,960]{2,1,0:T(8,128)(2,1)}, ...) | async-done | bytes 1769488 | tf_op jit(solution)/shard_map/psum | solution.py:328
  (887 shorter events, 458.8 us)
Async XLA Ops:
  7.2 94.7 %copy-start = (s32[1,4096]{1,0:T(1,128)S(1)}, s32[1,4096]{1,0:T(1,128)}, u32[]{:S(2)}) copy-start(s32[1,4096]{1,0:T(1,128)} %param.23) | copy-start | bytes 49156
  7.2 37.2 %copy-start.58 = (s32[32]{0:T(128)S(1)}, s32[32]{0:T(128)}, u32[]{:S(2)}) copy-start(s32[32]{0:T(128)} %param.22) | copy-start | bytes 388
  7.2 59.5 %copy-start.42 = (bf16[1,256,576]{1,2,0:T(8,128)(2,1)S(1)}, bf16[1,256,576]{1,2,0:T(8,128)(2,1)}, u32[]{:S(2)}) copy-start(bf16[1,256,576]{1,2,0:T(8,128)(2,1)} %param.21) | copy-start | bytes 884740
  7.2 89.3 %all-gather.11.cloned.1.call-start = ((), (), s32[]{:S(2)}) async-start(), calls=%async_computation.6 | async-start | bytes 5971968 | tf_op jit(solution)/shard_map/all_gather | solution.py:26
  11.7 146.8 %all-gather.13.cloned.1.call-start = ((), (), s32[]{:S(2)}) async-start(), calls=%async_computation.7 | async-start | bytes 3342336 | tf_op jit(solution)/shard_map/all_gather | solution.py:165
  42.6 57.0 %copy-start.59 = (bf16[2,192,576]{2,1,0:T(8,128)(2,1)S(1)}, bf16[2,192,576]{2,1,0:T(8,128)(2,1)}, u32[]{:S(2)}) copy-start(bf16[2,192,576]{2,1,0:T(8,128)(2,1)} %param.28) | copy-start | bytes 1327108
  70.0 31.7 %copy-start.83 = (f32[576]{0:T(1024)}, f32[576]{0:T(1024)S(1)}, u32[]{:S(2)}) copy-start(f32[576]{0:T(1024)S(1)} %get-tuple-element.958) | copy-start | bytes 6916
  70.0 206.0 %copy-start.63 = (f32[576]{0:T(1024)}, f32[576]{0:T(1024)S(1)}, u32[]{:S(2)}) copy-start(f32[576]{0:T(1024)S(1)} %get-tuple-element.957) | copy-start | bytes 6916
  70.0 31.7 %copy-start.97 = (f32[256]{0:T(256)}, f32[256]{0:T(256)S(1)}, u32[]{:S(2)}) copy-start(f32[256]{0:T(256)S(1)} %add_rsqrt_fusion.3) | copy-start | bytes 3076
  70.8 217.8 %copy-start.33 = (f32[256,32]{0,1:T(8,128)}, f32[256,32]{0,1:T(8,128)S(1)}, u32[]{:S(2)}) copy-start(f32[256,32]{0,1:T(8,128)S(1)} %get-tuple-element.1156) | copy-start | bytes 98308
  99.5 182.3 %all-gather.19.cloned.1.call-start = ((), (), s32[]{:S(2)}) async-start(), calls=%async_computation.16 | async-start | bytes 2211840 | tf_op jit(solution)/shard_map/all_gather | solution.py:144
  100.4 184.2 %all-gather.15.cloned.1.call-start = ((), (), s32[]{:S(2)}) async-start(), calls=%async_computation.8 | async-start | bytes 5971968 | tf_op jit(solution)/shard_map/all_gather | solution.py:26
  101.7 231.0 %all-gather.17.cloned.1.call-start = ((), (), s32[]{:S(2)}) async-start(), calls=%async_computation.9 | async-start | bytes 3342336 | tf_op jit(solution)/shard_map/all_gather | solution.py:165
  101.9 56.4 %copy-start.51 = (f32[256,960]{0,1:T(8,128)S(1)}, f32[256,960]{0,1:T(8,128)}, u32[]{:S(2)}) copy-start(f32[256,960]{0,1:T(8,128)} %copy-done.50) | copy-start | bytes 2949124
  158.3 126.3 %copy-start.75 = (f32[576]{0:T(1024)}, f32[576]{0:T(1024)S(1)}, u32[]{:S(2)}) copy-start(f32[576]{0:T(1024)S(1)} %get-tuple-element.956) | copy-start | bytes 6916
  158.3 306.6 %copy-start.65 = (f32[576]{0:T(1024)}, f32[576]{0:T(1024)S(1)}, u32[]{:S(2)}) copy-start(f32[576]{0:T(1024)S(1)} %get-tuple-element.955) | copy-start | bytes 6916
  237.8 35.9 %copy-start.43 = (bf16[1,256,576]{1,2,0:T(8,128)(2,1)S(1)}, bf16[1,256,576]{1,2,0:T(8,128)(2,1)}, u32[]{:S(2)}) copy-start(bf16[1,256,576]{1,2,0:T(8,128)(2,1)} %param.21) | copy-start | bytes 884740
  284.6 163.6 %copy-start.21 = (f32[256,576]{0,1:T(8,128)}, f32[256,576]{0,1:T(8,128)S(1)}, u32[]{:S(2)}) copy-start(f32[256,576]{0,1:T(8,128)S(1)} %get-tuple-element.1194) | copy-start | bytes 1769476
  287.7 168.2 %all-gather.21.cloned.1.call-start = ((), (), s32[]{:S(2)}) async-start(), calls=%async_computation.17 | async-start | bytes 2211840 | tf_op jit(solution)/shard_map/all_gather | solution.py:144
  288.3 352.7 %reduce-scatter.9.cloned.1.call-start = ((), (), s32[]{:S(2)}) async-start(), calls=%async_computation.10 | async-start | bytes 3342336 | tf_op jit(solution)/shard_map/reduce_scatter | solution.py:284
  339.6 72.5 %copy-start.37 = (f32[256,3,3,64]{0,3,2,1:T(8,128)S(1)}, f32[256,3,3,64]{0,3,2,1:T(8,128)}, u32[]{:S(2)}) copy-start(f32[256,3,3,64]{0,3,2,1:T(8,128)} %custom-call.5) | copy-start | bytes 1769476
  450.4 14.5 %copy-start.7 = (f32[256,576]{0,1:T(8,128)}, f32[256,576]{0,1:T(8,128)S(1)}, u32[]{:S(2)}) copy-start(f32[256,576]{0,1:T(8,128)S(1)} %get-tuple-element.1196) | copy-start | bytes 1769476
  578.8 63.2 %copy-start.22 = (f32[256,576]{0,1:T(8,128)S(1)}, f32[256,576]{0,1:T(8,128)}, u32[]{:S(2)}) copy-start(f32[256,576]{0,1:T(8,128)} %copy-done.21) | copy-start | bytes 1769476
  578.8 63.2 %copy-start.76 = (f32[576]{0:T(1024)S(1)}, f32[576]{0:T(1024)}, u32[]{:S(2)}) copy-start(f32[576]{0:T(1024)} %copy-done.75) | copy-start | bytes 6916
  578.8 63.2 %copy-start.95 = (f32[256]{0:T(256)S(1)}, f32[256]{0:T(256)}, u32[]{:S(2)}) copy-start(f32[256]{0:T(256)} %copy-done.94) | copy-start | bytes 3076
  578.8 244.8 %reduce-scatter.11.cloned.1.call-start = ((), (), s32[]{:S(2)}) async-start(), calls=%async_computation.11 | async-start | bytes 3342336 | tf_op jit(solution)/shard_map/reduce_scatter | solution.py:284
  579.6 65.0 %copy-start.19 = (f32[256,576]{0,1:T(8,128)S(1)}, f32[256,576]{0,1:T(8,128)}, u32[]{:S(2)}) copy-start(f32[256,576]{0,1:T(8,128)} %copy-done.18) | copy-start | bytes 1769476
  579.7 65.0 %copy-start.60 = (bf16[256,9,64]{0,2,1:T(8,128)(2,1)}, bf16[256,9,64]{0,2,1:T(8,128)(2,1)S(1)}, u32[]{:S(2)}) copy-start(bf16[256,9,64]{0,2,1:T(8,128)(2,1)S(1)} %pad_maximum_fusion.10) | copy-start | bytes 884740
  759.2 162.3 %reduce-scatter.15.cloned.1.call-start = ((), (), s32[]{:S(2)}) async-start(), calls=%async_computation.13 | async-start | bytes 5971968 | tf_op jit(solution)/shard_map/reduce_scatter | solution.py:36
  774.3 241.9 %reduce-scatter.13.cloned.1.call-start = ((), (), s32[]{:S(2)}) async-start(), calls=%async_computation.12 | async-start | bytes 5971968 | tf_op jit(solution)/shard_map/reduce_scatter | solution.py:36
  776.8 49.3 %copy-start.84 = (f32[576]{0:T(1024)S(1)}, f32[576]{0:T(1024)}, u32[]{:S(2)}) copy-start(f32[576]{0:T(1024)} %copy-done.83) | copy-start | bytes 6916
  776.8 49.3 %copy-start.98 = (f32[256]{0:T(256)S(1)}, f32[256]{0:T(256)}, u32[]{:S(2)}) copy-start(f32[256]{0:T(256)} %copy-done.97) | copy-start | bytes 3076
  836.6 256.6 %reduce-scatter.19.cloned.1.call-start = ((), (), s32[]{:S(2)}) async-start(), calls=%async_computation.15 | async-start | bytes 2211840 | tf_op jit(solution)/shard_map/reduce_scatter | solution.py:320
  839.9 331.1 %reduce-scatter.17.cloned.1.call-start = ((), (), s32[]{:S(2)}) async-start(), calls=%async_computation.14 | async-start | bytes 2211840 | tf_op jit(solution)/shard_map/reduce_scatter | solution.py:320
  842.1 328.9 %copy-start.104 = (u32[128]{0:T(128)S(1)}, u32[128]{0:T(128)}, u32[]{:S(2)}) copy-start(u32[128]{0:T(128)} %constant.213) | copy-start | bytes 1540
  842.1 330.2 %copy-start.100 = (bf16[576]{0:T(1024)(128)(2,1)S(1)}, bf16[576]{0:T(1024)(128)(2,1)}, u32[]{:S(2)}) copy-start(bf16[576]{0:T(1024)(128)(2,1)} %get-tuple-element.951) | copy-start | bytes 3460
  842.1 330.2 %copy-start.9 = (f32[256,576]{0,1:T(8,128)S(1)}, f32[256,576]{0,1:T(8,128)}, u32[]{:S(2)}) copy-start(f32[256,576]{0,1:T(8,128)} %copy-done.7) | copy-start | bytes 1769476
  842.1 455.6 %all-reduce.7.cloned.1.call-start = ((), (), s32[]{:S(2)}) async-start(), calls=%async_computation.18 | async-start | bytes 3710976 | tf_op jit(solution)/shard_map/psum | solution.py:328
  1019.5 156.0 %copy-start.101 = (bf16[576]{0:T(1024)(128)(2,1)S(1)}, bf16[576]{0:T(1024)(128)(2,1)}, u32[]{:S(2)}) copy-start(bf16[576]{0:T(1024)(128)(2,1)} %get-tuple-element.949) | copy-start | bytes 3460
  1019.5 156.0 %copy-start.102 = (bf16[576]{0:T(1024)(128)(2,1)S(1)}, bf16[576]{0:T(1024)(128)(2,1)}, u32[]{:S(2)}) copy-start(bf16[576]{0:T(1024)(128)(2,1)} %get-tuple-element.947) | copy-start | bytes 3460
  1019.5 156.0 %copy-start.44 = (bf16[1,256,576]{1,2,0:T(8,128)(2,1)S(1)}, bf16[1,256,576]{1,2,0:T(8,128)(2,1)}, u32[]{:S(2)}) copy-start(bf16[1,256,576]{1,2,0:T(8,128)(2,1)} %param.21) | copy-start | bytes 884740
  1019.5 156.0 %copy-start.62 = (bf16[256,9,64]{0,2,1:T(8,128)(2,1)S(1)}, bf16[256,9,64]{0,2,1:T(8,128)(2,1)}, u32[]{:S(2)}) copy-start(bf16[256,9,64]{0,2,1:T(8,128)(2,1)} %pad_maximum_fusion.11) | copy-start | bytes 884740
  1019.5 156.0 %copy-start.70 = (bf16[256,3,64]{0,2,1:T(8,128)(2,1)S(1)}, bf16[256,3,64]{0,2,1:T(8,128)(2,1)}, u32[]{:S(2)}) copy-start(bf16[256,3,64]{0,2,1:T(8,128)(2,1)} %copy-done.69) | copy-start | bytes 294916
  1019.5 156.0 %copy-start.74 = (bf16[256,192]{0,1:T(8,128)(2,1)S(1)}, bf16[256,192]{0,1:T(8,128)(2,1)}, u32[]{:S(2)}) copy-start(bf16[256,192]{0,1:T(8,128)(2,1)} %copy-done.73) | copy-start | bytes 294916
  1019.5 156.0 %copy-start.99 = (f32[256]{0:T(256)S(1)}, f32[256]{0:T(256)}, u32[]{:S(2)}) copy-start(f32[256]{0:T(256)} %copy-done.97) | copy-start | bytes 3076
  1175.4 53.1 %copy-start.17 = (f32[256,576]{0,1:T(8,128)S(1)}, f32[256,576]{0,1:T(8,128)}, u32[]{:S(2)}) copy-start(f32[256,576]{0,1:T(8,128)} %copy-done.15) | copy-start | bytes 1769476
  1175.4 53.1 %copy-start.85 = (f32[576]{0:T(1024)S(1)}, f32[576]{0:T(1024)}, u32[]{:S(2)}) copy-start(f32[576]{0:T(1024)} %copy-done.83) | copy-start | bytes 6916
  1228.5 76.3 %copy-start.1 = (s32[1,4096]{1,0:T(1,128)S(1)}, s32[1,4096]{1,0:T(1,128)}, u32[]{:S(2)}) copy-start(s32[1,4096]{1,0:T(1,128)} %param.23) | copy-start | bytes 49156
  (163 other events, 506.9 us)
Sparse Core Ops, SparseCore 0:
  11.8 84.6 all-gather.10
  99.7 39.6 all-gather.12
  142.3 52.6 all-gather.18
  197.2 80.3 all-gather.14
  287.8 44.8 all-gather.16
  335.4 52.6 all-gather.20
  578.9 61.9 reduce-scatter.8
  759.3 64.2 reduce-scatter.10
  827.5 93.9 reduce-scatter.14
  925.3 90.9 reduce-scatter.12
  1020.1 73.1 reduce-scatter.18
  1096.9 74.0 reduce-scatter.16
  1174.7 122.9 all-reduce.6
where the time goes:
time: 1330 us; the launch traced here: 1310 us
  waiting for transfers between devices  564 us (42%)
  matrix products  310 us (23%)
  local copies, waits for them, and re-layouts  169 us (13%)
  other arithmetic  137 us (10%)
  blocking collectives  109 us (8%)
  between operations  16.6 us (1%)
    reduce_scatter x2, waiting for transfers between devices, sent_together(): lax.psum_scatter(both, axis, scatter_dimension=dim, tiled=True)  169 us
    reduce_scatter x2, waiting for transfers between devices, local(): lax.psum_scatter(d_wdown.astype(jnp.bfloat16), 'fsdp', scatter_dimension=...  150 us
    reduce_scatter x2, waiting for transfers between devices, local(): lax.psum_scatter(dkv_all.astype(jnp.bfloat16), 'ctx', scatter_dimension=0...  107 us
    dot_general x32, matrix products, block_scores(): jnp.einsum('qkgd,nkd->kgqn', queries, key_part, preferred_element_type=jn...  92.7 us
    psum x1, waiting for transfers between devices, local(): lax.psum(shares[0].astype(jnp.bfloat16), 'ctx').astype(jnp.float32)  68.2 us
    all_gather x2, blocking collectives, local(): lax.all_gather(norm_gains[layer_idx], 'fsdp', axis=1, tiled=True)  59.1 us
    reduce_sum x16, other arithmetic, stat_step(): jnp.sum(jnp.exp(scores - new_top[..., None]), -1)  54 us
    all_gather x2, waiting for transfers between devices, local(): kv_all = lax.all_gather(kv_local, 'ctx', axis=0, tiled=True)  44 us
  transfers between devices with their start and end apart: 13, of which 9 were waited for; matrix products, arithmetic and copies ran while one was open for 27% of the time, Pallas kernels for 0%

commit v1 on v0

v1 whole, which is shorter than its diff:
```python
import functools

import jax
import jax.numpy as jnp
from jax import lax
from jax.experimental import pallas as pl
from jax.experimental.pallas import tpu as pltpu
from jax.sharding import PartitionSpec as P

D = 576
HEADS = 9
KV_HEADS = 3
GROUP = 3
HEAD_DIM = 64
FF = 1536
LAYERS = 2
BLK = 128
NBLK = 32
EPS = 1e-05
THETA = 100000.0
NEG = -1e30
F32 = jnp.float32
BF16 = jnp.bfloat16
LANES = GROUP * BLK
CTX = 16
FSDP = 8
SHARD = D // FSDP
HALF = FF // 2

PARTNER = [(i, i ^ 1) for i in range(CTX)]
SAME_CORE = [[2 * chip + core for chip in range(CTX // 2)] for core in range(2)]


def to_partner(x):
    return lax.ppermute(x, "ctx", PARTNER)


def over_chips(x):
    return lax.all_to_all(x, "ctx", 0, 0, axis_index_groups=SAME_CORE, tiled=True)


def over_fsdp(x):
    return lax.all_to_all(x, "fsdp", 0, 0, tiled=True)


def dot_tn(a, b):
    return lax.dot_general(a, b, (((0,), (0,)), ((), ())), preferred_element_type=F32)


def dot_nt(a, b):
    return lax.dot_general(a, b, (((1,), (1,)), ((), ())), preferred_element_type=F32)


def fill_keys(sc, own_ref, other_ref, kv_s):
    core = sc[2]
    for chip in range(CTX // 2):
        for half in range(2):
            lanes = slice(half * BLK, (half + 1) * BLK)
            block = sc[7 + 2 * (2 * chip + core) + half]
            kv_s[block] = own_ref[chip, :, 0, :, lanes]
            block = sc[7 + 2 * (2 * chip + 1 - core) + half]
            kv_s[block] = other_ref[chip, :, 0, :, lanes]


def fill_queries(sc, src_ref, dst):
    for half in range(2):
        lanes = slice(half * BLK, (half + 1) * BLK)
        which = jnp.bitwise_xor(half, sc[1])
        dst[which] = jnp.concatenate([src_ref[j, :, lanes] for j in range(GROUP)], axis=1)


def query_rows(sc, which):
    block = jnp.where(which == 0, sc[0], NBLK - 1 - sc[0])
    lane = lax.broadcasted_iota(jnp.int32, (1, LANES), 1)
    pos = block * BLK + jnp.bitwise_and(lane, BLK - 1)
    start = jnp.zeros((1, LANES), jnp.int32)
    for d in range(4):
        start = jnp.where(pos >= sc[3 + d], jnp.maximum(start, sc[3 + d]), start)
    return pos, start


def forward_kernel(sc, q_ref, own_ref, other_ref, o_ref, lse_ref, kv_s, q_s, o_s, acc_s, m_s, l_s):
    fill_keys(sc, own_ref, other_ref, kv_s)
    fill_queries(sc, q_ref, q_s)
    acc_s[...] = jnp.zeros_like(acc_s)
    m_s[...] = jnp.full_like(m_s, NEG)
    l_s[...] = jnp.zeros_like(l_s)
    low = sc[0]
    hi_doc0 = query_rows(sc, 1)[1] == 0
    sub = lax.broadcasted_iota(jnp.int32, (BLK, LANES), 0)

    def update(block, which, slot, valid):
        scores = dot_tn(kv_s[block, 0], q_s[which])
        scores = jnp.where(valid, scores, NEG)
        old = m_s[slot]
        new = jnp.maximum(old, jnp.max(scores, axis=0, keepdims=True))
        prob = jnp.exp(scores - new)
        shrink = jnp.exp(old - new)
        m_s[slot] = new
        l_s[slot] = l_s[slot] * shrink + jnp.sum(prob, axis=0, keepdims=True)
        acc_s[slot] = acc_s[slot] * shrink + jnp.dot(
            kv_s[block, 1], prob.astype(BF16), preferred_element_type=F32
        )

    def masked(block, which):
        pos, start = query_rows(sc, which)
        at = block * BLK + sub
        return (at >= start) & (at <= pos)

    def step(i, carry):
        update(i, 1, 2, hi_doc0)
        which = (i > low).astype(jnp.int32)
        block = jnp.where(i <= low, i, NBLK // 2 - 1 + i - low)
        update(block, which, which, masked(block, which))
        return carry

    lax.fori_loop(0, NBLK // 2, step, 0)
    update(NBLK - 1 - low, 1, 1, masked(NBLK - 1 - low, 1))
    top = jnp.maximum(m_s[1], m_s[2])
    w1, w2 = jnp.exp(m_s[1] - top), jnp.exp(m_s[2] - top)
    total = l_s[1] * w1 + l_s[2] * w2
    o_s[1] = (acc_s[1] * w1 + acc_s[2] * w2) / total
    lse_ref[0, 1] = top + jnp.log(total)
    o_s[0] = acc_s[0] / l_s[0]
    lse_ref[0, 0] = m_s[0] + jnp.log(l_s[0])
    for half in range(2):
        which = jnp.bitwise_xor(half, sc[1])
        mine = o_s[which]
        for j in range(GROUP):
            o_ref[j, :, half * BLK : (half + 1) * BLK] = mine[:, j * BLK : (j + 1) * BLK]


def backward_kernel(
    sc, q_ref, own_ref, other_ref, o_ref, do_ref, lse_ref,
    dq_ref, down_ref, dother_ref,
    kv_s, q_s, do_s, dq_s, dkv_s, delta_s,
):
    fill_keys(sc, own_ref, other_ref, kv_s)
    fill_queries(sc, q_ref, q_s)
    fill_queries(sc, do_ref, do_s)
    fill_queries(sc, o_ref, dq_s)
    for which in range(2):
        delta_s[which] = jnp.sum(dq_s[which] * do_s[which].astype(F32), axis=0, keepdims=True)
    dq_s[...] = jnp.zeros_like(dq_s)
    low = sc[0]
    hi_doc0 = query_rows(sc, 1)[1] == 0
    sub = lax.broadcasted_iota(jnp.int32, (BLK, LANES), 0)

    def tile(block, which, valid):
        key_t, val_t, q_t, do_t = kv_s[block, 0], kv_s[block, 1], q_s[which], do_s[which]
        scores = dot_tn(key_t, q_t)
        prob = jnp.where(valid, jnp.exp(scores - lse_ref[0, which]), 0.0)
        d_prob = dot_tn(val_t, do_t)
        d_score = (prob * (d_prob - delta_s[which])).astype(BF16)
        d_val = dot_nt(do_t, prob.astype(BF16))
        d_key = dot_nt(q_t, d_score)
        d_q = jnp.dot(key_t, d_score, preferred_element_type=F32)
        return d_key, d_val, d_q

    def masked(block, which):
        pos, start = query_rows(sc, which)
        at = block * BLK + sub
        return (at >= start) & (at <= pos)

    zero = jnp.zeros((NBLK // 2,) + dkv_s.shape[1:], F32)
    dkv_s[NBLK // 2 :] = zero

    def step(i, carry):
        d_key, d_val, d_q = tile(i, 1, hi_doc0)
        dq_s[2] = dq_s[2] + d_q
        dkv_s[i, 0] = d_key
        dkv_s[i, 1] = d_val
        which = (i > low).astype(jnp.int32)
        block = jnp.where(i <= low, i, NBLK // 2 - 1 + i - low)
        d_key, d_val, d_q = tile(block, which, masked(block, which))
        dq_s[which] = dq_s[which] + d_q
        dkv_s[block, 0] = dkv_s[block, 0] + d_key
        dkv_s[block, 1] = dkv_s[block, 1] + d_val
        return carry

    lax.fori_loop(0, NBLK // 2, step, 0)
    last = NBLK - 1 - low
    d_key, d_val, d_q = tile(last, 1, masked(last, 1))
    dkv_s[last, 0] = d_key
    dkv_s[last, 1] = d_val
    dq_s[1] = dq_s[1] + dq_s[2] + d_q
    core = sc[2]
    scale = HEAD_DIM**-0.5
    for half in range(2):
        lanes = slice(half * BLK, (half + 1) * BLK)
        which = jnp.bitwise_xor(half, sc[1])
        mine = dq_s[which] * scale
        for j in range(GROUP):
            dq_ref[j, :, lanes] = mine[:, j * BLK : (j + 1) * BLK]
        for chip in range(CTX // 2):
            block = sc[7 + 2 * (2 * chip + core) + half]
            down_ref[chip, :, 0, :, lanes] = dkv_s[block].astype(BF16)
            block = sc[7 + 2 * (2 * chip + 1 - core) + half]
            dother_ref[chip, :, 0, :, lanes] = dkv_s[block].astype(BF16)


ROWS = 2 * BLK
HEAD_SPEC = pl.BlockSpec((GROUP, HEAD_DIM, ROWS), lambda g, sc: (g, 0, 0))
KV_SPEC = pl.BlockSpec((CTX // 2, 2, 1, HEAD_DIM, ROWS), lambda g, sc: (0, 0, g, 0, 0))
LSE_SPEC = pl.BlockSpec((1, 2, 1, LANES), lambda g, sc: (g, 0, 0, 0))
HEAD_SHAPE = jax.ShapeDtypeStruct((HEADS, HEAD_DIM, ROWS), F32)
KV_SHAPE = jax.ShapeDtypeStruct((CTX // 2, 2, KV_HEADS, HEAD_DIM, ROWS), BF16)
LSE_SHAPE = jax.ShapeDtypeStruct((KV_HEADS, 2, 1, LANES), F32)
KERNEL_PARAMS = pltpu.CompilerParams(
    dimension_semantics=("arbitrary",), vmem_limit_bytes=40 * 2**20
)


def attention(scalars, q_t, own, other):
    return pl.pallas_call(
        forward_kernel,
        grid_spec=pltpu.PrefetchScalarGridSpec(
            num_scalar_prefetch=1,
            grid=(KV_HEADS,),
            in_specs=[HEAD_SPEC, KV_SPEC, KV_SPEC],
            out_specs=[HEAD_SPEC, LSE_SPEC],
            scratch_shapes=[
                pltpu.VMEM((NBLK, 2, HEAD_DIM, BLK), BF16),
                pltpu.VMEM((2, HEAD_DIM, LANES), BF16),
                pltpu.VMEM((2, HEAD_DIM, LANES), F32),
                pltpu.VMEM((3, HEAD_DIM, LANES), F32),
                pltpu.VMEM((3, 1, LANES), F32),
                pltpu.VMEM((3, 1, LANES), F32),
            ],
        ),
        out_shape=[HEAD_SHAPE, LSE_SHAPE],
        compiler_params=KERNEL_PARAMS,
        name="attention",
    )(scalars, q_t, own, other)


def attention_back(scalars, q_t, own, other, o_t, do_t, lse):
    return pl.pallas_call(
        backward_kernel,
        grid_spec=pltpu.PrefetchScalarGridSpec(
            num_scalar_prefetch=1,
            grid=(KV_HEADS,),
            in_specs=[HEAD_SPEC, KV_SPEC, KV_SPEC, HEAD_SPEC, HEAD_SPEC, LSE_SPEC],
            out_specs=[HEAD_SPEC, KV_SPEC, KV_SPEC],
            scratch_shapes=[
                pltpu.VMEM((NBLK, 2, HEAD_DIM, BLK), BF16),
                pltpu.VMEM((2, HEAD_DIM, LANES), BF16),
                pltpu.VMEM((2, HEAD_DIM, LANES), BF16),
                pltpu.VMEM((3, HEAD_DIM, LANES), F32),
                pltpu.VMEM((NBLK, 2, HEAD_DIM, BLK), F32),
                pltpu.VMEM((2, 1, LANES), F32),
            ],
        ),
        out_shape=[HEAD_SHAPE, KV_SHAPE, KV_SHAPE],
        compiler_params=KERNEL_PARAMS,
        name="attention_back",
    )(scalars, q_t, own, other, o_t, do_t, lse)


def rotate(x, cosine, sine):
    half = HEAD_DIM // 2
    first, second = x[:, :half], x[:, half:]
    return jnp.concatenate([first * cosine - second * sine, second * cosine + first * sine], 1)


def normed(hidden):
    inv_rms = lax.rsqrt(jnp.mean(hidden * hidden, -1, keepdims=True) + EPS)
    return hidden * inv_rms, inv_rms


def norm_back(d_unit, unit, inv_rms):
    return inv_rms * (d_unit - unit * jnp.mean(d_unit * unit, -1, keepdims=True))


def mm(a, b):
    return jnp.dot(a, b, preferred_element_type=F32)


def ein(spec, a, b):
    return jnp.einsum(spec, a, b, preferred_element_type=F32)


def local(tokens, block_order, doc_ids, norm_gains, w_qkv, w_out, w_gate_up, w_down, cotangent):
    place = lax.axis_index("ctx")
    core = jnp.bitwise_and(place, 1)
    first_core = core == 0
    kv_rows = 2 * KV_HEADS * HEAD_DIM
    q_rows = HEADS * HEAD_DIM

    gain_cols = jnp.transpose(norm_gains.reshape(2 * LAYERS, SHARD))
    proj = jnp.concatenate([w_qkv, w_out], 2)
    proj = jnp.concatenate([jnp.where(first_core, proj[0], proj[1]), gain_cols], 1)
    proj_own = over_fsdp(jnp.broadcast_to(proj[None], (FSDP,) + proj.shape)).reshape(D, -1)
    proj_other = to_partner(proj_own)
    proj_layer = [
        jnp.where(first_core, proj_own, proj_other),
        jnp.where(first_core, proj_other, proj_own),
    ]
    gains = jnp.transpose(proj_own[:, -2 * LAYERS :].astype(F32)).reshape(LAYERS, 2, D)
    wgu_cut = w_gate_up.reshape(LAYERS, SHARD, 2, FSDP, 2, FF // FSDP // 2)
    wgu_cut = jnp.where(first_core, wgu_cut[..., 0, :], wgu_cut[..., 1, :])
    wgu_cut = wgu_cut.reshape(LAYERS, SHARD, FF)
    wd_cut = w_down.reshape(LAYERS, 2, FF // FSDP // 2, D)
    wd_cut = jnp.where(first_core, wd_cut[:, 0], wd_cut[:, 1]).reshape(LAYERS, SHARD, HALF)
    mlp_cut = jnp.concatenate([wgu_cut, wd_cut], 2)
    mlp_own = [lax.all_gather(mlp_cut[l], "fsdp", axis=0, tiled=True) for l in range(LAYERS)]
    mlp_other = [to_partner(w) for w in mlp_own]

    def mlp_weights(layer):
        return [
            (w[:, :FF], w[:, FF:].reshape(HALF, D)) for w in (mlp_own[layer], mlp_other[layer])
        ]

    first_block = lax.dynamic_index_in_dim(block_order, 2 * place, 0, keepdims=False)
    low = jnp.minimum(first_block, NBLK - 1 - first_block)
    low_half = (first_block != low).astype(jnp.int32)
    starts = jnp.sum(
        (doc_ids[0][None, :] < jnp.arange(1, 5, dtype=jnp.int32)[:, None]).astype(jnp.int32), 1
    )
    scalars = jnp.concatenate([jnp.stack([low, low_half, core]), starts, block_order])
    lane = jnp.arange(ROWS, dtype=jnp.int32)
    pos = jnp.where(lane < BLK, first_block, NBLK - 2 - first_block) * BLK + lane
    inv_freq = THETA ** (-jnp.arange(HEAD_DIM // 2, dtype=F32) / (HEAD_DIM // 2))
    angles = pos.astype(F32)[None, :] * inv_freq[:, None]
    cosine, sine = jnp.cos(angles), jnp.sin(angles)

    hidden = tokens[0].astype(F32)
    saved = []
    for layer in range(LAYERS):
        wqkv = proj_layer[layer][:, : q_rows + kv_rows]
        wout = proj_layer[layer][:, q_rows + kv_rows : q_rows + kv_rows + D]
        unit_a, rms_a = normed(hidden)
        attn_in = (unit_a * gains[layer, 0]).astype(BF16)
        qkv_t = ein("de,td->et", wqkv, attn_in).reshape(-1, HEAD_DIM, ROWS)
        turned = rotate(qkv_t[: HEADS + KV_HEADS], cosine, sine)
        q_t = (turned[:HEADS] * HEAD_DIM**-0.5).astype(BF16)
        kv_t = jnp.concatenate([turned[HEADS:], qkv_t[HEADS + KV_HEADS :]], 0).astype(BF16)
        kv_t = kv_t.reshape(1, 2, KV_HEADS, HEAD_DIM, ROWS)
        kv_own = over_chips(jnp.broadcast_to(kv_t, (CTX // 2,) + kv_t.shape[1:]))
        kv_other = to_partner(kv_own)
        o_t, lse = attention(scalars, q_t, kv_own, kv_other)
        attn_out = o_t.astype(BF16).reshape(q_rows, ROWS)
        mid = hidden + ein("at,ad->td", attn_out, wout)
        unit_m, rms_m = normed(mid)
        mlp_in = (unit_m * gains[layer, 1]).astype(BF16)
        hidden = mid
        halves = []
        for wgu, wdown in mlp_weights(layer):
            gate_up = mm(mlp_in, wgu)
            inner = (jax.nn.silu(gate_up[:, :HALF]) * gate_up[:, HALF:]).astype(BF16)
            hidden = hidden + mm(inner, wdown)
            halves.append((wgu, wdown, gate_up, inner))
        saved.append(
            (wqkv, wout, unit_a, rms_a, attn_in, q_t, kv_own, kv_other, o_t, lse, attn_out,
             unit_m, rms_m, mlp_in, halves)
        )
    output = hidden.astype(BF16).reshape(1, ROWS, D)

    d_hidden = cotangent[0].astype(F32)
    mlp_shares = [None] * LAYERS
    proj_grads = [None] * LAYERS
    gain_grads = [None] * LAYERS
    for layer in reversed(range(LAYERS)):
        (wqkv, wout, unit_a, rms_a, attn_in, q_t, kv_own, kv_other, o_t, lse, attn_out,
         unit_m, rms_m, mlp_in, halves) = saved[layer]
        grad_b = d_hidden.astype(BF16)
        d_norm = 0.0
        packs = []
        for wgu, wdown, gate_up, inner in halves:
            d_inner = ein("td,fd->tf", grad_b, wdown)
            gate, up = gate_up[:, :HALF], gate_up[:, HALF:]
            sig = jax.nn.sigmoid(gate)
            d_gate = d_inner * up * sig * (1.0 + gate * (1.0 - sig))
            d_up = d_inner * (gate * sig)
            d_gu = jnp.concatenate([d_gate, d_up], 1).astype(BF16)
            d_norm = d_norm + ein("tf,df->td", d_gu, wgu)
            d_wdown = ein("tf,td->fd", inner, grad_b).astype(BF16)
            d_wgu = ein("td,tf->df", mlp_in, d_gu).astype(BF16)
            packs.append(jnp.concatenate([d_wgu, d_wdown.reshape(D, HALF)], 1))
        both = (packs[0].astype(F32) + to_partner(packs[1]).astype(F32)).astype(BF16)
        mlp_shares[layer] = lax.psum_scatter(both, "fsdp", scatter_dimension=0, tiled=True)
        d_gain_m = jnp.sum(d_norm * unit_m, 0)
        d_hidden = d_hidden + norm_back(d_norm * gains[layer, 1], unit_m, rms_m)
        grad_b = d_hidden.astype(BF16)
        d_wout = mm(attn_out, grad_b)
        do_t = ein("ad,td->at", wout, grad_b).astype(BF16).reshape(HEADS, HEAD_DIM, ROWS)
        dq_t, dkv_own, dkv_other = attention_back(scalars, q_t, kv_own, kv_other, o_t, do_t, lse)
        dkv = (dkv_own.astype(F32) + to_partner(dkv_other).astype(F32)).astype(BF16)
        dkv = jnp.sum(over_chips(dkv).astype(F32), 0)
        turned = jnp.concatenate([dq_t, dkv[0]], 0)
        d_qkv = jnp.concatenate([rotate(turned, cosine, -sine), dkv[1]], 0)
        d_qkv = d_qkv.astype(BF16).reshape(q_rows + kv_rows, ROWS)
        d_wqkv = ein("td,et->de", attn_in, d_qkv)
        d_norm = ein("et,de->td", d_qkv, wqkv)
        d_gain_a = jnp.sum(d_norm * unit_a, 0)
        d_hidden = d_hidden + norm_back(d_norm * gains[layer, 0], unit_a, rms_a)
        gain_grads[layer] = jnp.stack([d_gain_a, d_gain_m])
        proj_grads[layer] = jnp.concatenate([d_wqkv, d_wout], 1).astype(BF16)
    input_grad = d_hidden.reshape(1, ROWS, D)

    own = jnp.where(first_core, proj_grads[0], proj_grads[1])
    other = jnp.where(first_core, proj_grads[1], proj_grads[0])
    d_gains = jnp.transpose(jnp.stack(gain_grads).reshape(2 * LAYERS, D)).astype(BF16)
    own = own.astype(F32) + to_partner(other).astype(F32)
    own = jnp.concatenate([own.astype(BF16), d_gains], 1).reshape(FSDP, SHARD, -1)
    proj_share = jnp.sum(over_fsdp(own).astype(F32), 0)

    share = jnp.concatenate(
        [mlp_shares[0], mlp_shares[1], proj_share.astype(BF16)], 1
    )
    width = share.shape[1]
    pieces = over_chips(share.reshape(CTX // 2, SHARD // 8, width)).astype(F32)
    piece = jnp.sum(pieces.reshape(CTX // 2, SHARD // 8, width), 0).astype(BF16)
    total = over_chips(jnp.broadcast_to(piece[None], (CTX // 2,) + piece.shape)).reshape(SHARD, width)
    theirs = to_partner(total)
    d_gain = total[:, -2 * LAYERS :].astype(F32) + theirs[:, -2 * LAYERS :].astype(F32)
    gain_grad = jnp.transpose(d_gain).reshape(LAYERS, 2, SHARD)
    pair = (jnp.where(first_core, total, theirs), jnp.where(first_core, theirs, total))
    pw = FF + HALF
    proj = jnp.stack([t[:, 2 * pw : 2 * pw + 2 * q_rows + kv_rows] for t in pair]).astype(F32)
    qkv_grad, out_proj_grad = proj[..., : q_rows + kv_rows], proj[..., q_rows + kv_rows :]
    gate_up_grad, down_grad = [], []
    for layer in range(LAYERS):
        mine = [t[:, layer * pw : (layer + 1) * pw] for t in pair]
        cols = jnp.stack([t[:, :FF].reshape(SHARD, 2, FSDP, -1) for t in mine], 3)
        gate_up_grad.append(cols.reshape(SHARD, 2 * FF))
        rows = [t[:, FF:].reshape(FF // FSDP // 2, D) for t in mine]
        down_grad.append(jnp.concatenate(rows, 0))
    gate_up_grad = jnp.stack(gate_up_grad).astype(F32)
    down_grad = jnp.stack(down_grad).astype(F32)
    return (output, input_grad, gain_grad, qkv_grad, out_proj_grad, gate_up_grad, down_grad)


def solution(mesh):
    in_specs = (
        P("fsdp", "ctx", None),
        P(),
        P("fsdp", None),
        P(None, None, "fsdp"),
        P(None, "fsdp", None),
        P(None, "fsdp", None),
        P(None, "fsdp", None),
        P(None, "fsdp", None),
        P("fsdp", "ctx", None),
    )
    out_specs = (
        P("fsdp", "ctx", None),
        P("fsdp", "ctx", None),
        P(None, None, "fsdp"),
        P(None, "fsdp", None),
        P(None, "fsdp", None),
        P(None, "fsdp", None),
        P(None, "fsdp", None),
    )
    return jax.shard_map(local, mesh=mesh, in_specs=in_specs, out_specs=out_specs, check_vma=False)
```

time: 1330 us -> 630 us (0.47)
  waiting for transfers between devices: 564 us -> 143 us
  matrix products: 310 us -> 52.3 us
  Pallas kernels: 0 us -> 142 us
  local copies, waits for them, and re-layouts: 169 us -> 80.5 us
  other arithmetic: 137 us -> 49 us
  starting transfers between devices: 1 us -> 35.2 us
    reduce_scatter x6 -> x2, waiting for transfers between devices: 425 us -> 28.6 us  [local(): lax.psum_scatter(both, 'fsdp', scatter_dimension=0, tiled=True)]
    dot_general x136 -> x36, matrix products: 310 us -> 52.3 us  [the longest x26 38.6 us: ein(): return jnp.einsum(spec, a, b, preferred_element_type=F32)]
    pallas_call x0 -> x4, Pallas kernels: none -> 142 us  [the longest x2 75.3 us: attention_back(): pl.pallas_call(backward_kernel, grid_spec=pltpu.PrefetchScalarGridSpec(nu...]
    all_to_all x0 -> x4, blocking collectives: none -> 102 us  [the longest x3 69.4 us: over_chips(): lax.all_to_all(x, 'ctx', 0, 0, axis_index_groups=SAME_CORE, tiled=True)]
    all_to_all x0 -> x4, waiting for transfers between devices: none -> 75.3 us  [the longest x3 52.9 us: over_chips(): lax.all_to_all(x, 'ctx', 0, 0, axis_index_groups=SAME_CORE, tiled=True)]
    psum x1 -> x0, waiting for transfers between devices: 68.2 us -> none  [local(): lax.psum(shares[0].astype(jnp.bfloat16), 'ctx').astype(jnp.float32)]
    all_gather x2 -> x0, blocking collectives: 59.1 us -> none  [local(): lax.all_gather(norm_gains[layer_idx], 'fsdp', axis=1, tiled=True)]
    reduce_sum x18 -> x5, other arithmetic: 56.3 us -> 5.73 us  [the longest x2 3.36 us: local(): dkv = jnp.sum(over_chips(dkv).astype(F32), 0)]
  transfers between devices with their start and end apart: 13 -> 19, of which waited for: 9 -> 8; matrix products, arithmetic and copies ran while one was open for 27% -> 19% of each run, Pallas kernels for 0% -> 17%
where the time goes in v1:
time: 630 us; the launch traced here: 622 us
  waiting for transfers between devices  143 us (23%)
  Pallas kernels  142 us (23%)
  blocking collectives  102 us (16%)
  local copies, waits for them, and re-layouts  80.5 us (13%)
  matrix products  52.3 us (8%)
  other arithmetic  49 us (8%)
  starting transfers between devices  35.2 us (6%)
  between operations  18.6 us (3%)
    pallas_call x2, Pallas kernels, attention_back(): pl.pallas_call(backward_kernel, grid_spec=pltpu.PrefetchScalarGridSpec(nu...  75.3 us
    all_to_all x3, blocking collectives, over_chips(): lax.all_to_all(x, 'ctx', 0, 0, axis_index_groups=SAME_CORE, tiled=True)  69.4 us
    pallas_call x2, Pallas kernels, attention(): pl.pallas_call(forward_kernel, grid_spec=pltpu.PrefetchScalarGridSpec(num...  66.3 us
    all_to_all x3, waiting for transfers between devices, over_chips(): lax.all_to_all(x, 'ctx', 0, 0, axis_index_groups=SAME_CORE, tiled=True)  52.9 us
    dot_general x26, matrix products, ein(): return jnp.einsum(spec, a, b, preferred_element_type=F32)  38.6 us
    all_gather x2, waiting for transfers between devices, local(): lax.all_gather(mlp_cut[l], 'fsdp', axis=0, tiled=True)  34.2 us
    all_to_all x1, blocking collectives, over_fsdp(): return lax.all_to_all(x, 'fsdp', 0, 0, tiled=True)  32.2 us
    reduce_scatter x2, waiting for transfers between devices, local(): lax.psum_scatter(both, 'fsdp', scatter_dimension=0, tiled=True)  28.6 us
  transfers between devices with their start and end apart: 19, of which 8 were waited for; matrix products, arithmetic and copies ran while one was open for 19% of the time, Pallas kernels for 17%

profile of v1, /device:TPU:1, one launch (start us, length us, event | category | flops | bytes accessed | tf_op | source)
XLA Modules:
  0.0 622.0 jit_solution(2441532279760933653)
XLA Ops:
  10.6 8.3 %all-to-all-start = ((bf16[8,72,1540]{2,1,0:T(8,128)(2,1)}), bf16[8,72,1540]{2,1,0:T(8,128)(2,1)}, u32[]{:S(2)}, u32[]{:S(2)}) async-start(bf16[8,72,1540]{2,1,0:T(8,128)(2,1)} %broadcast_in_dim.16), calls=%async_computation | async-start | bytes 3833856 | tf_op jit(solution)/shard_map/all_to_all | solution.py:43
  23.2 22.3 %all-to-all-done = bf16[8,72,1540]{2,1,0:T(8,128)(2,1)} async-done(((bf16[8,72,1540]{2,1,0:T(8,128)(2,1)}), bf16[8,72,1540]{2,1,0:T(8,128)(2,1)}, u32[]{:S(2)}, u32[]{:S(2)}) %all-to-all-start) | async-done | bytes 1774112 | tf_op jit(solution)/shard_map/all_to_all | solution.py:43
  50.8 3.8 broadcast_select_fusion
  57.1 25.2 %all_to_all.40.own_ref = bf16[8,2,3,64,256]{4,3,2,1,0:T(8,128)(2,1)S(1)} all-to-all(bf16[8,2,3,64,256]{4,3,2,1,0:T(8,128)(2,1)S(1)} %broadcast_in_dim.19), channel_id=1, replica_groups={{0,16,32,48,64,80,96,112},{8,24,40,56,72,88,104,120},{1,17,33,49,65,81,..., dimensions={0} | all-to-all | bytes 3145728 | tf_op jit(solution)/shard_map/all_to_all | solution.py:39
  83.4 34.1 %all-gather.5.cloned.1.call-done = bf16[1,576,2304]{2,1,0:T(8,128)(2,1)} async-done(((bf16[1,72,2304]{2,1,0:T(8,128)(2,1)}), bf16[1,576,2304]{2,1,0:T(8,128)(2,1)}) %all-gather.5.cloned.1.call-update) | async-done | bytes 2654224 | tf_op jit(solution)/shard_map/all_gather | solution.py:306
  122.5 2.1 slice.334
  124.6 3.4 reshape.325
  128.0 32.7 %attention.2 = (f32[9,64,256]{2,1,0:T(8,128)S(1)}, f32[3,2,1,384]{3,2,1,0:T(1,128)S(1)}) custom-call(s32[39]{0:T(128)S(1)} %concatenate.94.sc, bf16[9,64,256]{2,1,0:T(8,128)(2,1)S(1)} %fusion.59.q_ref, bf16[8,2,3,64,256]{4,3,2,1,0:T(8,128)(2,1)S(1)} %all_to_all.40.own_ref, bf16[8,2,3,64,256]{4,3,2,1,0:T(8,128)(2,1)S(1)} %collective-permute-done.1.other_ref), custom_call_target="tpu_custom_call" | custom-call | tf_op jit(solution)/shard_map/attention/pallas_call | solution.py:215
  160.8 2.5 multiply_reduce_fusion.8
  168.0 2.1 slice.338
  170.2 2.7 reshape.326
  172.8 2.6 fusion.10
  182.7 4.1 all-to-all-start.2
  187.3 23.6 %all-to-all-done.2.own_ref = bf16[8,2,3,64,256]{4,3,2,1,0:T(8,128)(2,1)S(1)} async-done(((bf16[8,2,3,64,256]{4,3,2,1,0:T(8,128)(2,1)}), bf16[8,2,3,64,256]{4,3,2,1,0:T(8,128)(2,1)S(1)}, u32[]{:S(2)}, u32[]{:S(2)}) %all-to-all-start.2) | async-done | bytes 1572896 | tf_op jit(solution)/shard_map/all_to_all | solution.py:39
  212.4 2.1 slice.353
  214.5 3.4 reshape.328
  217.9 2.1 slice.357
  220.1 3.4 reshape.329
  224.6 33.6 %attention.3 = (f32[9,64,256]{2,1,0:T(8,128)S(1)}, f32[3,2,1,384]{3,2,1,0:T(1,128)S(1)}) custom-call(s32[39]{0:T(128)S(1)} %concatenate.94.sc, bf16[9,64,256]{2,1,0:T(8,128)(2,1)S(1)} %fusion.56.q_ref, bf16[8,2,3,64,256]{4,3,2,1,0:T(8,128)(2,1)S(1)} %all-to-all-done.2.own_ref, bf16[8,2,3,64,256]{4,3,2,1,0:T(8,128)(2,1)} %collective-permute-done.3.other_ref), custom_call_target="tpu_custom_call" | custom-call | tf_op jit(solution)/shard_map/attention/pallas_call | solution.py:215
  258.3 2.4 multiply_reduce_fusion.6
  264.8 2.4 fusion.2
  269.8 3.5 multiply_reduce_fusion
  275.3 2.2 copy.70
  277.6 3.2 reshape.337
  280.8 3.6 pad_maximum_fusion.1
  286.8 37.8 %attention_back.2 = (f32[9,64,256]{2,1,0:T(8,128)S(1)}, bf16[8,2,3,64,256]{4,3,2,1,0:T(8,128)(2,1)S(1)}, bf16[8,2,3,64,256]{4,3,2,1,0:T(8,128)(2,1)S(1)}) custom-call(s32[39]{0:T(128)S(1)} %concatenate.94.sc, bf16[9,64,256]{2,1,0:T(8,128)(2,1)S(1)} %copy-done.3, bf16[8,2,3,64,256]{4,3,2,1,0:T(8,128)(2,1)S(1)} %all-to-all-done.2.own_ref, ...), custom_call_target="tpu_custom_call" | custom-call | tf_op jit(solution)/shard_map/attention_back/pallas_call | solution.py:238
  325.8 3.0 collective-permute-done.5
  330.6 4.4 all-to-all-start.3
  338.0 2.3 reshape.336
  342.1 3.9 add_convert_fusion
  346.1 12.8 %all-to-all-done.3 = bf16[8,2,3,64,256]{4,3,2,1,0:T(8,128)(2,1)} async-done(((bf16[8,2,3,64,256]{4,3,2,1,0:T(8,128)(2,1)}), bf16[8,2,3,64,256]{4,3,2,1,0:T(8,128)(2,1)}, u32[]{:S(2)}, u32[]{:S(2)}) %all-to-all-start.3) | async-done | bytes 1572896 | tf_op jit(solution)/shard_map/all_to_all | solution.py:39
  367.8 2.3 copy.68
  370.1 3.2 reshape.335
  380.5 2.3 multiply_reduce_fusion.2
  385.0 37.6 %attention_back.3 = (f32[9,64,256]{2,1,0:T(8,128)S(1)}, bf16[8,2,3,64,256]{4,3,2,1,0:T(8,128)(2,1)S(1)}, bf16[8,2,3,64,256]{4,3,2,1,0:T(8,128)(2,1)}) custom-call(s32[39]{0:T(128)S(1)} %concatenate.94.sc, bf16[9,64,256]{2,1,0:T(8,128)(2,1)S(1)} %fusion.59.q_ref, bf16[8,2,3,64,256]{4,3,2,1,0:T(8,128)(2,1)S(1)} %all_to_all.40.own_ref, ...), custom_call_target="tpu_custom_call" | custom-call | tf_op jit(solution)/shard_map/attention_back/pallas_call | solution.py:238
  426.9 2.2 reshape.334
  431.0 3.2 add_convert_fusion.3
  434.2 4.4 all-to-all-start.4
  440.0 2.7 convolution_convert_fusion.4
  442.8 3.9 add_convert_fusion.1
  446.7 16.5 %all-to-all-done.4 = bf16[8,2,3,64,256]{4,3,2,1,0:T(8,128)(2,1)} async-done(((bf16[8,2,3,64,256]{4,3,2,1,0:T(8,128)(2,1)}), bf16[8,2,3,64,256]{4,3,2,1,0:T(8,128)(2,1)}, u32[]{:S(2)}, u32[]{:S(2)}) %all-to-all-start.4) | async-done | bytes 1572896 | tf_op jit(solution)/shard_map/all_to_all | solution.py:39
  466.8 2.4 broadcast_select_fusion.2
  473.9 3.4 add_convert_fusion.2
  477.4 32.2 %all_to_all.41 = bf16[8,72,1540]{2,1,0:T(8,128)(2,1)} all-to-all(bf16[8,72,1540]{2,1,0:T(8,128)(2,1)S(1)} %bitcast.167), channel_id=1, replica_groups=mesh['ctx'=16,'fsdp'=8] {'fsdp'}, dimensions={0} | all-to-all | bytes 3548160 | tf_op jit(solution)/shard_map/all_to_all | solution.py:43
  511.5 28.6 %reduce-scatter.3.cloned.1.call-done = bf16[72,2304]{1,0:T(8,128)(2,1)} async-done(((bf16[576,2304]{1,0:T(8,128)(2,1)}), bf16[72,2304]{1,0:T(8,128)(2,1)}) %reduce-scatter.3.cloned.1.call-update) | async-done | bytes 331792 | tf_op jit(solution)/shard_map/reduce_scatter | solution.py:381
  541.6 23.6 %all_to_all.42 = bf16[8,9,6148]{2,1,0:T(8,128)(2,1)S(1)} all-to-all(bf16[8,9,6148]{2,1,0:T(8,128)(2,1)S(1)} %reshape.339), channel_id=1, replica_groups={{0,16,32,48,64,80,96,112},{8,24,40,56,72,88,104,120},{1,17,33,49,65,81,..., dimensions={0} | all-to-all | bytes 1770624 | tf_op jit(solution)/shard_map/all_to_all | solution.py:39
  565.6 20.6 %all_to_all.43 = bf16[8,9,6148]{2,1,0:T(8,128)(2,1)S(1)} all-to-all(bf16[8,9,6148]{2,1,0:T(8,128)(2,1)S(1)} %broadcast_in_dim.21), channel_id=1, replica_groups={{0,16,32,48,64,80,96,112},{8,24,40,56,72,88,104,120},{1,17,33,49,65,81,..., dimensions={0} | all-to-all | bytes 1770624 | tf_op jit(solution)/shard_map/all_to_all | solution.py:39
  587.7 4.6 collective-permute-start.10
  (395 shorter events, 113.9 us)
Async XLA Ops:
  10.6 8.3 %copy-start.85 = (bf16[2,72,3072]{2,1,0:T(8,128)(2,1)S(1)}, bf16[2,72,3072]{2,1,0:T(8,128)(2,1)}, u32[]{:S(2)}) copy-start(bf16[2,72,3072]{2,1,0:T(8,128)(2,1)} %param.15) | copy-start | bytes 2654212
  10.6 35.0 %all-to-all-start = ((bf16[8,72,1540]{2,1,0:T(8,128)(2,1)}), bf16[8,72,1540]{2,1,0:T(8,128)(2,1)}, u32[]{:S(2)}, u32[]{:S(2)}) async-start(bf16[8,72,1540]{2,1,0:T(8,128)(2,1)} %broadcast_in_dim.16), calls=%async_computation | async-start | bytes 3833856 | tf_op jit(solution)/shard_map/all_to_all | solution.py:43
  18.9 98.7 %all-gather.5.cloned.1.call-start = ((), (), s32[]{:S(2)}) async-start(), calls=%async_computation.12 | async-start | bytes 2985984 | tf_op jit(solution)/shard_map/all_gather | solution.py:306
  22.8 24.6 %copy-start.110 = (s32[32]{0:T(128)S(1)}, s32[32]{0:T(128)}, u32[]{:S(2)}) copy-start(s32[32]{0:T(128)} %param.10) | copy-start | bytes 388
  22.8 26.5 %copy-start.60 = (bf16[1,256,576]{1,2,0:T(8,128)(2,1)S(1)}, bf16[1,256,576]{1,2,0:T(8,128)(2,1)}, u32[]{:S(2)}) copy-start(bf16[1,256,576]{1,2,0:T(8,128)(2,1)} %param.9) | copy-start | bytes 884740
  45.6 5.2 collective-permute-start
  47.3 139.5 %all-gather.7.cloned.1.call-start = ((), (), s32[]{:S(2)}) async-start(), calls=%async_computation.13 | async-start | bytes 2985984 | tf_op jit(solution)/shard_map/all_gather | solution.py:306
  49.6 6.2 %copy-start.99 = (f32[32,256]{1,0:T(8,128)}, f32[32,256]{1,0:T(8,128)S(1)}, u32[]{:S(2)}) copy-start(f32[32,256]{1,0:T(8,128)S(1)} %get-tuple-element.80) | copy-start | bytes 98308
  57.1 64.0 %copy-start.101 = (s32[1,4096]{1,0:T(1,128)S(1)}, s32[1,4096]{1,0:T(1,128)}, u32[]{:S(2)}) copy-start(s32[1,4096]{1,0:T(1,128)} %param.11) | copy-start | bytes 49156
  82.3 45.7 %collective-permute-start.1 = (bf16[8,2,3,64,256]{4,3,2,1,0:T(8,128)(2,1)S(1)}, bf16[8,2,3,64,256]{4,3,2,1,0:T(8,128)(2,1)S(1)}, u32[]{:S(2)}, u32[]{:S(2)}) collective-permute-start(bf16[8,2,3,64,256]{4,3,2,1,0:T(8,128)(2,1)S(1)} %all_to_all.40.own_ref), channel_id=1, source_target_pairs={{0,8},{8,0},{16,24},{24,16},{32,40},{40,32},{48,56},{56,48},{64,72... | collective-permute-start | bytes 4718600 | tf_op jit(solution)/shard_map/ppermute | solution.py:35
  117.6 50.4 %collective-permute-start.2 = (bf16[576,2304]{1,0:T(8,128)(2,1)}, bf16[576,2304]{1,0:T(8,128)(2,1)}, u32[]{:S(2)}, u32[]{:S(2)}) collective-permute-start(bf16[576,2304]{1,0:T(8,128)(2,1)} %bitcast.170), channel_id=1, source_target_pairs={{0,8},{8,0},{16,24},{24,16},{32,40},{40,32},{48,56},{56,48},{64,72... | collective-permute-start | bytes 7962632 | tf_op jit(solution)/shard_map/ppermute | solution.py:35
  128.0 32.8 %copy-start.61 = (bf16[1,256,576]{1,2,0:T(8,128)(2,1)S(1)}, bf16[1,256,576]{1,2,0:T(8,128)(2,1)}, u32[]{:S(2)}) copy-start(bf16[1,256,576]{1,2,0:T(8,128)(2,1)} %param.9) | copy-start | bytes 884740
  128.0 32.8 %copy-start = (bf16[8,2,3,64,256]{4,3,2,1,0:T(8,128)(2,1)}, bf16[8,2,3,64,256]{4,3,2,1,0:T(8,128)(2,1)S(1)}, u32[]{:S(2)}) copy-start(bf16[8,2,3,64,256]{4,3,2,1,0:T(8,128)(2,1)S(1)} %collective-permute-done.1.other_ref) | copy-start | bytes 4718596
  164.1 8.7 %copy-start.12 = (bf16[256,576]{0,1:T(8,128)(2,1)}, bf16[256,576]{0,1:T(8,128)(2,1)S(1)}, u32[]{:S(2)}) copy-start(bf16[256,576]{0,1:T(8,128)(2,1)S(1)} %multiply_convert_fusion.14) | copy-start | bytes 884740
  182.7 28.1 %all-to-all-start.2 = ((bf16[8,2,3,64,256]{4,3,2,1,0:T(8,128)(2,1)}), bf16[8,2,3,64,256]{4,3,2,1,0:T(8,128)(2,1)S(1)}, u32[]{:S(2)}, u32[]{:S(2)}) async-start(bf16[8,2,3,64,256]{4,3,2,1,0:T(8,128)(2,1)} %broadcast_in_dim.20), calls=%async_computation.2 | async-start | bytes 3145728 | tf_op jit(solution)/shard_map/all_to_all | solution.py:39
  186.9 31.1 %collective-permute-start.4 = (bf16[576,2304]{1,0:T(8,128)(2,1)}, bf16[576,2304]{1,0:T(8,128)(2,1)}, u32[]{:S(2)}, u32[]{:S(2)}) collective-permute-start(bf16[576,2304]{1,0:T(8,128)(2,1)} %bitcast.174), channel_id=1, source_target_pairs={{0,8},{8,0},{16,24},{24,16},{32,40},{40,32},{48,56},{56,48},{64,72... | collective-permute-start | bytes 7962632 | tf_op jit(solution)/shard_map/ppermute | solution.py:35
  210.8 13.8 %collective-permute-start.3 = (bf16[8,2,3,64,256]{4,3,2,1,0:T(8,128)(2,1)S(1)}, bf16[8,2,3,64,256]{4,3,2,1,0:T(8,128)(2,1)}, u32[]{:S(2)}, u32[]{:S(2)}) collective-permute-start(bf16[8,2,3,64,256]{4,3,2,1,0:T(8,128)(2,1)S(1)} %all-to-all-done.2.own_ref), channel_id=1, source_target_pairs={{0,8},{8,0},{16,24},{24,16},{32,40},{40,32},{48,56},{56,48},{64,72... | collective-permute-start | bytes 4718600 | tf_op jit(solution)/shard_map/ppermute | solution.py:35
  224.6 33.7 %copy-start.2 = (bf16[9,64,256]{2,1,0:T(8,128)(2,1)}, bf16[9,64,256]{2,1,0:T(8,128)(2,1)S(1)}, u32[]{:S(2)}) copy-start(bf16[9,64,256]{2,1,0:T(8,128)(2,1)S(1)} %fusion.56.q_ref) | copy-start | bytes 884740
  224.6 33.7 %copy-start.26 = (f32[256,576]{0,1:T(8,128)S(1)}, f32[256,576]{0,1:T(8,128)}, u32[]{:S(2)}) copy-start(f32[256,576]{0,1:T(8,128)} %copy-done.25) | copy-start | bytes 1769476
  260.7 9.1 %copy-start.22 = (f32[256,576]{0,1:T(8,128)}, f32[256,576]{0,1:T(8,128)S(1)}, u32[]{:S(2)}) copy-start(f32[256,576]{0,1:T(8,128)S(1)} %get-tuple-element.85) | copy-start | bytes 1769476
  260.8 9.0 %copy-start.106 = (f32[256]{0:T(256)}, f32[256]{0:T(256)S(1)}, u32[]{:S(2)}) copy-start(f32[256]{0:T(256)S(1)} %add_rsqrt_fusion) | copy-start | bytes 3076
  260.9 7.0 %copy-start.14 = (bf16[256,576]{0,1:T(8,128)(2,1)}, bf16[256,576]{0,1:T(8,128)(2,1)S(1)}, u32[]{:S(2)}) copy-start(bf16[256,576]{0,1:T(8,128)(2,1)S(1)} %multiply_convert_fusion.12) | copy-start | bytes 884740
  267.9 6.0 copy-start.80
  284.4 57.7 %collective-permute-start.8 = (bf16[576,2304]{1,0:T(8,128)(2,1)}, bf16[576,2304]{1,0:T(8,128)(2,1)}, u32[]{:S(2)}, u32[]{:S(2)}) collective-permute-start(bf16[576,2304]{1,0:T(8,128)(2,1)} %pad_maximum_fusion.1), channel_id=1, source_target_pairs={{0,8},{8,0},{16,24},{24,16},{32,40},{40,32},{48,56},{56,48},{64,72... | collective-permute-start | bytes 7962632 | tf_op jit(solution)/shard_map/ppermute | solution.py:35
  325.3 3.5 collective-permute-start.5
  330.6 4.5 copy-start.79
  330.6 28.3 %all-to-all-start.3 = ((bf16[8,2,3,64,256]{4,3,2,1,0:T(8,128)(2,1)}), bf16[8,2,3,64,256]{4,3,2,1,0:T(8,128)(2,1)}, u32[]{:S(2)}, u32[]{:S(2)}) async-start(bf16[8,2,3,64,256]{4,3,2,1,0:T(8,128)(2,1)} %add_convert_fusion.4), calls=%async_computation.3 | async-start | bytes 3145728 | tf_op jit(solution)/shard_map/all_to_all | solution.py:39
  335.0 176.4 %reduce-scatter.5.cloned.1.call-start = ((), (), s32[]{:S(2)}) async-start(), calls=%async_computation.11 | async-start | bytes 2985984 | tf_op jit(solution)/shard_map/reduce_scatter | solution.py:381
  346.1 14.6 %copy-start.11 = (f32[9,64,256]{2,1,0:T(8,128)S(1)}, f32[9,64,256]{2,1,0:T(8,128)}, u32[]{:S(2)}) copy-start(f32[9,64,256]{2,1,0:T(8,128)} %copy-done.10) | copy-start | bytes 1769476
  364.1 14.0 %copy-start.72 = (bf16[256,576]{0,1:T(8,128)(2,1)}, bf16[256,576]{0,1:T(8,128)(2,1)S(1)}, u32[]{:S(2)}) copy-start(bf16[256,576]{0,1:T(8,128)(2,1)S(1)} %get-tuple-element.39) | copy-start | bytes 884740
  366.4 6.9 %copy-start.96 = (bf16[256,768]{1,0:T(8,128)(2,1)}, bf16[256,768]{1,0:T(8,128)(2,1)S(1)}, u32[]{:S(2)}) copy-start(bf16[256,768]{1,0:T(8,128)(2,1)S(1)} %get-tuple-element.45) | copy-start | bytes 1179652
  367.8 5.5 copy-start.13
  376.8 66.0 %collective-permute-start.7 = (bf16[576,2304]{1,0:T(8,128)(2,1)}, bf16[576,2304]{1,0:T(8,128)(2,1)}, u32[]{:S(2)}, u32[]{:S(2)}) collective-permute-start(bf16[576,2304]{1,0:T(8,128)(2,1)} %pad_maximum_fusion), channel_id=1, source_target_pairs={{0,8},{8,0},{16,24},{24,16},{32,40},{40,32},{48,56},{56,48},{64,72... | collective-permute-start | bytes 7962632 | tf_op jit(solution)/shard_map/ppermute | solution.py:35
  383.0 55.6 %copy-start.17 = (f32[256,576]{0,1:T(8,128)}, f32[256,576]{0,1:T(8,128)S(1)}, u32[]{:S(2)}) copy-start(f32[256,576]{0,1:T(8,128)S(1)} %multiply_add_fusion) | copy-start | bytes 1769476
  385.0 39.5 %copy-start.21 = (f32[256,576]{0,1:T(8,128)S(1)}, f32[256,576]{0,1:T(8,128)}, u32[]{:S(2)}) copy-start(f32[256,576]{0,1:T(8,128)} %copy-done.19) | copy-start | bytes 1769476
  385.0 39.5 %copy-start.71 = (bf16[9,64,256]{2,1,0:T(8,128)(2,1)S(1)}, bf16[9,64,256]{2,1,0:T(8,128)(2,1)}, u32[]{:S(2)}) copy-start(bf16[9,64,256]{2,1,0:T(8,128)(2,1)} %copy-done.70) | copy-start | bytes 884740
  423.7 7.2 %collective-permute-start.6 = (bf16[8,2,3,64,256]{4,3,2,1,0:T(8,128)(2,1)}, bf16[8,2,3,64,256]{4,3,2,1,0:T(8,128)(2,1)}, u32[]{:S(2)}, u32[]{:S(2)}) collective-permute-start(bf16[8,2,3,64,256]{4,3,2,1,0:T(8,128)(2,1)} %get-tuple-element.26), channel_id=1, source_target_pairs={{0,8},{8,0},{16,24},{24,16},{32,40},{40,32},{48,56},{56,48},{64,72... | collective-permute-start | bytes 4718600 | tf_op jit(solution)/shard_map/ppermute | solution.py:35
  434.2 29.0 %all-to-all-start.4 = ((bf16[8,2,3,64,256]{4,3,2,1,0:T(8,128)(2,1)}), bf16[8,2,3,64,256]{4,3,2,1,0:T(8,128)(2,1)}, u32[]{:S(2)}, u32[]{:S(2)}) async-start(bf16[8,2,3,64,256]{4,3,2,1,0:T(8,128)(2,1)} %add_convert_fusion.3), calls=%async_computation.4 | async-start | bytes 3145728 | tf_op jit(solution)/shard_map/all_to_all | solution.py:39
  438.6 101.5 %reduce-scatter.3.cloned.1.call-start = ((), (), s32[]{:S(2)}) async-start(), calls=%async_computation.10 | async-start | bytes 2985984 | tf_op jit(solution)/shard_map/reduce_scatter | solution.py:381
  469.2 4.7 collective-permute-start.9
  586.2 6.0 copy-start.24
  586.2 6.0 copy-start.39
  587.7 6.1 copy-start.41
  587.7 6.1 copy-start.81
  587.7 8.4 %collective-permute-start.10 = (bf16[72,6148]{1,0:T(8,128)(2,1)}, bf16[72,6148]{1,0:T(8,128)(2,1)S(1)}, u32[]{:S(2)}, u32[]{:S(2)}) collective-permute-start(bf16[72,6148]{1,0:T(8,128)(2,1)} %reshape.340), channel_id=1, source_target_pairs={{0,8},{8,0},{16,24},{24,16},{32,40},{40,32},{48,56},{56,48},{64,72... | collective-permute-start | bytes 2655944 | tf_op jit(solution)/shard_map/ppermute | solution.py:35
  607.8 4.8 copy-start.89
  607.9 4.8 copy-start.90
  607.9 4.8 copy-start.91
  (82 other events, 170.7 us)
Sparse Core Ops, SparseCore 0:
  47.5 70.0 all-gather.4
  120.5 57.6 all-gather.6
  346.2 74.9 reduce-scatter.4
  446.8 93.2 reduce-scatter.2

commit v2 on v1

v2 whole, which is shorter than its diff:
```python
import functools

import jax
import jax.numpy as jnp
from jax import lax
from jax.experimental import pallas as pl
from jax.experimental.pallas import tpu as pltpu
from jax.sharding import PartitionSpec as P

D = 576
HEADS = 9
KV_HEADS = 3
GROUP = 3
HEAD_DIM = 64
FF = 1536
LAYERS = 2
BLK = 128
NBLK = 32
EPS = 1e-05
THETA = 100000.0
NEG = -1e30
F32 = jnp.float32
BF16 = jnp.bfloat16
LANES = GROUP * BLK
CTX = 16
FSDP = 8
SHARD = D // FSDP
HALF = FF // 2
Q_ROWS = HEADS * HEAD_DIM
KV_ROWS = 2 * KV_HEADS * HEAD_DIM

PARTNER = [(i, i ^ 1) for i in range(CTX)]
SAME_CORE = [[2 * chip + core for chip in range(CTX // 2)] for core in range(2)]


def to_partner(x):
    return lax.ppermute(x, "ctx", PARTNER)


def over_chips(x):
    return lax.all_to_all(x, "ctx", 0, 0, axis_index_groups=SAME_CORE, tiled=True)


def over_fsdp(x):
    return lax.all_to_all(x, "fsdp", 0, 0, tiled=True)


def gather_fsdp(x):
    return over_fsdp(jnp.broadcast_to(x[None], (FSDP,) + x.shape)).reshape(-1, x.shape[1])


def scatter_fsdp(x):
    parts = over_fsdp(x.reshape(FSDP, -1, x.shape[1]))
    return jnp.sum(parts.astype(F32), 0).astype(BF16)


def sum_pair(a, b):
    return (a.astype(F32) + b.astype(F32)).astype(BF16)


def sum_chips(x):
    for bit in (2, 4, 8):
        x = sum_pair(x, lax.ppermute(x, "ctx", [(i, i ^ bit) for i in range(CTX)]))
    return x


def dot_tn(a, b):
    return lax.dot_general(a, b, (((0,), (0,)), ((), ())), preferred_element_type=F32)


def dot_nt(a, b):
    return lax.dot_general(a, b, (((1,), (1,)), ((), ())), preferred_element_type=F32)


UNROLL_F = 9
UNROLL_B = 3
CHUNK = 4
KEYS = CHUNK * BLK
CHUNKS = NBLK // CHUNK


def fill_keys(sc, own_ref, other_ref, kv_s):
    core = sc[2]
    for chip in range(CTX // 2):
        for half in range(2):
            lanes = slice(half * BLK, (half + 1) * BLK)
            block = sc[7 + 2 * (2 * chip + core) + half]
            kv_s[block] = own_ref[chip, :, 0, :, lanes]
            block = sc[7 + 2 * (2 * chip + 1 - core) + half]
            kv_s[block] = other_ref[chip, :, 0, :, lanes]


def fill_queries(sc, src_ref, dst):
    for half in range(2):
        lanes = slice(half * BLK, (half + 1) * BLK)
        which = jnp.bitwise_xor(half, sc[1])
        dst[which] = jnp.concatenate([src_ref[j, :, lanes] for j in range(GROUP)], axis=1)


def query_rows(sc, which):
    block = jnp.where(which == 0, sc[0], NBLK - 1 - sc[0])
    lane = lax.broadcasted_iota(jnp.int32, (1, LANES), 1)
    pos = block * BLK + jnp.bitwise_and(lane, BLK - 1)
    start = jnp.zeros((1, LANES), jnp.int32)
    for d in range(4):
        start = jnp.where(pos >= sc[3 + d], jnp.maximum(start, sc[3 + d]), start)
    return pos, start


def chunk_of(sc, t):
    high = (NBLK - sc[0] + CHUNK - 1) // CHUNK
    which = (t < high).astype(jnp.int32)
    return which, jnp.where(t < high, t, t - high)


def keys_of(kv_s, chunk, kind):
    return jnp.concatenate([kv_s[chunk * CHUNK + j, kind] for j in range(CHUNK)], axis=1)


def seen(pos_s, which, chunk):
    at = lax.broadcasted_iota(jnp.int32, (KEYS, LANES), 0)
    base = chunk * KEYS
    return (at >= pos_s[which, 1:2] - base) & (at <= pos_s[which, 0:1] - base)


def fill_rows(sc, pos_s):
    for which in range(2):
        pos, start = query_rows(sc, which)
        pos_s[which, 0:1] = pos
        pos_s[which, 1:2] = start


def forward_kernel(sc, q_ref, own_ref, other_ref, o_ref, lse_ref, kv_s, q_s, acc_s, m_s, l_s, pos_s):
    fill_keys(sc, own_ref, other_ref, kv_s)
    fill_queries(sc, q_ref, q_s)
    fill_rows(sc, pos_s)
    acc_s[...] = jnp.zeros_like(acc_s)
    m_s[...] = jnp.full_like(m_s, NEG)
    l_s[...] = jnp.zeros_like(l_s)

    def step(t, carry):
        which, chunk = chunk_of(sc, t)
        scores = dot_tn(keys_of(kv_s, chunk, 0), q_s[which])
        scores = jnp.where(seen(pos_s, which, chunk), scores, NEG)
        old = m_s[which]
        new = jnp.maximum(old, jnp.max(scores, axis=0, keepdims=True))
        prob = jnp.exp(scores - new)
        shrink = jnp.exp(old - new)
        m_s[which] = new
        l_s[which] = l_s[which] * shrink + jnp.sum(prob, axis=0, keepdims=True)
        acc_s[which] = acc_s[which] * shrink + jnp.dot(
            keys_of(kv_s, chunk, 1), prob.astype(BF16), preferred_element_type=F32
        )
        return carry

    lax.fori_loop(0, CHUNKS + 1, step, 0, unroll=UNROLL_F)
    for which in range(2):
        acc_s[which] = acc_s[which] / l_s[which]
        lse_ref[0, which] = m_s[which] + jnp.log(l_s[which])
    for half in range(2):
        mine = acc_s[jnp.bitwise_xor(half, sc[1])]
        for j in range(GROUP):
            o_ref[j, :, half * BLK : (half + 1) * BLK] = mine[:, j * BLK : (j + 1) * BLK]


def backward_kernel(
    sc, q_ref, own_ref, other_ref, o_ref, do_ref, lse_ref,
    dq_ref, down_ref, dother_ref,
    kv_s, q_s, do_s, dq_s, dkv_s, delta_s, pos_s,
):
    fill_keys(sc, own_ref, other_ref, kv_s)
    fill_queries(sc, q_ref, q_s)
    fill_queries(sc, do_ref, do_s)
    fill_queries(sc, o_ref, dq_s)
    fill_rows(sc, pos_s)
    for which in range(2):
        delta_s[which] = jnp.sum(dq_s[which] * do_s[which].astype(F32), axis=0, keepdims=True)
    dq_s[...] = jnp.zeros_like(dq_s)
    dkv_s[...] = jnp.zeros_like(dkv_s)

    def step(t, carry):
        which, chunk = chunk_of(sc, t)
        key_t, val_t, q_t, do_t = keys_of(kv_s, chunk, 0), keys_of(kv_s, chunk, 1), q_s[which], do_s[which]
        scores = dot_tn(key_t, q_t)
        prob = jnp.where(seen(pos_s, which, chunk), jnp.exp(scores - lse_ref[0, which]), 0.0)
        d_prob = dot_tn(val_t, do_t)
        d_score = (prob * (d_prob - delta_s[which])).astype(BF16)
        d_val = dot_nt(do_t, prob.astype(BF16))
        d_key = dot_nt(q_t, d_score)
        dq_s[which] = dq_s[which] + jnp.dot(key_t, d_score, preferred_element_type=F32)
        for j in range(CHUNK):
            lanes = slice(j * BLK, (j + 1) * BLK)
            dkv_s[chunk * CHUNK + j, 0] = dkv_s[chunk * CHUNK + j, 0] + d_key[:, lanes]
            dkv_s[chunk * CHUNK + j, 1] = dkv_s[chunk * CHUNK + j, 1] + d_val[:, lanes]
        return carry

    lax.fori_loop(0, CHUNKS + 1, step, 0, unroll=UNROLL_B)
    core = sc[2]
    scale = HEAD_DIM**-0.5
    for half in range(2):
        lanes = slice(half * BLK, (half + 1) * BLK)
        mine = dq_s[jnp.bitwise_xor(half, sc[1])] * scale
        for j in range(GROUP):
            dq_ref[j, :, lanes] = mine[:, j * BLK : (j + 1) * BLK]
        for chip in range(CTX // 2):
            block = sc[7 + 2 * (2 * chip + core) + half]
            down_ref[chip, :, 0, :, lanes] = dkv_s[block].astype(BF16)
            block = sc[7 + 2 * (2 * chip + 1 - core) + half]
            dother_ref[chip, :, 0, :, lanes] = dkv_s[block].astype(BF16)


ROWS = 2 * BLK
HEAD_SPEC = pl.BlockSpec((GROUP, HEAD_DIM, ROWS), lambda g, sc: (g, 0, 0))
KV_SPEC = pl.BlockSpec((CTX // 2, 2, 1, HEAD_DIM, ROWS), lambda g, sc: (0, 0, g, 0, 0))
LSE_SPEC = pl.BlockSpec((1, 2, 1, LANES), lambda g, sc: (g, 0, 0, 0))
HEAD_SHAPE = jax.ShapeDtypeStruct((HEADS, HEAD_DIM, ROWS), F32)
KV_SHAPE = jax.ShapeDtypeStruct((CTX // 2, 2, KV_HEADS, HEAD_DIM, ROWS), BF16)
LSE_SHAPE = jax.ShapeDtypeStruct((KV_HEADS, 2, 1, LANES), F32)
KERNEL_PARAMS = pltpu.CompilerParams(
    dimension_semantics=("arbitrary",), vmem_limit_bytes=40 * 2**20
)


def attention(scalars, q_t, own, other):
    return pl.pallas_call(
        forward_kernel,
        grid_spec=pltpu.PrefetchScalarGridSpec(
            num_scalar_prefetch=1,
            grid=(KV_HEADS,),
            in_specs=[HEAD_SPEC, KV_SPEC, KV_SPEC],
            out_specs=[HEAD_SPEC, LSE_SPEC],
            scratch_shapes=[
                pltpu.VMEM((NBLK, 2, HEAD_DIM, BLK), BF16),
                pltpu.VMEM((2, HEAD_DIM, LANES), BF16),
                pltpu.VMEM((2, HEAD_DIM, LANES), F32),
                pltpu.VMEM((2, 1, LANES), F32),
                pltpu.VMEM((2, 1, LANES), F32),
                pltpu.VMEM((2, 8, LANES), jnp.int32),
            ],
        ),
        out_shape=[HEAD_SHAPE, LSE_SHAPE],
        compiler_params=KERNEL_PARAMS,
        name="attention",
    )(scalars, q_t, own, other)


def attention_back(scalars, q_t, own, other, o_t, do_t, lse):
    return pl.pallas_call(
        backward_kernel,
        grid_spec=pltpu.PrefetchScalarGridSpec(
            num_scalar_prefetch=1,
            grid=(KV_HEADS,),
            in_specs=[HEAD_SPEC, KV_SPEC, KV_SPEC, HEAD_SPEC, HEAD_SPEC, LSE_SPEC],
            out_specs=[HEAD_SPEC, KV_SPEC, KV_SPEC],
            scratch_shapes=[
                pltpu.VMEM((NBLK, 2, HEAD_DIM, BLK), BF16),
                pltpu.VMEM((2, HEAD_DIM, LANES), BF16),
                pltpu.VMEM((2, HEAD_DIM, LANES), BF16),
                pltpu.VMEM((2, HEAD_DIM, LANES), F32),
                pltpu.VMEM((NBLK, 2, HEAD_DIM, BLK), F32),
                pltpu.VMEM((2, 1, LANES), F32),
                pltpu.VMEM((2, 8, LANES), jnp.int32),
            ],
        ),
        out_shape=[HEAD_SHAPE, KV_SHAPE, KV_SHAPE],
        compiler_params=KERNEL_PARAMS,
        name="attention_back",
    )(scalars, q_t, own, other, o_t, do_t, lse)


def rotate(x, cosine, sine):
    half = HEAD_DIM // 2
    first, second = x[:, :half], x[:, half:]
    return jnp.concatenate([first * cosine - second * sine, second * cosine + first * sine], 1)


def normed(hidden):
    inv_rms = lax.rsqrt(jnp.mean(hidden * hidden, -1, keepdims=True) + EPS)
    return hidden * inv_rms, inv_rms


def norm_back(d_unit, unit, inv_rms):
    return inv_rms * (d_unit - unit * jnp.mean(d_unit * unit, -1, keepdims=True))


def mm(a, b):
    return jnp.dot(a, b, preferred_element_type=F32)


def ein(spec, a, b):
    return jnp.einsum(spec, a, b, preferred_element_type=F32)


def local(tokens, block_order, doc_ids, norm_gains, w_qkv, w_out, w_gate_up, w_down, cotangent):
    place = lax.axis_index("ctx")
    core = jnp.bitwise_and(place, 1)
    first_core = core == 0

    def my_half(left, right):
        return jnp.where(first_core, left, right)

    def in_order(own, other):
        return my_half(own, other), my_half(other, own)

    gain_cols = jnp.transpose(norm_gains.reshape(2 * LAYERS, SHARD))
    cut = (Q_ROWS + KV_ROWS + D) // 2
    wgu_cut = w_gate_up.reshape(LAYERS, SHARD, 2, FSDP, 2, FF // FSDP // 2)
    wgu_cut = my_half(wgu_cut[..., 0, :], wgu_cut[..., 1, :]).reshape(LAYERS, SHARD, FF)
    wd_cut = w_down.reshape(LAYERS, 2, FF // FSDP // 2, D)
    wd_cut = my_half(wd_cut[:, 0], wd_cut[:, 1])
    projs, mlps = [], []
    for layer in range(LAYERS):
        proj = jnp.concatenate([w_qkv[layer], w_out[layer]], 1)
        proj = my_half(proj[:, :cut], proj[:, cut:])
        if layer == 0:
            proj = jnp.concatenate([proj, gain_cols], 1)
        own = gather_fsdp(proj)
        if layer == 0:
            gains = jnp.transpose(own[:, cut:].astype(F32)).reshape(LAYERS, 2, D)
        pair = in_order(own, to_partner(own))
        projs.append(jnp.concatenate([half[:, :cut] for half in pair], 1))
        wgu, wdown = gather_fsdp(wgu_cut[layer]), gather_fsdp(wd_cut[layer])
        mlps.append([(wgu, wdown), (to_partner(wgu), to_partner(wdown))])

    first_block = lax.dynamic_index_in_dim(block_order, 2 * place, 0, keepdims=False)
    low = jnp.minimum(first_block, NBLK - 1 - first_block)
    low_half = (first_block != low).astype(jnp.int32)
    starts = jnp.sum(
        (doc_ids[0][None, :] < jnp.arange(1, 5, dtype=jnp.int32)[:, None]).astype(jnp.int32), 1
    )
    scalars = jnp.concatenate([jnp.stack([low, low_half, core]), starts, block_order])
    lane = jnp.arange(ROWS, dtype=jnp.int32)
    pos = jnp.where(lane < BLK, first_block, NBLK - 2 - first_block) * BLK + lane
    inv_freq = THETA ** (-jnp.arange(HEAD_DIM // 2, dtype=F32) / (HEAD_DIM // 2))
    angles = pos.astype(F32)[None, :] * inv_freq[:, None]
    cosine, sine = jnp.cos(angles), jnp.sin(angles)

    hidden = tokens[0].astype(F32)
    saved = []
    for layer in range(LAYERS):
        wqkv, wout = projs[layer][:, : Q_ROWS + KV_ROWS], projs[layer][:, Q_ROWS + KV_ROWS :]
        unit_a, rms_a = normed(hidden)
        attn_in = (unit_a * gains[layer, 0]).astype(BF16)
        qkv_t = ein("de,td->et", wqkv, attn_in).reshape(-1, HEAD_DIM, ROWS)
        turned = rotate(qkv_t[: HEADS + KV_HEADS], cosine, sine)
        q_t = (turned[:HEADS] * HEAD_DIM**-0.5).astype(BF16)
        kv_t = jnp.concatenate([turned[HEADS:], qkv_t[HEADS + KV_HEADS :]], 0).astype(BF16)
        kv_t = kv_t.reshape(1, 2, KV_HEADS, HEAD_DIM, ROWS)
        kv_own = over_chips(jnp.broadcast_to(kv_t, (CTX // 2,) + kv_t.shape[1:]))
        kv_other = to_partner(kv_own)
        o_t, lse = attention(scalars, q_t, kv_own, kv_other)
        attn_out = o_t.astype(BF16).reshape(Q_ROWS, ROWS)
        mid = hidden + ein("at,ad->td", attn_out, wout)
        unit_m, rms_m = normed(mid)
        mlp_in = (unit_m * gains[layer, 1]).astype(BF16)
        hidden = mid
        halves = []
        for wgu, wdown in mlps[layer]:
            gate_up = mm(mlp_in, wgu)
            inner = (jax.nn.silu(gate_up[:, :HALF]) * gate_up[:, HALF:]).astype(BF16)
            hidden = hidden + mm(inner, wdown)
            halves.append((wgu, wdown, gate_up, inner))
        saved.append(
            (wqkv, wout, unit_a, rms_a, attn_in, q_t, kv_own, kv_other, o_t, lse, attn_out,
             unit_m, rms_m, mlp_in, halves)
        )
    output = hidden.astype(BF16).reshape(1, ROWS, D)

    d_hidden = cotangent[0].astype(F32)
    shares = [None] * LAYERS
    gain_grads = [None] * LAYERS
    for layer in reversed(range(LAYERS)):
        (wqkv, wout, unit_a, rms_a, attn_in, q_t, kv_own, kv_other, o_t, lse, attn_out,
         unit_m, rms_m, mlp_in, halves) = saved[layer]
        grad_b = d_hidden.astype(BF16)
        d_norm = 0.0
        wgu_parts, wd_parts = [], []
        for wgu, wdown, gate_up, inner in halves:
            d_inner = ein("td,fd->tf", grad_b, wdown)
            gate, up = gate_up[:, :HALF], gate_up[:, HALF:]
            sig = jax.nn.sigmoid(gate)
            d_gate = d_inner * up * sig * (1.0 + gate * (1.0 - sig))
            d_up = d_inner * (gate * sig)
            d_gu = jnp.concatenate([d_gate, d_up], 1).astype(BF16)
            d_norm = d_norm + ein("tf,df->td", d_gu, wgu)
            wd_parts.append(ein("tf,td->fd", inner, grad_b).astype(BF16))
            wgu_parts.append(ein("td,tf->df", mlp_in, d_gu).astype(BF16))
        d_wgu = sum_pair(wgu_parts[0], to_partner(wgu_parts[1]))
        d_wdown = sum_pair(wd_parts[0], to_partner(wd_parts[1]))
        d_gain_m = jnp.sum(d_norm * unit_m, 0)
        d_hidden = d_hidden + norm_back(d_norm * gains[layer, 1], unit_m, rms_m)
        grad_b = d_hidden.astype(BF16)
        d_wout = mm(attn_out, grad_b)
        do_t = ein("ad,td->at", wout, grad_b).astype(BF16).reshape(HEADS, HEAD_DIM, ROWS)
        if layer == 0:
            do_t, d_wgu, d_wdown = lax.optimization_barrier((do_t, d_wgu, d_wdown))
        dq_t, dkv_own, dkv_other = attention_back(scalars, q_t, kv_own, kv_other, o_t, do_t, lse)
        dkv = (dkv_own.astype(F32) + to_partner(dkv_other).astype(F32)).astype(BF16)
        dkv = jnp.sum(over_chips(dkv).astype(F32), 0)
        turned = jnp.concatenate([dq_t, dkv[0]], 0)
        d_qkv = jnp.concatenate([rotate(turned, cosine, -sine), dkv[1]], 0)
        d_qkv = d_qkv.astype(BF16).reshape(Q_ROWS + KV_ROWS, ROWS)
        d_wqkv = ein("td,et->de", attn_in, d_qkv)
        d_norm = ein("et,de->td", d_qkv, wqkv)
        d_gain_a = jnp.sum(d_norm * unit_a, 0)
        d_hidden = d_hidden + norm_back(d_norm * gains[layer, 0], unit_a, rms_a)
        gain_grads[layer] = jnp.stack([d_gain_a, d_gain_m])
        d_proj = jnp.concatenate([d_wqkv, d_wout], 1).astype(BF16)
        mine, theirs = my_half(d_proj[:, :cut], d_proj[:, cut:]), my_half(d_proj[:, cut:], d_proj[:, :cut])
        d_proj = sum_pair(mine, to_partner(theirs))
        if layer == 0:
            d_gains = jnp.transpose(jnp.stack(gain_grads).reshape(2 * LAYERS, D)).astype(BF16)
            d_proj = jnp.concatenate([d_proj, d_gains], 1)
        mlp_share = jnp.concatenate(
            [scatter_fsdp(d_wgu), scatter_fsdp(d_wdown).reshape(SHARD, HALF)], 1
        )
        proj_share = scatter_fsdp(d_proj)
        if layer == 0:
            shares[layer] = sum_chips(mlp_share), sum_chips(proj_share)
        else:
            both = sum_chips(jnp.concatenate([mlp_share, proj_share], 1))
            shares[layer] = both[:, : FF + HALF], both[:, FF + HALF :]
    input_grad = d_hidden.reshape(1, ROWS, D)

    proj_grads, gate_up_grad, down_grad = [], [], []
    for layer in range(LAYERS):
        mlp_share, proj_share = shares[layer]
        pair = in_order(mlp_share, to_partner(mlp_share))
        cols = jnp.stack([half[:, :FF].reshape(SHARD, 2, FSDP, -1) for half in pair], 3)
        gate_up_grad.append(cols.reshape(SHARD, 2 * FF).astype(F32))
        rows = [half[:, FF:].reshape(FF // FSDP // 2, D) for half in pair]
        down_grad.append(jnp.concatenate(rows, 0).astype(F32))
        theirs = to_partner(proj_share)
        if layer == 0:
            d_gain = proj_share[:, cut:].astype(F32) + theirs[:, cut:].astype(F32)
            gain_grad = jnp.transpose(d_gain).reshape(LAYERS, 2, SHARD)
        pair = in_order(proj_share[:, :cut], theirs[:, :cut])
        proj_grads.append(jnp.concatenate(pair, 1).astype(F32))
    qkv_grad = jnp.stack([g[:, : Q_ROWS + KV_ROWS] for g in proj_grads])
    out_proj_grad = jnp.stack([g[:, Q_ROWS + KV_ROWS :] for g in proj_grads])
    gate_up_grad, down_grad = jnp.stack(gate_up_grad), jnp.stack(down_grad)
    return (output, input_grad, gain_grad, qkv_grad, out_proj_grad, gate_up_grad, down_grad)


def solution(mesh):
    in_specs = (
        P("fsdp", "ctx", None),
        P(),
        P("fsdp", None),
        P(None, None, "fsdp"),
        P(None, "fsdp", None),
        P(None, "fsdp", None),
        P(None, "fsdp", None),
        P(None, "fsdp", None),
        P("fsdp", "ctx", None),
    )
    out_specs = (
        P("fsdp", "ctx", None),
        P("fsdp", "ctx", None),
        P(None, None, "fsdp"),
        P(None, "fsdp", None),
        P(None, "fsdp", None),
        P(None, "fsdp", None),
        P(None, "fsdp", None),
    )
    return jax.shard_map(local, mesh=mesh, in_specs=in_specs, out_specs=out_specs, check_vma=False)
```

time: 630 us -> 599 us (0.951)
  blocking collectives: 102 us -> 0 us
  starting transfers between devices: 35.2 us -> 111 us
  waiting for transfers between devices: 143 us -> 209 us
  Pallas kernels: 142 us -> 78.1 us
  between operations: 18.6 us -> 5.65 us
  local copies, waits for them, and re-layouts: 80.5 us -> 69.6 us
  other arithmetic: 49 us -> 58.4 us
    all_to_all x1 -> x12, waiting for transfers between devices: 22.3 us -> 127 us  [over_fsdp(): return lax.all_to_all(x, 'fsdp', 0, 0, tiled=True)]
    all_to_all x4 -> x0, blocking collectives: 102 us -> none  [the longest x3 69.4 us: over_chips(): lax.all_to_all(x, 'ctx', 0, 0, axis_index_groups=SAME_CORE, tiled=True)]
    all_to_all x1 -> x12, starting transfers between devices: 8.29 us -> 61.2 us  [over_fsdp(): return lax.all_to_all(x, 'fsdp', 0, 0, tiled=True)]
    pallas_call x2, Pallas kernels: 66.3 us -> 31.8 us  [attention(): pl.pallas_call(forward_kernel, grid_spec=pltpu.PrefetchScalarGridSpec(num...]
    all_gather x2 -> x0, waiting for transfers between devices: 34.2 us -> none  [local(): lax.all_gather(mlp_cut[l], 'fsdp', axis=0, tiled=True)]
    pallas_call x2, Pallas kernels: 75.3 us -> 46.3 us  [attention_back(): pl.pallas_call(backward_kernel, grid_spec=pltpu.PrefetchScalarGridSpec(nu...]
    reduce_scatter x2 -> x0, waiting for transfers between devices: 28.6 us -> none  [local(): lax.psum_scatter(both, 'fsdp', scatter_dimension=0, tiled=True)]
    ppermute x0 -> x9, waiting for transfers between devices: none -> 28 us  [sum_chips(): x = sum_pair(x, lax.ppermute(x, 'ctx', [(i, i ^ bit) for i in range(CTX)]))]
  transfers between devices with their start and end apart: 19 -> 45, of which waited for: 8 -> 20; matrix products, arithmetic and copies ran while one was open for 19% -> 27% of each run, Pallas kernels for 17% -> 13%
where the time goes in v2:
time: 599 us; the launch traced here: 588 us
  waiting for transfers between devices  209 us (35%)
  starting transfers between devices  111 us (19%)
  Pallas kernels  78.1 us (13%)
  local copies, waits for them, and re-layouts  69.6 us (12%)
  other arithmetic  58.4 us (10%)
  matrix products  56.5 us (9%)
    all_to_all x12, waiting for transfers between devices, over_fsdp(): return lax.all_to_all(x, 'fsdp', 0, 0, tiled=True)  127 us
    all_to_all x12, starting transfers between devices, over_fsdp(): return lax.all_to_all(x, 'fsdp', 0, 0, tiled=True)  61.2 us
    all_to_all x4, waiting for transfers between devices, over_chips(): lax.all_to_all(x, 'ctx', 0, 0, axis_index_groups=SAME_CORE, tiled=True)  52.6 us
    pallas_call x2, Pallas kernels, attention_back(): pl.pallas_call(backward_kernel, grid_spec=pltpu.PrefetchScalarGridSpec(nu...  46.3 us
    dot_general x26, matrix products, ein(): return jnp.einsum(spec, a, b, preferred_element_type=F32)  39.2 us
    pallas_call x2, Pallas kernels, attention(): pl.pallas_call(forward_kernel, grid_spec=pltpu.PrefetchScalarGridSpec(num...  31.8 us
    ppermute x9, waiting for transfers between devices, sum_chips(): x = sum_pair(x, lax.ppermute(x, 'ctx', [(i, i ^ bit) for i in range(CTX)]))  28 us
    ppermute x20, starting transfers between devices, to_partner(): return lax.ppermute(x, 'ctx', PARTNER)  21 us
  transfers between devices with their start and end apart: 45, of which 20 were waited for; matrix products, arithmetic and copies ran while one was open for 27% of the time, Pallas kernels for 13%

profile of v2, /device:TPU:1, one launch (start us, length us, event | category | flops | bytes accessed | tf_op | source)
XLA Modules:
  0.0 587.6 jit_solution(2201077152134841631)
XLA Ops:
  4.6 8.2 %all-to-all-start = ((bf16[8,72,772]{2,1,0:T(8,128)(2,1)}), bf16[8,72,772]{2,1,0:T(8,128)(2,1)S(1)}, u32[]{:S(2)}, u32[]{:S(2)}) async-start(bf16[8,72,772]{2,1,0:T(8,128)(2,1)} %broadcast_in_dim.32), calls=%async_computation | async-start | bytes 2064384 | tf_op jit(solution)/shard_map/all_to_all | solution.py:45
  14.9 15.0 %all-to-all-done = bf16[8,72,772]{2,1,0:T(8,128)(2,1)S(1)} async-done(((bf16[8,72,772]{2,1,0:T(8,128)(2,1)}), bf16[8,72,772]{2,1,0:T(8,128)(2,1)S(1)}, u32[]{:S(2)}, u32[]{:S(2)}) %all-to-all-start) | async-done | bytes 889376 | tf_op jit(solution)/shard_map/all_to_all | solution.py:45
  30.8 3.6 all-to-all-start.4
  45.1 4.8 all-to-all-done.4
  51.4 4.7 all-to-all-start.1
  56.0 4.4 reshape.414
  63.3 15.6 %all-to-all-done.1.own_ref = bf16[8,2,3,64,256]{4,3,2,1,0:T(8,128)(2,1)S(1)} async-done(((bf16[8,2,3,64,256]{4,3,2,1,0:T(8,128)(2,1)}), bf16[8,2,3,64,256]{4,3,2,1,0:T(8,128)(2,1)S(1)}, u32[]{:S(2)}, u32[]{:S(2)}) %all-to-all-start.1) | async-done | bytes 1572896 | tf_op jit(solution)/shard_map/all_to_all | solution.py:41
  80.2 4.3 all-to-all-start.2
  87.6 22.0 %all-to-all-done.2 = bf16[8,72,1536]{2,1,0:T(8,128)(2,1)} async-done(((bf16[8,72,1536]{2,1,0:T(8,128)(2,1)}), bf16[8,72,1536]{2,1,0:T(8,128)(2,1)}, u32[]{:S(2)}, u32[]{:S(2)}) %all-to-all-start.2) | async-done | bytes 1769504 | tf_op jit(solution)/shard_map/all_to_all | solution.py:45
  110.6 4.2 all-to-all-start.3
  118.1 13.5 %all-to-all-done.3 = bf16[8,96,576]{2,1,0:T(8,128)(2,1)} async-done(((bf16[8,96,576]{2,1,0:T(8,128)(2,1)}), bf16[8,96,576]{2,1,0:T(8,128)(2,1)}, u32[]{:S(2)}, u32[]{:S(2)}) %all-to-all-start.3) | async-done | bytes 884768 | tf_op jit(solution)/shard_map/all_to_all | solution.py:45
  132.5 4.2 all-to-all-start.7
  141.7 15.5 %attention.2 = (f32[9,64,256]{2,1,0:T(8,128)S(1)}, f32[3,2,1,384]{3,2,1,0:T(1,128)S(1)}) custom-call(s32[39]{0:T(128)S(1)} %concatenate.119.sc, bf16[9,64,256]{2,1,0:T(8,128)(2,1)S(1)} %fusion.29.q_ref, bf16[8,2,3,64,256]{4,3,2,1,0:T(8,128)(2,1)S(1)} %all-to-all-done.1.own_ref, bf16[8,2,3,64,256]{4,3,2,1,0:T(8,128)(2,1)S(1)} %collective-permute-done.1.other_ref), custom_call_target="tpu_custom_call" | custom-call | tf_op jit(solution)/shard_map/attention/pallas_call | solution.py:225
  171.5 3.6 all-to-all-start.5
  177.1 22.5 %all-to-all-done.5.own_ref = bf16[8,2,3,64,256]{4,3,2,1,0:T(8,128)(2,1)S(1)} async-done(((bf16[8,2,3,64,256]{4,3,2,1,0:T(8,128)(2,1)}), bf16[8,2,3,64,256]{4,3,2,1,0:T(8,128)(2,1)S(1)}, u32[]{:S(2)}, u32[]{:S(2)}) %all-to-all-start.5) | async-done | bytes 1572896 | tf_op jit(solution)/shard_map/all_to_all | solution.py:41
  201.8 6.8 %all-to-all-start.6 = ((bf16[8,72,1536]{2,1,0:T(8,128)(2,1)}), bf16[8,72,1536]{2,1,0:T(8,128)(2,1)}, u32[]{:S(2)}, u32[]{:S(2)}) async-start(bf16[8,72,1536]{2,1,0:T(8,128)(2,1)} %broadcast_in_dim.43), calls=%async_computation.6 | async-start | bytes 3538944 | tf_op jit(solution)/shard_map/all_to_all | solution.py:45
  212.0 21.8 %all-to-all-done.6 = bf16[8,72,1536]{2,1,0:T(8,128)(2,1)} async-done(((bf16[8,72,1536]{2,1,0:T(8,128)(2,1)}), bf16[8,72,1536]{2,1,0:T(8,128)(2,1)}, u32[]{:S(2)}, u32[]{:S(2)}) %all-to-all-start.6) | async-done | bytes 1769504 | tf_op jit(solution)/shard_map/all_to_all | solution.py:45
  235.9 16.4 %attention.3 = (f32[9,64,256]{2,1,0:T(8,128)S(1)}, f32[3,2,1,384]{3,2,1,0:T(1,128)S(1)}) custom-call(s32[39]{0:T(128)S(1)} %concatenate.119.sc, bf16[9,64,256]{2,1,0:T(8,128)(2,1)S(1)} %fusion.26.q_ref, bf16[8,2,3,64,256]{4,3,2,1,0:T(8,128)(2,1)S(1)} %all-to-all-done.5.own_ref, bf16[8,2,3,64,256]{4,3,2,1,0:T(8,128)(2,1)} %collective-permute-done.5.other_ref), custom_call_target="tpu_custom_call" | custom-call | tf_op jit(solution)/shard_map/attention/pallas_call | solution.py:225
  266.4 23.6 %attention_back.2 = (f32[9,64,256]{2,1,0:T(8,128)S(1)}, bf16[8,2,3,64,256]{4,3,2,1,0:T(8,128)(2,1)S(1)}, bf16[8,2,3,64,256]{4,3,2,1,0:T(8,128)(2,1)}) custom-call(s32[39]{0:T(128)S(1)} %concatenate.119.sc, bf16[9,64,256]{2,1,0:T(8,128)(2,1)S(1)} %fusion.26.q_ref, bf16[8,2,3,64,256]{4,3,2,1,0:T(8,128)(2,1)S(1)} %all-to-all-done.5.own_ref, ...), custom_call_target="tpu_custom_call" | custom-call | tf_op jit(solution)/shard_map/attention_back/pallas_call | solution.py:248
  296.1 4.2 all-to-all-start.12
  302.2 3.2 add_convert_fusion.3
  305.4 11.7 %all-to-all-done.12 = bf16[8,96,576]{2,1,0:T(8,128)(2,1)} async-done(((bf16[8,96,576]{2,1,0:T(8,128)(2,1)}), bf16[8,96,576]{2,1,0:T(8,128)(2,1)}, u32[]{:S(2)}, u32[]{:S(2)}) %all-to-all-start.12) | async-done | bytes 884768 | tf_op jit(solution)/shard_map/all_to_all | solution.py:45
  317.1 4.3 all-to-all-start.8
  326.6 3.6 add_convert_fusion
  330.2 14.6 %all-to-all-done.8 = bf16[8,2,3,64,256]{4,3,2,1,0:T(8,128)(2,1)} async-done(((bf16[8,2,3,64,256]{4,3,2,1,0:T(8,128)(2,1)}), bf16[8,2,3,64,256]{4,3,2,1,0:T(8,128)(2,1)}, u32[]{:S(2)}, u32[]{:S(2)}) %all-to-all-start.8) | async-done | bytes 1572896 | tf_op jit(solution)/shard_map/all_to_all | solution.py:41
  344.8 4.3 all-to-all-start.11
  366.0 8.1 %all-to-all-done.11 = bf16[8,72,1536]{2,1,0:T(8,128)(2,1)} async-done(((bf16[8,72,1536]{2,1,0:T(8,128)(2,1)}), bf16[8,72,1536]{2,1,0:T(8,128)(2,1)}, u32[]{:S(2)}, u32[]{:S(2)}) %all-to-all-start.11) | async-done | bytes 1769504 | tf_op jit(solution)/shard_map/all_to_all | solution.py:45
  374.1 4.2 all-to-all-start.13
  380.8 3.0 multiply_reduce_fusion.2
  385.6 8.4 %all-to-all-done.13 = bf16[8,72,768]{2,1,0:T(8,128)(2,1)} async-done(((bf16[8,72,768]{2,1,0:T(8,128)(2,1)}), bf16[8,72,768]{2,1,0:T(8,128)(2,1)}, u32[]{:S(2)}, u32[]{:S(2)}) %all-to-all-start.13) | async-done | bytes 884768 | tf_op jit(solution)/shard_map/all_to_all | solution.py:45
  397.5 8.8 %collective-permute-done.20 = bf16[72,3072]{1,0:T(8,128)(2,1)S(1)} collective-permute-done((bf16[72,3072]{1,0:T(8,128)(2,1)S(1)}, bf16[72,3072]{1,0:T(8,128)(2,1)S(1)}, u32[]{:S(2)}, u32[]{:S(2)}) %collective-permute-start.20) | collective-permute-done | bytes 442400 | tf_op jit(solution)/shard_map/ppermute | solution.py:63
  409.7 3.3 add_convert_fusion.1
  415.2 4.4 all-to-all-start.15
  426.6 22.7 %attention_back.3 = (f32[9,64,256]{2,1,0:T(8,128)S(1)}, bf16[8,2,3,64,256]{4,3,2,1,0:T(8,128)(2,1)S(1)}, bf16[8,2,3,64,256]{4,3,2,1,0:T(8,128)(2,1)}) custom-call(s32[39]{0:T(128)S(1)} %concatenate.119.sc, bf16[9,64,256]{2,1,0:T(8,128)(2,1)S(1)} %fusion.29.q_ref, bf16[8,2,3,64,256]{4,3,2,1,0:T(8,128)(2,1)S(1)} %all-to-all-done.1.own_ref, ...), custom_call_target="tpu_custom_call" | custom-call | tf_op jit(solution)/shard_map/attention_back/pallas_call | solution.py:248
  452.6 6.9 %all-to-all-start.14 = ((bf16[8,72,1536]{2,1,0:T(8,128)(2,1)}), bf16[8,72,1536]{2,1,0:T(8,128)(2,1)}, u32[]{:S(2)}, u32[]{:S(2)}) async-start(bf16[8,72,1536]{2,1,0:T(8,128)(2,1)} %bitcast.189), calls=%async_computation.14 | async-start | bytes 3538944 | tf_op jit(solution)/shard_map/all_to_all | solution.py:45
  467.3 17.5 %all-to-all-done.14 = bf16[8,72,1536]{2,1,0:T(8,128)(2,1)} async-done(((bf16[8,72,1536]{2,1,0:T(8,128)(2,1)}), bf16[8,72,1536]{2,1,0:T(8,128)(2,1)}, u32[]{:S(2)}, u32[]{:S(2)}) %all-to-all-start.14) | async-done | bytes 1769504 | tf_op jit(solution)/shard_map/all_to_all | solution.py:45
  489.2 3.2 add_convert_fusion.2
  492.4 4.9 all-to-all-start.9
  505.9 3.6 pad_maximum_fusion.11
  512.2 11.3 %collective-permute-done.25 = bf16[72,2304]{1,0:T(8,128)(2,1)} collective-permute-done((bf16[72,2304]{1,0:T(8,128)(2,1)}, bf16[72,2304]{1,0:T(8,128)(2,1)}, u32[]{:S(2)}, u32[]{:S(2)}) %collective-permute-start.25) | collective-permute-done | bytes 331808 | tf_op jit(solution)/shard_map/ppermute | solution.py:63
  524.7 3.7 collective-permute-start.26
  542.8 5.8 all-to-all-start.10
  553.6 3.1 stack_reshape.17
  556.7 3.5 pad_maximum_fusion.10
  562.1 3.7 all-to-all-done.10
  574.2 3.0 collective-permute-start.15
  577.3 3.1 collective-permute-done.15
  580.4 3.3 collective-permute-start.16
  (448 shorter events, 181.9 us)
Async XLA Ops:
  4.6 25.3 %all-to-all-start = ((bf16[8,72,772]{2,1,0:T(8,128)(2,1)}), bf16[8,72,772]{2,1,0:T(8,128)(2,1)S(1)}, u32[]{:S(2)}, u32[]{:S(2)}) async-start(bf16[8,72,772]{2,1,0:T(8,128)(2,1)} %broadcast_in_dim.32), calls=%async_computation | async-start | bytes 2064384 | tf_op jit(solution)/shard_map/all_to_all | solution.py:45
  30.8 19.1 %all-to-all-start.4 = ((bf16[8,72,768]{2,1,0:T(8,128)(2,1)}), bf16[8,72,768]{2,1,0:T(8,128)(2,1)S(1)}, u32[]{:S(2)}, u32[]{:S(2)}) async-start(bf16[8,72,768]{2,1,0:T(8,128)(2,1)} %broadcast_in_dim.40), calls=%async_computation.4 | async-start | bytes 1769472 | tf_op jit(solution)/shard_map/all_to_all | solution.py:45
  36.0 3.4 collective-permute-start
  37.7 313.3 %copy-start.74 = (f32[32,256]{1,0:T(8,128)}, f32[32,256]{1,0:T(8,128)S(1)}, u32[]{:S(2)}) copy-start(f32[32,256]{1,0:T(8,128)S(1)} %get-tuple-element.89) | copy-start | bytes 98308
  51.4 27.5 %all-to-all-start.1 = ((bf16[8,2,3,64,256]{4,3,2,1,0:T(8,128)(2,1)}), bf16[8,2,3,64,256]{4,3,2,1,0:T(8,128)(2,1)S(1)}, u32[]{:S(2)}, u32[]{:S(2)}) async-start(bf16[8,2,3,64,256]{4,3,2,1,0:T(8,128)(2,1)} %broadcast_in_dim.35), calls=%async_computation.1 | async-start | bytes 3145728 | tf_op jit(solution)/shard_map/all_to_all | solution.py:41
  80.2 29.4 %all-to-all-start.2 = ((bf16[8,72,1536]{2,1,0:T(8,128)(2,1)}), bf16[8,72,1536]{2,1,0:T(8,128)(2,1)}, u32[]{:S(2)}, u32[]{:S(2)}) async-start(bf16[8,72,1536]{2,1,0:T(8,128)(2,1)} %broadcast_in_dim.37), calls=%async_computation.2 | async-start | bytes 3538944 | tf_op jit(solution)/shard_map/all_to_all | solution.py:45
  84.6 57.1 %collective-permute-start.1 = (bf16[8,2,3,64,256]{4,3,2,1,0:T(8,128)(2,1)S(1)}, bf16[8,2,3,64,256]{4,3,2,1,0:T(8,128)(2,1)S(1)}, u32[]{:S(2)}, u32[]{:S(2)}) collective-permute-start(bf16[8,2,3,64,256]{4,3,2,1,0:T(8,128)(2,1)S(1)} %all-to-all-done.1.own_ref), channel_id=1, source_target_pairs={{0,8},{8,0},{16,24},{24,16},{32,40},{40,32},{48,56},{56,48},{64,72... | collective-permute-start | bytes 4718600 | tf_op jit(solution)/shard_map/ppermute | solution.py:37
  87.4 30.3 %copy-start.97 = (s32[1,4096]{1,0:T(1,128)S(1)}, s32[1,4096]{1,0:T(1,128)}, u32[]{:S(2)}) copy-start(s32[1,4096]{1,0:T(1,128)} %param.11) | copy-start | bytes 49156
  87.4 52.5 %collective-permute-start.4 = (bf16[576,768]{1,0:T(8,128)(2,1)}, bf16[576,768]{1,0:T(8,128)(2,1)}, u32[]{:S(2)}, u32[]{:S(2)}) collective-permute-start(bf16[576,768]{1,0:T(8,128)(2,1)} %bitcast.194), channel_id=1, source_target_pairs={{0,8},{8,0},{16,24},{24,16},{32,40},{40,32},{48,56},{56,48},{64,72... | collective-permute-start | bytes 2654216 | tf_op jit(solution)/shard_map/ppermute | solution.py:37
  110.6 20.9 %all-to-all-start.3 = ((bf16[8,96,576]{2,1,0:T(8,128)(2,1)}), bf16[8,96,576]{2,1,0:T(8,128)(2,1)}, u32[]{:S(2)}, u32[]{:S(2)}) async-start(bf16[8,96,576]{2,1,0:T(8,128)(2,1)} %broadcast_in_dim.39), calls=%async_computation.3 | async-start | bytes 1966080 | tf_op jit(solution)/shard_map/all_to_all | solution.py:45
  114.9 43.5 %collective-permute-start.2 = (bf16[576,1536]{1,0:T(8,128)(2,1)}, bf16[576,1536]{1,0:T(8,128)(2,1)}, u32[]{:S(2)}, u32[]{:S(2)}) collective-permute-start(bf16[576,1536]{1,0:T(8,128)(2,1)} %bitcast.16), channel_id=1, source_target_pairs={{0,8},{8,0},{16,24},{24,16},{32,40},{40,32},{48,56},{56,48},{64,72... | collective-permute-start | bytes 5308424 | tf_op jit(solution)/shard_map/ppermute | solution.py:37
  132.5 37.6 %all-to-all-start.7 = ((bf16[8,96,576]{2,1,0:T(8,128)(2,1)}), bf16[8,96,576]{2,1,0:T(8,128)(2,1)}, u32[]{:S(2)}, u32[]{:S(2)}) async-start(bf16[8,96,576]{2,1,0:T(8,128)(2,1)} %broadcast_in_dim.45), calls=%async_computation.7 | async-start | bytes 1966080 | tf_op jit(solution)/shard_map/all_to_all | solution.py:45
  139.0 28.1 %collective-permute-start.3 = (bf16[768,576]{0,1:T(8,128)(2,1)}, bf16[768,576]{0,1:T(8,128)(2,1)S(1)}, u32[]{:S(2)}, u32[]{:S(2)}) collective-permute-start(bf16[768,576]{0,1:T(8,128)(2,1)} %copy.96), channel_id=1, source_target_pairs={{0,8},{8,0},{16,24},{24,16},{32,40},{40,32},{48,56},{56,48},{64,72... | collective-permute-start | bytes 2654216 | tf_op jit(solution)/shard_map/ppermute | solution.py:37
  171.5 28.0 %all-to-all-start.5 = ((bf16[8,2,3,64,256]{4,3,2,1,0:T(8,128)(2,1)}), bf16[8,2,3,64,256]{4,3,2,1,0:T(8,128)(2,1)S(1)}, u32[]{:S(2)}, u32[]{:S(2)}) async-start(bf16[8,2,3,64,256]{4,3,2,1,0:T(8,128)(2,1)} %broadcast_in_dim.41), calls=%async_computation.5 | async-start | bytes 3145728 | tf_op jit(solution)/shard_map/all_to_all | solution.py:41
  201.8 31.9 %all-to-all-start.6 = ((bf16[8,72,1536]{2,1,0:T(8,128)(2,1)}), bf16[8,72,1536]{2,1,0:T(8,128)(2,1)}, u32[]{:S(2)}, u32[]{:S(2)}) async-start(bf16[8,72,1536]{2,1,0:T(8,128)(2,1)} %broadcast_in_dim.43), calls=%async_computation.6 | async-start | bytes 3538944 | tf_op jit(solution)/shard_map/all_to_all | solution.py:45
  208.6 27.3 %collective-permute-start.5 = (bf16[8,2,3,64,256]{4,3,2,1,0:T(8,128)(2,1)S(1)}, bf16[8,2,3,64,256]{4,3,2,1,0:T(8,128)(2,1)}, u32[]{:S(2)}, u32[]{:S(2)}) collective-permute-start(bf16[8,2,3,64,256]{4,3,2,1,0:T(8,128)(2,1)S(1)} %all-to-all-done.5.own_ref), channel_id=1, source_target_pairs={{0,8},{8,0},{16,24},{24,16},{32,40},{40,32},{48,56},{56,48},{64,72... | collective-permute-start | bytes 4718600 | tf_op jit(solution)/shard_map/ppermute | solution.py:37
  212.0 49.5 %collective-permute-start.7 = (bf16[768,576]{0,1:T(8,128)(2,1)}, bf16[768,576]{0,1:T(8,128)(2,1)}, u32[]{:S(2)}, u32[]{:S(2)}) collective-permute-start(bf16[768,576]{0,1:T(8,128)(2,1)} %copy.97), channel_id=1, source_target_pairs={{0,8},{8,0},{16,24},{24,16},{32,40},{40,32},{48,56},{56,48},{64,72... | collective-permute-start | bytes 2654216 | tf_op jit(solution)/shard_map/ppermute | solution.py:37
  233.8 26.8 %collective-permute-start.6 = (bf16[576,1536]{1,0:T(8,128)(2,1)}, bf16[576,1536]{1,0:T(8,128)(2,1)S(1)}, u32[]{:S(2)}, u32[]{:S(2)}) collective-permute-start(bf16[576,1536]{1,0:T(8,128)(2,1)} %bitcast.27), channel_id=1, source_target_pairs={{0,8},{8,0},{16,24},{24,16},{32,40},{40,32},{48,56},{56,48},{64,72... | collective-permute-start | bytes 5308424 | tf_op jit(solution)/shard_map/ppermute | solution.py:37
  258.0 34.4 %copy-start.55 = (bf16[256,768]{1,0:T(8,128)(2,1)}, bf16[256,768]{1,0:T(8,128)(2,1)S(1)}, u32[]{:S(2)}) copy-start(bf16[256,768]{1,0:T(8,128)(2,1)S(1)} %get-tuple-element.60) | copy-start | bytes 1179652
  264.9 27.6 %collective-permute-start.18 = (bf16[768,576]{0,1:T(8,128)(2,1)S(1)}, bf16[768,576]{0,1:T(8,128)(2,1)S(1)}, u32[]{:S(2)}, u32[]{:S(2)}) collective-permute-start(bf16[768,576]{0,1:T(8,128)(2,1)S(1)} %convolution_convert_fusion.6), channel_id=1, source_target_pairs={{0,8},{8,0},{16,24},{24,16},{32,40},{40,32},{48,56},{56,48},{64,72... | collective-permute-start | bytes 2654216 | tf_op jit(solution)/shard_map/ppermute | solution.py:37
  292.0 10.3 %collective-permute-start.8 = (bf16[8,2,3,64,256]{4,3,2,1,0:T(8,128)(2,1)}, bf16[8,2,3,64,256]{4,3,2,1,0:T(8,128)(2,1)}, u32[]{:S(2)}, u32[]{:S(2)}) collective-permute-start(bf16[8,2,3,64,256]{4,3,2,1,0:T(8,128)(2,1)} %get-tuple-element.25), channel_id=1, source_target_pairs={{0,8},{8,0},{16,24},{24,16},{32,40},{40,32},{48,56},{56,48},{64,72... | collective-permute-start | bytes 4718600 | tf_op jit(solution)/shard_map/ppermute | solution.py:37
  296.1 21.0 %all-to-all-start.12 = ((bf16[8,96,576]{2,1,0:T(8,128)(2,1)}), bf16[8,96,576]{2,1,0:T(8,128)(2,1)}, u32[]{:S(2)}, u32[]{:S(2)}) async-start(bf16[8,96,576]{2,1,0:T(8,128)(2,1)} %bitcast.192), calls=%async_computation.12 | async-start | bytes 1966080 | tf_op jit(solution)/shard_map/all_to_all | solution.py:45
  302.2 24.4 %collective-permute-start.17 = (bf16[576,1536]{1,0:T(8,128)(2,1)}, bf16[576,1536]{1,0:T(8,128)(2,1)}, u32[]{:S(2)}, u32[]{:S(2)}) collective-permute-start(bf16[576,1536]{1,0:T(8,128)(2,1)} %convolution_convert_fusion), channel_id=1, source_target_pairs={{0,8},{8,0},{16,24},{24,16},{32,40},{40,32},{48,56},{56,48},{64,72... | collective-permute-start | bytes 5308424 | tf_op jit(solution)/shard_map/ppermute | solution.py:37
  317.1 27.7 %all-to-all-start.8 = ((bf16[8,2,3,64,256]{4,3,2,1,0:T(8,128)(2,1)}), bf16[8,2,3,64,256]{4,3,2,1,0:T(8,128)(2,1)}, u32[]{:S(2)}, u32[]{:S(2)}) async-start(bf16[8,2,3,64,256]{4,3,2,1,0:T(8,128)(2,1)} %add_convert_fusion.3), calls=%async_computation.8 | async-start | bytes 3145728 | tf_op jit(solution)/shard_map/all_to_all | solution.py:41
  344.8 29.4 %all-to-all-start.11 = ((bf16[8,72,1536]{2,1,0:T(8,128)(2,1)}), bf16[8,72,1536]{2,1,0:T(8,128)(2,1)}, u32[]{:S(2)}, u32[]{:S(2)}) async-start(bf16[8,72,1536]{2,1,0:T(8,128)(2,1)} %bitcast.190), calls=%async_computation.11 | async-start | bytes 3538944 | tf_op jit(solution)/shard_map/all_to_all | solution.py:45
  355.9 51.2 %collective-permute-start.10 = (bf16[768,576]{0,1:T(8,128)(2,1)}, bf16[768,576]{0,1:T(8,128)(2,1)}, u32[]{:S(2)}, u32[]{:S(2)}) collective-permute-start(bf16[768,576]{0,1:T(8,128)(2,1)} %convolution_convert_fusion.8), channel_id=1, source_target_pairs={{0,8},{8,0},{16,24},{24,16},{32,40},{40,32},{48,56},{56,48},{64,72... | collective-permute-start | bytes 2654216 | tf_op jit(solution)/shard_map/ppermute | solution.py:37
  357.9 6.5 %collective-permute-start.19 = (bf16[576,768]{1,0:T(8,128)(2,1)S(1)}, bf16[576,768]{1,0:T(8,128)(2,1)S(1)}, u32[]{:S(2)}, u32[]{:S(2)}) collective-permute-start(bf16[576,768]{1,0:T(8,128)(2,1)S(1)} %broadcast_select_fusion.1), channel_id=1, source_target_pairs={{0,8},{8,0},{16,24},{24,16},{32,40},{40,32},{48,56},{56,48},{64,72... | collective-permute-start | bytes 2654216 | tf_op jit(solution)/shard_map/ppermute | solution.py:37
  360.7 48.9 %collective-permute-start.9 = (bf16[576,1536]{1,0:T(8,128)(2,1)}, bf16[576,1536]{1,0:T(8,128)(2,1)}, u32[]{:S(2)}, u32[]{:S(2)}) collective-permute-start(bf16[576,1536]{1,0:T(8,128)(2,1)} %convolution_convert_fusion.2), channel_id=1, source_target_pairs={{0,8},{8,0},{16,24},{24,16},{32,40},{40,32},{48,56},{56,48},{64,72... | collective-permute-start | bytes 5308424 | tf_op jit(solution)/shard_map/ppermute | solution.py:37
  374.1 19.8 %all-to-all-start.13 = ((bf16[8,72,768]{2,1,0:T(8,128)(2,1)}), bf16[8,72,768]{2,1,0:T(8,128)(2,1)}, u32[]{:S(2)}, u32[]{:S(2)}) async-start(bf16[8,72,768]{2,1,0:T(8,128)(2,1)} %bitcast.193), calls=%async_computation.13 | async-start | bytes 1769472 | tf_op jit(solution)/shard_map/all_to_all | solution.py:45
  395.3 10.9 %collective-permute-start.20 = (bf16[72,3072]{1,0:T(8,128)(2,1)S(1)}, bf16[72,3072]{1,0:T(8,128)(2,1)S(1)}, u32[]{:S(2)}, u32[]{:S(2)}) collective-permute-start(bf16[72,3072]{1,0:T(8,128)(2,1)S(1)} %pad_maximum_fusion.25), channel_id=1, source_target_pairs={{0,16},{8,24},{16,0},{24,8},{32,48},{40,56},{48,32},{56,40},{64,80... | collective-permute-start | bytes 1327112 | tf_op jit(solution)/shard_map/ppermute | solution.py:63
  407.1 12.4 %collective-permute-start.21 = (bf16[72,3072]{1,0:T(8,128)(2,1)}, bf16[72,3072]{1,0:T(8,128)(2,1)}, u32[]{:S(2)}, u32[]{:S(2)}) collective-permute-start(bf16[72,3072]{1,0:T(8,128)(2,1)} %add_convert_fusion.10), channel_id=1, source_target_pairs={{0,32},{8,40},{16,48},{24,56},{32,0},{40,8},{48,16},{56,24},{64,96... | collective-permute-start | bytes 1327112 | tf_op jit(solution)/shard_map/ppermute | solution.py:63
  415.2 37.4 %all-to-all-start.15 = ((bf16[8,96,576]{2,1,0:T(8,128)(2,1)}), bf16[8,96,576]{2,1,0:T(8,128)(2,1)}, u32[]{:S(2)}, u32[]{:S(2)}) async-start(bf16[8,96,576]{2,1,0:T(8,128)(2,1)} %bitcast.191), calls=%async_computation.15 | async-start | bytes 1966080 | tf_op jit(solution)/shard_map/all_to_all | solution.py:45
  421.7 37.9 %collective-permute-start.22 = (bf16[72,3072]{1,0:T(8,128)(2,1)}, bf16[72,3072]{1,0:T(8,128)(2,1)}, u32[]{:S(2)}, u32[]{:S(2)}) collective-permute-start(bf16[72,3072]{1,0:T(8,128)(2,1)} %add_convert_fusion.9), channel_id=1, source_target_pairs={{0,64},{8,72},{16,80},{24,88},{32,96},{40,104},{48,112},{56,120},{... | collective-permute-start | bytes 1327112 | tf_op jit(solution)/shard_map/ppermute | solution.py:63
  450.5 38.6 %collective-permute-start.11 = (bf16[8,2,3,64,256]{4,3,2,1,0:T(8,128)(2,1)}, bf16[8,2,3,64,256]{4,3,2,1,0:T(8,128)(2,1)}, u32[]{:S(2)}, u32[]{:S(2)}) collective-permute-start(bf16[8,2,3,64,256]{4,3,2,1,0:T(8,128)(2,1)} %get-tuple-element.30), channel_id=1, source_target_pairs={{0,8},{8,0},{16,24},{24,16},{32,40},{40,32},{48,56},{56,48},{64,72... | collective-permute-start | bytes 4718600 | tf_op jit(solution)/shard_map/ppermute | solution.py:37
  452.6 32.2 %all-to-all-start.14 = ((bf16[8,72,1536]{2,1,0:T(8,128)(2,1)}), bf16[8,72,1536]{2,1,0:T(8,128)(2,1)}, u32[]{:S(2)}, u32[]{:S(2)}) async-start(bf16[8,72,1536]{2,1,0:T(8,128)(2,1)} %bitcast.189), calls=%async_computation.14 | async-start | bytes 3538944 | tf_op jit(solution)/shard_map/all_to_all | solution.py:45
  460.8 4.9 collective-permute-start.23
  465.4 35.1 %collective-permute-start.28 = (bf16[72,2304]{1,0:T(8,128)(2,1)}, bf16[72,2304]{1,0:T(8,128)(2,1)}, u32[]{:S(2)}, u32[]{:S(2)}) collective-permute-start(bf16[72,2304]{1,0:T(8,128)(2,1)} %slice.413), channel_id=1, source_target_pairs={{0,8},{8,0},{16,24},{24,16},{32,40},{40,32},{48,56},{56,48},{64,72... | collective-permute-start | bytes 995336 | tf_op jit(solution)/shard_map/ppermute | solution.py:37
  488.1 9.1 %collective-permute-start.24 = (bf16[72,2304]{1,0:T(8,128)(2,1)}, bf16[72,2304]{1,0:T(8,128)(2,1)}, u32[]{:S(2)}, u32[]{:S(2)}) collective-permute-start(bf16[72,2304]{1,0:T(8,128)(2,1)} %pad_maximum_fusion.29), channel_id=1, source_target_pairs={{0,16},{8,24},{16,0},{24,8},{32,48},{40,56},{48,32},{56,40},{64,80... | collective-permute-start | bytes 995336 | tf_op jit(solution)/shard_map/ppermute | solution.py:63
  492.4 36.0 %all-to-all-start.9 = ((bf16[8,2,3,64,256]{4,3,2,1,0:T(8,128)(2,1)}), bf16[8,2,3,64,256]{4,3,2,1,0:T(8,128)(2,1)S(1)}, u32[]{:S(2)}, u32[]{:S(2)}) async-start(bf16[8,2,3,64,256]{4,3,2,1,0:T(8,128)(2,1)} %add_convert_fusion.2), calls=%async_computation.9 | async-start | bytes 3145728 | tf_op jit(solution)/shard_map/all_to_all | solution.py:41
  499.1 24.4 %collective-permute-start.25 = (bf16[72,2304]{1,0:T(8,128)(2,1)}, bf16[72,2304]{1,0:T(8,128)(2,1)}, u32[]{:S(2)}, u32[]{:S(2)}) collective-permute-start(bf16[72,2304]{1,0:T(8,128)(2,1)} %add_convert_fusion.13), channel_id=1, source_target_pairs={{0,32},{8,40},{16,48},{24,56},{32,0},{40,8},{48,16},{56,24},{64,96... | collective-permute-start | bytes 995336 | tf_op jit(solution)/shard_map/ppermute | solution.py:63
  524.7 10.1 %collective-permute-start.26 = (bf16[72,2304]{1,0:T(8,128)(2,1)S(1)}, bf16[72,2304]{1,0:T(8,128)(2,1)}, u32[]{:S(2)}, u32[]{:S(2)}) collective-permute-start(bf16[72,2304]{1,0:T(8,128)(2,1)S(1)} %add_convert_fusion.12), channel_id=1, source_target_pairs={{0,64},{8,72},{16,80},{24,88},{32,96},{40,104},{48,112},{56,120},{... | collective-permute-start | bytes 995336 | tf_op jit(solution)/shard_map/ppermute | solution.py:63
  531.6 8.4 %collective-permute-start.12 = (bf16[576,768]{1,0:T(8,128)(2,1)}, bf16[576,768]{1,0:T(8,128)(2,1)}, u32[]{:S(2)}, u32[]{:S(2)}) collective-permute-start(bf16[576,768]{1,0:T(8,128)(2,1)} %broadcast_select_fusion.2), channel_id=1, source_target_pairs={{0,8},{8,0},{16,24},{24,16},{32,40},{40,32},{48,56},{56,48},{64,72... | collective-permute-start | bytes 2654216 | tf_op jit(solution)/shard_map/ppermute | solution.py:37
  535.9 12.7 %collective-permute-start.27 = (bf16[72,2304]{1,0:T(8,128)(2,1)S(1)}, bf16[72,2304]{1,0:T(8,128)(2,1)}, u32[]{:S(2)}, u32[]{:S(2)}) collective-permute-start(bf16[72,2304]{1,0:T(8,128)(2,1)S(1)} %add_convert_fusion.11), channel_id=1, source_target_pairs={{0,8},{8,0},{16,24},{24,16},{32,40},{40,32},{48,56},{56,48},{64,72... | collective-permute-start | bytes 995336 | tf_op jit(solution)/shard_map/ppermute | solution.py:37
  542.8 23.0 %all-to-all-start.10 = ((bf16[8,72,772]{2,1,0:T(8,128)(2,1)}), bf16[8,72,772]{2,1,0:T(8,128)(2,1)S(1)}, u32[]{:S(2)}, u32[]{:S(2)}) async-start(bf16[8,72,772]{2,1,0:T(8,128)(2,1)} %bitcast.47), calls=%async_computation.10 | async-start | bytes 2064384 | tf_op jit(solution)/shard_map/all_to_all | solution.py:45
  566.0 4.3 collective-permute-start.13
  570.3 3.9 collective-permute-start.14
  574.2 6.1 %collective-permute-start.15 = (bf16[72,772]{1,0:T(8,128)(2,1)S(1)}, bf16[72,772]{1,0:T(8,128)(2,1)S(1)}, u32[]{:S(2)}, u32[]{:S(2)}) collective-permute-start(bf16[72,772]{1,0:T(8,128)(2,1)S(1)} %add_convert_fusion.17), channel_id=1, source_target_pairs={{0,64},{8,72},{16,80},{24,88},{32,96},{40,104},{48,112},{56,120},{... | collective-permute-start | bytes 333512 | tf_op jit(solution)/shard_map/ppermute | solution.py:63
  580.4 4.3 collective-permute-start.16
  (102 other events, 591.6 us)

commit v3 on v2

--- a/solution.py
+++ b/solution.py
@@ -307,19 +307,23 @@
     wgu_cut = w_gate_up.reshape(LAYERS, SHARD, 2, FSDP, 2, FF // FSDP // 2)
     wgu_cut = my_half(wgu_cut[..., 0, :], wgu_cut[..., 1, :]).reshape(LAYERS, SHARD, FF)
     wd_cut = w_down.reshape(LAYERS, 2, FF // FSDP // 2, D)
-    wd_cut = my_half(wd_cut[:, 0], wd_cut[:, 1])
-    projs, mlps = [], []
-    for layer in range(LAYERS):
-        proj = jnp.concatenate([w_qkv[layer], w_out[layer]], 1)
-        proj = my_half(proj[:, :cut], proj[:, cut:])
-        if layer == 0:
-            proj = jnp.concatenate([proj, gain_cols], 1)
-        own = gather_fsdp(proj)
-        if layer == 0:
-            gains = jnp.transpose(own[:, cut:].astype(F32)).reshape(LAYERS, 2, D)
-        pair = in_order(own, to_partner(own))
-        projs.append(jnp.concatenate([half[:, :cut] for half in pair], 1))
-        wgu, wdown = gather_fsdp(wgu_cut[layer]), gather_fsdp(wd_cut[layer])
+    wd_cut = my_half(wd_cut[:, 0], wd_cut[:, 1]).reshape(LAYERS, SHARD, HALF)
+    proj_cut = jnp.concatenate([w_qkv, w_out], 2)
+    proj_cut = my_half(proj_cut[..., :cut], proj_cut[..., cut:])
+    first = jnp.concatenate([proj_cut[0], gain_cols], 1)
+    packs = [
+        jnp.concatenate([wgu_cut[0], wd_cut[0]], 1),
+        jnp.concatenate([wgu_cut[1], wd_cut[1], proj_cut[1]], 1),
+    ]
+    packs[0], first = lax.optimization_barrier((packs[0], first))
+    packs = [lax.all_gather(p, "fsdp", axis=0, tiled=True) for p in packs]
+    first = gather_fsdp(first)
+    gains = jnp.transpose(first[:, cut:].astype(F32)).reshape(LAYERS, 2, D)
+    projs = [first[:, :cut], packs[1][:, FF + HALF :]]
+    projs = [jnp.concatenate(in_order(own, to_partner(own)), 1) for own in projs]
+    mlps = []
+    for pack in packs:
+        wgu, wdown = pack[:, :FF], pack[:, FF : FF + HALF].reshape(HALF, D)
         mlps.append([(wgu, wdown), (to_partner(wgu), to_partner(wdown))])
 
     first_block = lax.dynamic_index_in_dim(block_order, 2 * place, 0, keepdims=False)
@@ -386,14 +390,16 @@
             wd_parts.append(ein("tf,td->fd", inner, grad_b).astype(BF16))
             wgu_parts.append(ein("td,tf->df", mlp_in, d_gu).astype(BF16))
         d_wgu = sum_pair(wgu_parts[0], to_partner(wgu_parts[1]))
-        d_wdown = sum_pair(wd_parts[0], to_partner(wd_parts[1]))
+        d_wdown = sum_pair(wd_parts[0], to_partner(wd_parts[1])).reshape(D, HALF)
+        d_mlp = jnp.concatenate([d_wgu, d_wdown], 1)
         d_gain_m = jnp.sum(d_norm * unit_m, 0)
         d_hidden = d_hidden + norm_back(d_norm * gains[layer, 1], unit_m, rms_m)
         grad_b = d_hidden.astype(BF16)
         d_wout = mm(attn_out, grad_b)
         do_t = ein("ad,td->at", wout, grad_b).astype(BF16).reshape(HEADS, HEAD_DIM, ROWS)
         if layer == 0:
-            do_t, d_wgu, d_wdown = lax.optimization_barrier((do_t, d_wgu, d_wdown))
+            do_t, d_mlp = lax.optimization_barrier((do_t, d_mlp))
+        mlp_share = lax.psum_scatter(d_mlp, "fsdp", scatter_dimension=0, tiled=True)
         dq_t, dkv_own, dkv_other = attention_back(scalars, q_t, kv_own, kv_other, o_t, do_t, lse)
         dkv = (dkv_own.astype(F32) + to_partner(dkv_other).astype(F32)).astype(BF16)
         dkv = jnp.sum(over_chips(dkv).astype(F32), 0)
@@ -411,15 +417,7 @@
         if layer == 0:
             d_gains = jnp.transpose(jnp.stack(gain_grads).reshape(2 * LAYERS, D)).astype(BF16)
             d_proj = jnp.concatenate([d_proj, d_gains], 1)
-        mlp_share = jnp.concatenate(
-            [scatter_fsdp(d_wgu), scatter_fsdp(d_wdown).reshape(SHARD, HALF)], 1
-        )
-        proj_share = scatter_fsdp(d_proj)
-        if layer == 0:
-            shares[layer] = sum_chips(mlp_share), sum_chips(proj_share)
-        else:
-            both = sum_chips(jnp.concatenate([mlp_share, proj_share], 1))
-            shares[layer] = both[:, : FF + HALF], both[:, FF + HALF :]
+        shares[layer] = sum_chips(mlp_share), sum_chips(scatter_fsdp(d_proj))
     input_grad = d_hidden.reshape(1, ROWS, D)
 
     proj_grads, gate_up_grad, down_grad = [], [], []

time: 599 us -> 550 us (0.918)
  blocking collectives: 0 us -> 68.6 us
  starting transfers between devices: 111 us -> 53.3 us
  waiting for transfers between devices: 209 us -> 172 us
  other arithmetic: 58.4 us -> 39.2 us
  between operations: 5.65 us -> 18.4 us
  local copies, waits for them, and re-layouts: 69.6 us -> 61.9 us
  matrix products: 56.5 us -> 49.9 us
    all_to_all x12 -> x2, waiting for transfers between devices: 127 us -> 33.7 us  [over_fsdp(): return lax.all_to_all(x, 'fsdp', 0, 0, tiled=True)]
    all_to_all x0 -> x3, blocking collectives: none -> 68.6 us  [the longest x2 49.4 us: over_chips(): lax.all_to_all(x, 'ctx', 0, 0, axis_index_groups=SAME_CORE, tiled=True)]
    all_gather x0 -> x2, waiting for transfers between devices: none -> 49.6 us  [local(): packs = [lax.all_gather(p, 'fsdp', axis=0, tiled=True) for p in packs]]
    all_to_all x12 -> x2, starting transfers between devices: 61.2 us -> 11.9 us  [over_fsdp(): return lax.all_to_all(x, 'fsdp', 0, 0, tiled=True)]
    all_to_all x4 -> x2, waiting for transfers between devices: 52.6 us -> 9.99 us  [over_chips(): lax.all_to_all(x, 'ctx', 0, 0, axis_index_groups=SAME_CORE, tiled=True)]
    ppermute x9 -> x12, waiting for transfers between devices: 28 us -> 52.8 us  [sum_chips(): x = sum_pair(x, lax.ppermute(x, 'ctx', [(i, i ^ bit) for i in range(CTX)]))]
    reduce_scatter x0 -> x2, waiting for transfers between devices: none -> 23.1 us  [local(): mlp_share = lax.psum_scatter(d_mlp, 'fsdp', scatter_dimension=0, tiled=True)]
    broadcast_in_dim x9 -> x1, local copies, waits for them, and re-layouts: 9.88 us -> 1.04 us  [gather_fsdp(): jnp.broadcast_to(x[None], (FSDP,) + x.shape)]
  transfers between devices with their start and end apart: 45 -> 40, of which waited for: 20 -> 18; matrix products, arithmetic and copies ran while one was open for 27% -> 20% of each run, Pallas kernels for 13% -> 10%
where the time goes in v3:
time: 550 us; the launch traced here: 541 us
  waiting for transfers between devices  172 us (31%)
  Pallas kernels  77.5 us (14%)
  blocking collectives  68.6 us (12%)
  local copies, waits for them, and re-layouts  61.9 us (11%)
  starting transfers between devices  53.3 us (10%)
  matrix products  49.9 us (9%)
  other arithmetic  39.2 us (7%)
  between operations  18.4 us (3%)
    ppermute x12, waiting for transfers between devices, sum_chips(): x = sum_pair(x, lax.ppermute(x, 'ctx', [(i, i ^ bit) for i in range(CTX)]))  52.8 us
    all_gather x2, waiting for transfers between devices, local(): packs = [lax.all_gather(p, 'fsdp', axis=0, tiled=True) for p in packs]  49.6 us
    all_to_all x2, blocking collectives, over_chips(): lax.all_to_all(x, 'ctx', 0, 0, axis_index_groups=SAME_CORE, tiled=True)  49.4 us
    pallas_call x2, Pallas kernels, attention_back(): pl.pallas_call(backward_kernel, grid_spec=pltpu.PrefetchScalarGridSpec(nu...  45.7 us
    dot_general x26, matrix products, ein(): return jnp.einsum(spec, a, b, preferred_element_type=F32)  35 us
    all_to_all x2, waiting for transfers between devices, over_fsdp(): return lax.all_to_all(x, 'fsdp', 0, 0, tiled=True)  33.7 us
    pallas_call x2, Pallas kernels, attention(): pl.pallas_call(forward_kernel, grid_spec=pltpu.PrefetchScalarGridSpec(num...  31.8 us
    reduce_scatter x2, waiting for transfers between devices, local(): mlp_share = lax.psum_scatter(d_mlp, 'fsdp', scatter_dimension=0, tiled=True)  23.1 us
  transfers between devices with their start and end apart: 40, of which 18 were waited for; matrix products, arithmetic and copies ran while one was open for 20% of the time, Pallas kernels for 10%

profile of v3, /device:TPU:1, one launch (start us, length us, event | category | flops | bytes accessed | tf_op | source)
XLA Modules:
  0.0 540.7 jit_solution(12650943939975723545)
XLA Ops:
  7.2 4.4 reshape.392
  16.8 8.3 %all-to-all-start = ((bf16[8,72,772]{2,1,0:T(8,128)(2,1)}), bf16[8,72,772]{2,1,0:T(8,128)(2,1)S(1)}, u32[]{:S(2)}, u32[]{:S(2)}) async-start(bf16[8,72,772]{2,1,0:T(8,128)(2,1)} %broadcast_in_dim.14), calls=%async_computation | async-start | bytes 2064384 | tf_op jit(solution)/shard_map/all_to_all | solution.py:45
  28.5 16.9 %all-to-all-done = bf16[8,72,772]{2,1,0:T(8,128)(2,1)S(1)} async-done(((bf16[8,72,772]{2,1,0:T(8,128)(2,1)}), bf16[8,72,772]{2,1,0:T(8,128)(2,1)S(1)}, u32[]{:S(2)}, u32[]{:S(2)}) %all-to-all-start) | async-done | bytes 889376 | tf_op jit(solution)/shard_map/all_to_all | solution.py:45
  51.0 24.7 %all_to_all.35.own_ref = bf16[8,2,3,64,256]{4,3,2,1,0:T(8,128)(2,1)S(1)} all-to-all(bf16[8,2,3,64,256]{4,3,2,1,0:T(8,128)(2,1)S(1)} %broadcast_in_dim.17), channel_id=1, replica_groups={{0,16,32,48,64,80,96,112},{8,24,40,56,72,88,104,120},{1,17,33,49,65,81,..., dimensions={0} | all-to-all | bytes 3145728 | tf_op jit(solution)/shard_map/all_to_all | solution.py:41
  75.7 3.5 collective-permute-start.1
  79.3 17.0 %all-gather.3.cloned.1.call-done = bf16[576,2304]{1,0:T(8,128)(2,1)} async-done(((bf16[72,2304]{1,0:T(8,128)(2,1)}), bf16[576,2304]{1,0:T(8,128)(2,1)}) %all-gather.3.cloned.1.call-update) | async-done | bytes 2654224 | tf_op jit(solution)/shard_map/all_gather | solution.py:319
  96.3 2.8 slice.365
  103.5 15.5 %attention.2 = (f32[9,64,256]{2,1,0:T(8,128)S(1)}, f32[3,2,1,384]{3,2,1,0:T(1,128)S(1)}) custom-call(s32[39]{0:T(128)S(1)} %concatenate.122.sc, bf16[9,64,256]{2,1,0:T(8,128)(2,1)S(1)} %fusion.29.q_ref, bf16[8,2,3,64,256]{4,3,2,1,0:T(8,128)(2,1)S(1)} %all_to_all.35.own_ref, bf16[8,2,3,64,256]{4,3,2,1,0:T(8,128)(2,1)S(1)} %collective-permute-done.1.other_ref), custom_call_target="tpu_custom_call" | custom-call | tf_op jit(solution)/shard_map/attention/pallas_call | solution.py:225
  123.1 2.7 reshape.399
  132.8 32.6 %all-gather.5.cloned.1.call-done = bf16[576,3072]{1,0:T(8,128)(2,1)} async-done(((bf16[72,3072]{1,0:T(8,128)(2,1)}), bf16[576,3072]{1,0:T(8,128)(2,1)}) %all-gather.5.cloned.1.call-update) | async-done | bytes 3538960 | tf_op jit(solution)/shard_map/all_gather | solution.py:319
  167.8 2.3 fusion.84
  170.4 2.5 multiply_reduce_fusion.7
  177.4 24.7 %all_to_all.36.own_ref = bf16[8,2,3,64,256]{4,3,2,1,0:T(8,128)(2,1)S(1)} all-to-all(bf16[8,2,3,64,256]{4,3,2,1,0:T(8,128)(2,1)S(1)} %broadcast_in_dim.18), channel_id=1, replica_groups={{0,16,32,48,64,80,96,112},{8,24,40,56,72,88,104,120},{1,17,33,49,65,81,..., dimensions={0} | all-to-all | bytes 3145728 | tf_op jit(solution)/shard_map/all_to_all | solution.py:41
  204.5 3.4 reshape.401
  212.2 16.4 %attention.3 = (f32[9,64,256]{2,1,0:T(8,128)S(1)}, f32[3,2,1,384]{3,2,1,0:T(1,128)S(1)}) custom-call(s32[39]{0:T(128)S(1)} %concatenate.122.sc, bf16[9,64,256]{2,1,0:T(8,128)(2,1)S(1)} %fusion.26.q_ref, bf16[8,2,3,64,256]{4,3,2,1,0:T(8,128)(2,1)S(1)} %all_to_all.36.own_ref, bf16[8,2,3,64,256]{4,3,2,1,0:T(8,128)(2,1)} %collective-permute-done.5.other_ref), custom_call_target="tpu_custom_call" | custom-call | tf_op jit(solution)/shard_map/attention/pallas_call | solution.py:225
  238.0 3.0 multiply_reduce_fusion
  241.9 23.0 %attention_back.2 = (f32[9,64,256]{2,1,0:T(8,128)S(1)}, bf16[8,2,3,64,256]{4,3,2,1,0:T(8,128)(2,1)S(1)}, bf16[8,2,3,64,256]{4,3,2,1,0:T(8,128)(2,1)S(1)}) custom-call(s32[39]{0:T(128)S(1)} %concatenate.122.sc, bf16[9,64,256]{2,1,0:T(8,128)(2,1)S(1)} %fusion.26.q_ref, bf16[8,2,3,64,256]{4,3,2,1,0:T(8,128)(2,1)S(1)} %all_to_all.36.own_ref, ...), custom_call_target="tpu_custom_call" | custom-call | tf_op jit(solution)/shard_map/attention_back/pallas_call | solution.py:248
  270.5 4.4 all-to-all-start.3
  276.4 2.5 add_convert_fusion.4
  278.9 2.4 copy.63
  281.3 3.2 reshape.410
  284.6 2.3 add_convert_fusion
  288.6 10.0 %all-to-all-done.3 = bf16[8,2,3,64,256]{4,3,2,1,0:T(8,128)(2,1)} async-done(((bf16[8,2,3,64,256]{4,3,2,1,0:T(8,128)(2,1)}), bf16[8,2,3,64,256]{4,3,2,1,0:T(8,128)(2,1)}, u32[]{:S(2)}, u32[]{:S(2)}) %all-to-all-start.3) | async-done | bytes 1572896 | tf_op jit(solution)/shard_map/all_to_all | solution.py:41
  306.9 2.3 multiply_convert_fusion.1
  323.6 2.3 reshape.405
  325.8 2.4 add_convert_fusion.1
  332.5 22.7 %attention_back.3 = (f32[9,64,256]{2,1,0:T(8,128)S(1)}, bf16[8,2,3,64,256]{4,3,2,1,0:T(8,128)(2,1)S(1)}, bf16[8,2,3,64,256]{4,3,2,1,0:T(8,128)(2,1)}) custom-call(s32[39]{0:T(128)S(1)} %concatenate.122.sc, bf16[9,64,256]{2,1,0:T(8,128)(2,1)S(1)} %fusion.29.q_ref, bf16[8,2,3,64,256]{4,3,2,1,0:T(8,128)(2,1)S(1)} %all_to_all.35.own_ref, ...), custom_call_target="tpu_custom_call" | custom-call | tf_op jit(solution)/shard_map/attention_back/pallas_call | solution.py:248
  355.2 2.4 add_convert_fusion.5
  357.7 19.2 %all_to_all.37 = bf16[8,72,768]{2,1,0:T(8,128)(2,1)S(1)} all-to-all(bf16[8,72,768]{2,1,0:T(8,128)(2,1)S(1)} %bitcast.168), channel_id=1, replica_groups=mesh['ctx'=16,'fsdp'=8] {'fsdp'}, dimensions={0} | all-to-all | bytes 1769472 | tf_op jit(solution)/shard_map/all_to_all | solution.py:45
  377.1 3.6 collective-permute-done.18
  381.4 3.1 add_convert_fusion.2
  384.6 4.4 all-to-all-start.4
  390.7 2.9 collective-permute-start.20
  394.8 17.9 %collective-permute-done.20 = bf16[72,768]{1,0:T(8,128)(2,1)S(1)} collective-permute-done((bf16[72,768]{1,0:T(8,128)(2,1)S(1)}, bf16[72,768]{1,0:T(8,128)(2,1)S(1)}, u32[]{:S(2)}, u32[]{:S(2)}) %collective-permute-start.20) | collective-permute-done | bytes 110624 | tf_op jit(solution)/shard_map/ppermute | solution.py:63
  422.6 2.7 fusion.20
  428.4 3.6 all-to-all-start.5
  434.3 16.9 %all-to-all-done.5 = bf16[8,72,772]{2,1,0:T(8,128)(2,1)S(1)} async-done(((bf16[8,72,772]{2,1,0:T(8,128)(2,1)}), bf16[8,72,772]{2,1,0:T(8,128)(2,1)S(1)}, u32[]{:S(2)}, u32[]{:S(2)}) %all-to-all-start.5) | async-done | bytes 889376 | tf_op jit(solution)/shard_map/all_to_all | solution.py:45
  452.6 5.1 collective-permute-done.13
  458.3 3.8 collective-permute-done.14
  463.2 7.1 %collective-permute-done.15 = bf16[72,772]{1,0:T(8,128)(2,1)S(1)} collective-permute-done((bf16[72,772]{1,0:T(8,128)(2,1)S(1)}, bf16[72,772]{1,0:T(8,128)(2,1)S(1)}, u32[]{:S(2)}, u32[]{:S(2)}) %collective-permute-start.15) | collective-permute-done | bytes 111200 | tf_op jit(solution)/shard_map/ppermute | solution.py:63
  470.4 2.6 collective-permute-start.16
  472.9 23.1 %reduce-scatter.3.cloned.1.call-done = bf16[72,2304]{1,0:T(8,128)(2,1)} async-done(((bf16[576,2304]{1,0:T(8,128)(2,1)}), bf16[72,2304]{1,0:T(8,128)(2,1)}) %reduce-scatter.3.cloned.1.call-update) | async-done | bytes 331792 | tf_op jit(solution)/shard_map/reduce_scatter | solution.py:402
  496.5 2.3 collective-permute-start.31
  499.5 4.2 collective-permute-done.22
  506.1 5.2 collective-permute-done.23
  511.4 2.8 collective-permute-start.24
  514.9 5.8 %collective-permute-done.24 = bf16[72,2304]{1,0:T(8,128)(2,1)S(1)} collective-permute-done((bf16[72,2304]{1,0:T(8,128)(2,1)S(1)}, bf16[72,2304]{1,0:T(8,128)(2,1)S(1)}, u32[]{:S(2)}, u32[]{:S(2)}) %collective-permute-start.24) | collective-permute-done | bytes 331808 | tf_op jit(solution)/shard_map/ppermute | solution.py:63
  520.8 3.6 collective-permute-start.25
  (435 shorter events, 121.7 us)
Async XLA Ops:
  7.2 89.1 %all-gather.3.cloned.1.call-start = ((), (), s32[]{:S(2)}) async-start(), calls=%async_computation.9 | async-start | bytes 2985984 | tf_op jit(solution)/shard_map/all_gather | solution.py:319
  16.8 28.6 %all-to-all-start = ((bf16[8,72,772]{2,1,0:T(8,128)(2,1)}), bf16[8,72,772]{2,1,0:T(8,128)(2,1)S(1)}, u32[]{:S(2)}, u32[]{:S(2)}) async-start(bf16[8,72,772]{2,1,0:T(8,128)(2,1)} %broadcast_in_dim.14), calls=%async_computation | async-start | bytes 2064384 | tf_op jit(solution)/shard_map/all_to_all | solution.py:45
  25.1 140.3 %all-gather.5.cloned.1.call-start = ((), (), s32[]{:S(2)}) async-start(), calls=%async_computation.10 | async-start | bytes 3981312 | tf_op jit(solution)/shard_map/all_gather | solution.py:319
  45.4 3.0 collective-permute-start
  46.6 253.8 %copy-start.92 = (f32[32,256]{1,0:T(8,128)}, f32[32,256]{1,0:T(8,128)S(1)}, u32[]{:S(2)}) copy-start(f32[32,256]{1,0:T(8,128)S(1)} %get-tuple-element.90) | copy-start | bytes 98308
  75.7 27.7 %collective-permute-start.1 = (bf16[8,2,3,64,256]{4,3,2,1,0:T(8,128)(2,1)S(1)}, bf16[8,2,3,64,256]{4,3,2,1,0:T(8,128)(2,1)S(1)}, u32[]{:S(2)}, u32[]{:S(2)}) collective-permute-start(bf16[8,2,3,64,256]{4,3,2,1,0:T(8,128)(2,1)S(1)} %all_to_all.35.own_ref), channel_id=1, source_target_pairs={{0,8},{8,0},{16,24},{24,16},{32,40},{40,32},{48,56},{56,48},{64,72... | collective-permute-start | bytes 4718600 | tf_op jit(solution)/shard_map/ppermute | solution.py:37
  99.1 68.7 %collective-permute-start.2 = (bf16[576,1536]{1,0:T(8,128)(2,1)}, bf16[576,1536]{1,0:T(8,128)(2,1)}, u32[]{:S(2)}, u32[]{:S(2)}) collective-permute-start(bf16[576,1536]{1,0:T(8,128)(2,1)} %slice.365), channel_id=1, source_target_pairs={{0,8},{8,0},{16,24},{24,16},{32,40},{40,32},{48,56},{56,48},{64,72... | collective-permute-start | bytes 5308424 | tf_op jit(solution)/shard_map/ppermute | solution.py:37
  120.8 47.0 %copy-start.15 = (bf16[256,576]{0,1:T(8,128)(2,1)}, bf16[256,576]{0,1:T(8,128)(2,1)S(1)}, u32[]{:S(2)}) copy-start(bf16[256,576]{0,1:T(8,128)(2,1)S(1)} %multiply_convert_fusion.14) | copy-start | bytes 884740
  127.0 43.4 %collective-permute-start.3 = (bf16[768,576]{0,1:T(8,128)(2,1)}, bf16[768,576]{0,1:T(8,128)(2,1)}, u32[]{:S(2)}, u32[]{:S(2)}) collective-permute-start(bf16[768,576]{0,1:T(8,128)(2,1)} %copy.55), channel_id=1, source_target_pairs={{0,8},{8,0},{16,24},{24,16},{32,40},{40,32},{48,56},{56,48},{64,72... | collective-permute-start | bytes 2654216 | tf_op jit(solution)/shard_map/ppermute | solution.py:37
  166.6 6.3 %collective-permute-start.4 = (bf16[576,768]{1,0:T(8,128)(2,1)S(1)}, bf16[576,768]{1,0:T(8,128)(2,1)S(1)}, u32[]{:S(2)}, u32[]{:S(2)}) collective-permute-start(bf16[576,768]{1,0:T(8,128)(2,1)S(1)} %slice.374), channel_id=1, source_target_pairs={{0,8},{8,0},{16,24},{24,16},{32,40},{40,32},{48,56},{56,48},{64,72... | collective-permute-start | bytes 2654216 | tf_op jit(solution)/shard_map/ppermute | solution.py:37
  202.1 10.1 %collective-permute-start.5 = (bf16[8,2,3,64,256]{4,3,2,1,0:T(8,128)(2,1)S(1)}, bf16[8,2,3,64,256]{4,3,2,1,0:T(8,128)(2,1)}, u32[]{:S(2)}, u32[]{:S(2)}) collective-permute-start(bf16[8,2,3,64,256]{4,3,2,1,0:T(8,128)(2,1)S(1)} %all_to_all.36.own_ref), channel_id=1, source_target_pairs={{0,8},{8,0},{16,24},{24,16},{32,40},{40,32},{48,56},{56,48},{64,72... | collective-permute-start | bytes 4718600 | tf_op jit(solution)/shard_map/ppermute | solution.py:37
  204.5 30.2 %collective-permute-start.6 = (bf16[576,1536]{1,0:T(8,128)(2,1)}, bf16[576,1536]{1,0:T(8,128)(2,1)}, u32[]{:S(2)}, u32[]{:S(2)}) collective-permute-start(bf16[576,1536]{1,0:T(8,128)(2,1)} %slice.384), channel_id=1, source_target_pairs={{0,8},{8,0},{16,24},{24,16},{32,40},{40,32},{48,56},{56,48},{64,72... | collective-permute-start | bytes 5308424 | tf_op jit(solution)/shard_map/ppermute | solution.py:37
  210.2 26.8 %collective-permute-start.7 = (bf16[768,576]{0,1:T(8,128)(2,1)}, bf16[768,576]{0,1:T(8,128)(2,1)S(1)}, u32[]{:S(2)}, u32[]{:S(2)}) collective-permute-start(bf16[768,576]{0,1:T(8,128)(2,1)} %copy.56), channel_id=1, source_target_pairs={{0,8},{8,0},{16,24},{24,16},{32,40},{40,32},{48,56},{56,48},{64,72... | collective-permute-start | bytes 2654216 | tf_op jit(solution)/shard_map/ppermute | solution.py:37
  230.9 34.2 %copy-start.17 = (bf16[256,576]{0,1:T(8,128)(2,1)}, bf16[256,576]{0,1:T(8,128)(2,1)S(1)}, u32[]{:S(2)}) copy-start(bf16[256,576]{0,1:T(8,128)(2,1)S(1)} %multiply_convert_fusion.12) | copy-start | bytes 884740
  238.0 29.5 %copy-start.69 = (bf16[256,768]{1,0:T(8,128)(2,1)}, bf16[256,768]{1,0:T(8,128)(2,1)S(1)}, u32[]{:S(2)}) copy-start(bf16[256,768]{1,0:T(8,128)(2,1)S(1)} %get-tuple-element.64) | copy-start | bytes 1179652
  265.0 3.8 collective-permute-start.8
  266.9 17.7 %collective-permute-start.26 = (bf16[576,1536]{1,0:T(8,128)(2,1)}, bf16[576,1536]{1,0:T(8,128)(2,1)}, u32[]{:S(2)}, u32[]{:S(2)}) collective-permute-start(bf16[576,1536]{1,0:T(8,128)(2,1)} %convolution_convert_fusion), channel_id=1, source_target_pairs={{0,8},{8,0},{16,24},{24,16},{32,40},{40,32},{48,56},{56,48},{64,72... | collective-permute-start | bytes 5308424 | tf_op jit(solution)/shard_map/ppermute | solution.py:37
  268.7 7.7 %collective-permute-start.27 = (bf16[768,576]{0,1:T(8,128)(2,1)}, bf16[768,576]{0,1:T(8,128)(2,1)}, u32[]{:S(2)}, u32[]{:S(2)}) collective-permute-start(bf16[768,576]{0,1:T(8,128)(2,1)} %convolution_convert_fusion.6), channel_id=1, source_target_pairs={{0,8},{8,0},{16,24},{24,16},{32,40},{40,32},{48,56},{56,48},{64,72... | collective-permute-start | bytes 2654216 | tf_op jit(solution)/shard_map/ppermute | solution.py:37
  270.5 28.1 %all-to-all-start.3 = ((bf16[8,2,3,64,256]{4,3,2,1,0:T(8,128)(2,1)}), bf16[8,2,3,64,256]{4,3,2,1,0:T(8,128)(2,1)}, u32[]{:S(2)}, u32[]{:S(2)}) async-start(bf16[8,2,3,64,256]{4,3,2,1,0:T(8,128)(2,1)} %add_convert_fusion.3), calls=%async_computation.3 | async-start | bytes 3145728 | tf_op jit(solution)/shard_map/all_to_all | solution.py:41
  275.0 147.4 %reduce-scatter.5.cloned.1.call-start = ((), (), s32[]{:S(2)}) async-start(), calls=%async_computation.12 | async-start | bytes 2985984 | tf_op jit(solution)/shard_map/reduce_scatter | solution.py:402
  311.1 14.7 %collective-permute-start.9 = (bf16[576,1536]{1,0:T(8,128)(2,1)}, bf16[576,1536]{1,0:T(8,128)(2,1)}, u32[]{:S(2)}, u32[]{:S(2)}) collective-permute-start(bf16[576,1536]{1,0:T(8,128)(2,1)} %convolution_convert_fusion.2), channel_id=1, source_target_pairs={{0,8},{8,0},{16,24},{24,16},{32,40},{40,32},{48,56},{56,48},{64,72... | collective-permute-start | bytes 5308424 | tf_op jit(solution)/shard_map/ppermute | solution.py:37
  312.4 7.8 %collective-permute-start.10 = (bf16[768,576]{0,1:T(8,128)(2,1)S(1)}, bf16[768,576]{0,1:T(8,128)(2,1)S(1)}, u32[]{:S(2)}, u32[]{:S(2)}) collective-permute-start(bf16[768,576]{0,1:T(8,128)(2,1)S(1)} %convolution_convert_fusion.8), channel_id=1, source_target_pairs={{0,8},{8,0},{16,24},{24,16},{32,40},{40,32},{48,56},{56,48},{64,72... | collective-permute-start | bytes 2654216 | tf_op jit(solution)/shard_map/ppermute | solution.py:37
  313.9 41.3 %collective-permute-start.17 = (bf16[576,768]{1,0:T(8,128)(2,1)}, bf16[576,768]{1,0:T(8,128)(2,1)}, u32[]{:S(2)}, u32[]{:S(2)}) collective-permute-start(bf16[576,768]{1,0:T(8,128)(2,1)} %broadcast_select_fusion), channel_id=1, source_target_pairs={{0,8},{8,0},{16,24},{24,16},{32,40},{40,32},{48,56},{56,48},{64,72... | collective-permute-start | bytes 2654216 | tf_op jit(solution)/shard_map/ppermute | solution.py:37
  355.2 26.2 %collective-permute-start.11 = (bf16[8,2,3,64,256]{4,3,2,1,0:T(8,128)(2,1)}, bf16[8,2,3,64,256]{4,3,2,1,0:T(8,128)(2,1)}, u32[]{:S(2)}, u32[]{:S(2)}) collective-permute-start(bf16[8,2,3,64,256]{4,3,2,1,0:T(8,128)(2,1)} %get-tuple-element.33), channel_id=1, source_target_pairs={{0,8},{8,0},{16,24},{24,16},{32,40},{40,32},{48,56},{56,48},{64,72... | collective-permute-start | bytes 4718600 | tf_op jit(solution)/shard_map/ppermute | solution.py:37
  377.1 3.7 collective-permute-start.18
  381.4 8.2 %collective-permute-start.19 = (bf16[72,768]{1,0:T(8,128)(2,1)}, bf16[72,768]{1,0:T(8,128)(2,1)}, u32[]{:S(2)}, u32[]{:S(2)}) collective-permute-start(bf16[72,768]{1,0:T(8,128)(2,1)} %add_convert_fusion.21), channel_id=1, source_target_pairs={{0,32},{8,40},{16,48},{24,56},{32,0},{40,8},{48,16},{56,24},{64,96... | collective-permute-start | bytes 331784 | tf_op jit(solution)/shard_map/ppermute | solution.py:63
  384.6 32.0 %all-to-all-start.4 = ((bf16[8,2,3,64,256]{4,3,2,1,0:T(8,128)(2,1)}), bf16[8,2,3,64,256]{4,3,2,1,0:T(8,128)(2,1)}, u32[]{:S(2)}, u32[]{:S(2)}) async-start(bf16[8,2,3,64,256]{4,3,2,1,0:T(8,128)(2,1)} %add_convert_fusion.2), calls=%async_computation.4 | async-start | bytes 3145728 | tf_op jit(solution)/shard_map/all_to_all | solution.py:41
  389.0 107.0 %reduce-scatter.3.cloned.1.call-start = ((), (), s32[]{:S(2)}) async-start(), calls=%async_computation.11 | async-start | bytes 2985984 | tf_op jit(solution)/shard_map/reduce_scatter | solution.py:402
  389.6 25.4 %copy-start.20 = (f32[256,576]{0,1:T(8,128)S(1)}, f32[256,576]{0,1:T(8,128)}, u32[]{:S(2)}) copy-start(f32[256,576]{0,1:T(8,128)} %copy-done.19) | copy-start | bytes 1769476
  389.6 25.4 %copy-start.74 = (bf16[9,64,256]{2,1,0:T(8,128)(2,1)S(1)}, bf16[9,64,256]{2,1,0:T(8,128)(2,1)}, u32[]{:S(2)}) copy-start(bf16[9,64,256]{2,1,0:T(8,128)(2,1)} %copy-done.73) | copy-start | bytes 884740
  390.7 22.1 %collective-permute-start.20 = (bf16[72,768]{1,0:T(8,128)(2,1)S(1)}, bf16[72,768]{1,0:T(8,128)(2,1)S(1)}, u32[]{:S(2)}, u32[]{:S(2)}) collective-permute-start(bf16[72,768]{1,0:T(8,128)(2,1)S(1)} %add_convert_fusion.20), channel_id=1, source_target_pairs={{0,64},{8,72},{16,80},{24,88},{32,96},{40,104},{48,112},{56,120},{... | collective-permute-start | bytes 331784 | tf_op jit(solution)/shard_map/ppermute | solution.py:63
  412.8 3.2 collective-permute-start.21
  421.3 4.2 collective-permute-start.12
  422.4 9.7 %collective-permute-start.28 = (bf16[72,2304]{1,0:T(8,128)(2,1)}, bf16[72,2304]{1,0:T(8,128)(2,1)}, u32[]{:S(2)}, u32[]{:S(2)}) collective-permute-start(bf16[72,2304]{1,0:T(8,128)(2,1)} %reduce-scatter.5.cloned.1.call-done), channel_id=1, source_target_pairs={{0,16},{8,24},{16,0},{24,8},{32,48},{40,56},{48,32},{56,40},{64,80... | collective-permute-start | bytes 995336 | tf_op jit(solution)/shard_map/ppermute | solution.py:63
  428.4 22.8 %all-to-all-start.5 = ((bf16[8,72,772]{2,1,0:T(8,128)(2,1)}), bf16[8,72,772]{2,1,0:T(8,128)(2,1)S(1)}, u32[]{:S(2)}, u32[]{:S(2)}) async-start(bf16[8,72,772]{2,1,0:T(8,128)(2,1)} %bitcast.38), calls=%async_computation.5 | async-start | bytes 2064384 | tf_op jit(solution)/shard_map/all_to_all | solution.py:45
  432.1 30.1 %copy-start.62 = (bf16[1,256,576]{1,2,0:T(8,128)(2,1)S(1)}, bf16[1,256,576]{1,2,0:T(8,128)(2,1)}, u32[]{:S(2)}) copy-start(bf16[1,256,576]{1,2,0:T(8,128)(2,1)} %param.9) | copy-start | bytes 884740
  432.1 30.1 %copy-start.84 = (f32[256,576]{0,1:T(8,128)S(1)}, f32[256,576]{0,1:T(8,128)}, u32[]{:S(2)}) copy-start(f32[256,576]{0,1:T(8,128)} %get-tuple-element.100) | copy-start | bytes 1769476
  433.3 24.5 %collective-permute-start.29 = (bf16[72,2304]{1,0:T(8,128)(2,1)S(1)}, bf16[72,2304]{1,0:T(8,128)(2,1)S(1)}, u32[]{:S(2)}, u32[]{:S(2)}) collective-permute-start(bf16[72,2304]{1,0:T(8,128)(2,1)S(1)} %add_convert_fusion.10), channel_id=1, source_target_pairs={{0,32},{8,40},{16,48},{24,56},{32,0},{40,8},{48,16},{56,24},{64,96... | collective-permute-start | bytes 995336 | tf_op jit(solution)/shard_map/ppermute | solution.py:63
  451.3 6.4 %collective-permute-start.13 = (bf16[72,772]{1,0:T(8,128)(2,1)S(1)}, bf16[72,772]{1,0:T(8,128)(2,1)S(1)}, u32[]{:S(2)}, u32[]{:S(2)}) collective-permute-start(bf16[72,772]{1,0:T(8,128)(2,1)S(1)} %reduce_sum.174), channel_id=1, source_target_pairs={{0,16},{8,24},{16,0},{24,8},{32,48},{40,56},{48,32},{56,40},{64,80... | collective-permute-start | bytes 333512 | tf_op jit(solution)/shard_map/ppermute | solution.py:63
  457.7 4.3 collective-permute-start.14
  457.9 38.5 %collective-permute-start.30 = (bf16[72,2304]{1,0:T(8,128)(2,1)S(1)}, bf16[72,2304]{1,0:T(8,128)(2,1)S(1)}, u32[]{:S(2)}, u32[]{:S(2)}) collective-permute-start(bf16[72,2304]{1,0:T(8,128)(2,1)S(1)} %add_convert_fusion.9), channel_id=1, source_target_pairs={{0,64},{8,72},{16,80},{24,88},{32,96},{40,104},{48,112},{56,120},{... | collective-permute-start | bytes 995336 | tf_op jit(solution)/shard_map/ppermute | solution.py:63
  462.1 8.2 %collective-permute-start.15 = (bf16[72,772]{1,0:T(8,128)(2,1)S(1)}, bf16[72,772]{1,0:T(8,128)(2,1)S(1)}, u32[]{:S(2)}, u32[]{:S(2)}) collective-permute-start(bf16[72,772]{1,0:T(8,128)(2,1)S(1)} %add_convert_fusion.17), channel_id=1, source_target_pairs={{0,64},{8,72},{16,80},{24,88},{32,96},{40,104},{48,112},{56,120},{... | collective-permute-start | bytes 333512 | tf_op jit(solution)/shard_map/ppermute | solution.py:63
  470.4 28.5 %collective-permute-start.16 = (bf16[72,772]{1,0:T(8,128)(2,1)S(1)}, bf16[72,772]{1,0:T(8,128)(2,1)S(1)}, u32[]{:S(2)}, u32[]{:S(2)}) collective-permute-start(bf16[72,772]{1,0:T(8,128)(2,1)S(1)} %add_convert_fusion.16), channel_id=1, source_target_pairs={{0,8},{8,0},{16,24},{24,16},{32,40},{40,32},{48,56},{56,48},{64,72... | collective-permute-start | bytes 333512 | tf_op jit(solution)/shard_map/ppermute | solution.py:37
  496.1 7.6 %collective-permute-start.22 = (bf16[72,2304]{1,0:T(8,128)(2,1)}, bf16[72,2304]{1,0:T(8,128)(2,1)S(1)}, u32[]{:S(2)}, u32[]{:S(2)}) collective-permute-start(bf16[72,2304]{1,0:T(8,128)(2,1)} %reduce-scatter.3.cloned.1.call-done), channel_id=1, source_target_pairs={{0,16},{8,24},{16,0},{24,8},{32,48},{40,56},{48,32},{56,40},{64,80... | collective-permute-start | bytes 995336 | tf_op jit(solution)/shard_map/ppermute | solution.py:63
  496.5 28.8 %collective-permute-start.31 = (bf16[72,2304]{1,0:T(8,128)(2,1)S(1)}, bf16[72,2304]{1,0:T(8,128)(2,1)S(1)}, u32[]{:S(2)}, u32[]{:S(2)}) collective-permute-start(bf16[72,2304]{1,0:T(8,128)(2,1)S(1)} %add_convert_fusion.8), channel_id=1, source_target_pairs={{0,8},{8,0},{16,24},{24,16},{32,40},{40,32},{48,56},{56,48},{64,72... | collective-permute-start | bytes 995336 | tf_op jit(solution)/shard_map/ppermute | solution.py:37
  504.8 6.5 %collective-permute-start.23 = (bf16[72,2304]{1,0:T(8,128)(2,1)S(1)}, bf16[72,2304]{1,0:T(8,128)(2,1)S(1)}, u32[]{:S(2)}, u32[]{:S(2)}) collective-permute-start(bf16[72,2304]{1,0:T(8,128)(2,1)S(1)} %add_convert_fusion.13), channel_id=1, source_target_pairs={{0,32},{8,40},{16,48},{24,56},{32,0},{40,8},{48,16},{56,24},{64,96... | collective-permute-start | bytes 995336 | tf_op jit(solution)/shard_map/ppermute | solution.py:63
  511.4 9.3 %collective-permute-start.24 = (bf16[72,2304]{1,0:T(8,128)(2,1)S(1)}, bf16[72,2304]{1,0:T(8,128)(2,1)S(1)}, u32[]{:S(2)}, u32[]{:S(2)}) collective-permute-start(bf16[72,2304]{1,0:T(8,128)(2,1)S(1)} %add_convert_fusion.12), channel_id=1, source_target_pairs={{0,64},{8,72},{16,80},{24,88},{32,96},{40,104},{48,112},{56,120},{... | collective-permute-start | bytes 995336 | tf_op jit(solution)/shard_map/ppermute | solution.py:63
  520.8 4.9 collective-permute-start.25
  (93 other events, 427.5 us)
Sparse Core Ops, SparseCore 0:
  15.9 80.3 all-gather.2
  98.6 66.7 all-gather.4
  288.7 74.1 reduce-scatter.4
  415.6 80.4 reduce-scatter.2

commit v4 on v3

--- a/solution.py
+++ b/solution.py
@@ -268,6 +268,130 @@
     )(scalars, q_t, own, other, o_t, do_t, lse)
 
 
+ANY_SPEC = pl.BlockSpec(memory_space=pl.ANY)
+
+
+def arrange_kernel(me, *refs):
+    pieces, outs, sems = refs[:FSDP], refs[FSDP:-1], refs[-1]
+    copies, at = [], 0
+    for k, out in enumerate(outs):
+        width = out.shape[2]
+        for d, piece in enumerate(pieces):
+            copies.append(
+                pltpu.make_async_copy(
+                    piece.at[:, pl.ds(at, width)], out.at[jnp.bitwise_xor(me[0], d)], sems.at[k, d]
+                )
+            )
+        at += width
+    for copy in copies:
+        copy.start()
+    for copy in copies:
+        copy.wait()
+
+
+def arrange(me, pieces, widths):
+    rows = pieces[0].shape[0]
+    return pl.pallas_call(
+        arrange_kernel,
+        grid_spec=pltpu.PrefetchScalarGridSpec(
+            num_scalar_prefetch=1,
+            grid=(),
+            in_specs=[ANY_SPEC] * FSDP,
+            out_specs=[ANY_SPEC] * len(widths),
+            scratch_shapes=[pltpu.SemaphoreType.DMA((len(widths), FSDP))],
+        ),
+        out_shape=[jax.ShapeDtypeStruct((FSDP, rows, w), BF16) for w in widths],
+        name="arrange",
+    )(me, *pieces)
+
+
+def dispatch_kernel(me, x_ref, *refs):
+    outs, sems = refs[:FSDP], refs[FSDP]
+    copies = [
+        pltpu.make_async_copy(x_ref.at[jnp.bitwise_xor(me[0], d)], outs[d], sems.at[d])
+        for d in range(FSDP)
+    ]
+    for copy in copies:
+        copy.start()
+    for copy in copies:
+        copy.wait()
+
+
+def dispatch(me, x):
+    return pl.pallas_call(
+        dispatch_kernel,
+        grid_spec=pltpu.PrefetchScalarGridSpec(
+            num_scalar_prefetch=1,
+            grid=(),
+            in_specs=[ANY_SPEC],
+            out_specs=[ANY_SPEC] * FSDP,
+            scratch_shapes=[pltpu.SemaphoreType.DMA((FSDP,))],
+        ),
+        out_shape=[jax.ShapeDtypeStruct(x.shape[1:], BF16)] * FSDP,
+        name="dispatch",
+    )(me, x)
+
+
+def across(x, d):
+    return lax.ppermute(x, "fsdp", [(i, i ^ d) for i in range(FSDP)]) if d else x
+
+
+UNITS = FF // FSDP // 2
+
+
+def unpack_kernel(sc, *refs):
+    mlp0, mlp0_p, qkv0, qkv0_p, all1, all1_p, qkv_ref, out_ref, gu_ref = refs
+
+    def layer_out(layer, halves, qkv_halves, qkv_at, wout_at):
+        for half in range(2):
+            mlp = halves[half]
+            for k in range(2):
+                for i in range(FSDP):
+                    src = k * HALF + i * UNITS
+                    dst = k * FF + i * 2 * UNITS + half * UNITS
+                    gu_ref[layer, :, dst : dst + UNITS] = mlp[:, src : src + UNITS].astype(F32)
+            cut = (Q_ROWS + KV_ROWS) // 2
+            qkv_ref[layer, :, half * cut : (half + 1) * cut] = (
+                qkv_halves[half][:, qkv_at : qkv_at + cut].astype(F32)
+            )
+            cut = D // 2
+            out_ref[layer, :, half * cut : (half + 1) * cut] = (
+                mlp[:, wout_at : wout_at + cut].astype(F32)
+            )
+
+    def both(order):
+        m0, q0, a1 = [mlp0, mlp0_p][::order], [qkv0, qkv0_p][::order], [all1, all1_p][::order]
+        layer_out(0, m0, q0, 0, FF + HALF)
+        layer_out(1, a1, a1, FF + HALF + D // 2, FF + HALF)
+
+    @pl.when(sc[0] == 0)
+    def _():
+        both(1)
+
+    @pl.when(sc[0] != 0)
+    def _():
+        both(-1)
+
+
+def unpack(core, mlp0, mlp0_p, qkv0, qkv0_p, all1, all1_p):
+    return pl.pallas_call(
+        unpack_kernel,
+        grid_spec=pltpu.PrefetchScalarGridSpec(
+            num_scalar_prefetch=1,
+            grid=(),
+            in_specs=[pl.BlockSpec(memory_space=pltpu.VMEM)] * 6,
+            out_specs=[pl.BlockSpec(memory_space=pltpu.VMEM)] * 3,
+        ),
+        out_shape=[
+            jax.ShapeDtypeStruct((LAYERS, SHARD, Q_ROWS + KV_ROWS), F32),
+            jax.ShapeDtypeStruct((LAYERS, SHARD, D), F32),
+            jax.ShapeDtypeStruct((LAYERS, SHARD, 2 * FF), F32),
+        ],
+        compiler_params=pltpu.CompilerParams(vmem_limit_bytes=40 * 2**20),
+        name="unpack",
+    )(core, mlp0, mlp0_p, qkv0, qkv0_p, all1, all1_p)
+
+
 def rotate(x, cosine, sine):
     half = HEAD_DIM // 2
     first, second = x[:, :half], x[:, half:]
@@ -295,6 +419,7 @@
     place = lax.axis_index("ctx")
     core = jnp.bitwise_and(place, 1)
     first_core = core == 0
+    me = lax.axis_index("fsdp").reshape(1)
 
     def my_half(left, right):
         return jnp.where(first_core, left, right)
@@ -311,20 +436,19 @@
     proj_cut = jnp.concatenate([w_qkv, w_out], 2)
     proj_cut = my_half(proj_cut[..., :cut], proj_cut[..., cut:])
     first = jnp.concatenate([proj_cut[0], gain_cols], 1)
-    packs = [
-        jnp.concatenate([wgu_cut[0], wd_cut[0]], 1),
-        jnp.concatenate([wgu_cut[1], wd_cut[1], proj_cut[1]], 1),
-    ]
-    packs[0], first = lax.optimization_barrier((packs[0], first))
-    packs = [lax.all_gather(p, "fsdp", axis=0, tiled=True) for p in packs]
+    packs = [jnp.concatenate([wgu_cut[l], wd_cut[l]], 1) for l in range(LAYERS)]
     first = gather_fsdp(first)
+    pieces = [across(packs[0], d) for d in range(FSDP)]
+    pack1 = lax.all_gather(packs[1], "fsdp", axis=0, tiled=True)
     gains = jnp.transpose(first[:, cut:].astype(F32)).reshape(LAYERS, 2, D)
-    projs = [first[:, :cut], packs[1][:, FF + HALF :]]
-    projs = [jnp.concatenate(in_order(own, to_partner(own)), 1) for own in projs]
-    mlps = []
-    for pack in packs:
-        wgu, wdown = pack[:, :FF], pack[:, FF : FF + HALF].reshape(HALF, D)
-        mlps.append([(wgu, wdown), (to_partner(wgu), to_partner(wdown))])
+
+    def whole_proj(own):
+        return jnp.concatenate(in_order(own, to_partner(own)), 1)
+
+    def both_halves(wgu, wdown):
+        return [(wgu, wdown), (to_partner(wgu), to_partner(wdown))]
+
+    projs, mlps = [whole_proj(first[:, :cut])], []
 
     first_block = lax.dynamic_index_in_dim(block_order, 2 * place, 0, keepdims=False)
     low = jnp.minimum(first_block, NBLK - 1 - first_block)
@@ -351,8 +475,17 @@
         kv_t = jnp.concatenate([turned[HEADS:], qkv_t[HEADS + KV_HEADS :]], 0).astype(BF16)
         kv_t = kv_t.reshape(1, 2, KV_HEADS, HEAD_DIM, ROWS)
         kv_own = over_chips(jnp.broadcast_to(kv_t, (CTX // 2,) + kv_t.shape[1:]))
+        if layer == 0:
+            kv_own, pieces, late = lax.optimization_barrier((kv_own, pieces, proj_cut[1]))
+            wgu, wdown = arrange(me, pieces, (FF, HALF))
+            mlps.append(both_halves(wgu.reshape(D, FF), wdown.reshape(HALF, D)))
+            late = gather_fsdp(late)
+        else:
+            mlps.append(both_halves(pack1[:, :FF], pack1[:, FF:].reshape(HALF, D)))
         kv_other = to_partner(kv_own)
         o_t, lse = attention(scalars, q_t, kv_own, kv_other)
+        if layer == 0:
+            projs.append(whole_proj(late))
         attn_out = o_t.astype(BF16).reshape(Q_ROWS, ROWS)
         mid = hidden + ein("at,ad->td", attn_out, wout)
         unit_m, rms_m = normed(mid)
@@ -371,7 +504,7 @@
     output = hidden.astype(BF16).reshape(1, ROWS, D)
 
     d_hidden = cotangent[0].astype(F32)
-    shares = [None] * LAYERS
+    shares = []
     gain_grads = [None] * LAYERS
     for layer in reversed(range(LAYERS)):
         (wqkv, wout, unit_a, rms_a, attn_in, q_t, kv_own, kv_other, o_t, lse, attn_out,
@@ -389,17 +522,27 @@
             d_norm = d_norm + ein("tf,df->td", d_gu, wgu)
             wd_parts.append(ein("tf,td->fd", inner, grad_b).astype(BF16))
             wgu_parts.append(ein("td,tf->df", mlp_in, d_gu).astype(BF16))
-        d_wgu = sum_pair(wgu_parts[0], to_partner(wgu_parts[1]))
-        d_wdown = sum_pair(wd_parts[0], to_partner(wd_parts[1])).reshape(D, HALF)
-        d_mlp = jnp.concatenate([d_wgu, d_wdown], 1)
         d_gain_m = jnp.sum(d_norm * unit_m, 0)
         d_hidden = d_hidden + norm_back(d_norm * gains[layer, 1], unit_m, rms_m)
         grad_b = d_hidden.astype(BF16)
         d_wout = mm(attn_out, grad_b)
         do_t = ein("ad,td->at", wout, grad_b).astype(BF16).reshape(HEADS, HEAD_DIM, ROWS)
         if layer == 0:
-            do_t, d_mlp = lax.optimization_barrier((do_t, d_mlp))
-        mlp_share = lax.psum_scatter(d_mlp, "fsdp", scatter_dimension=0, tiled=True)
+            do_t, wgu_parts, wd_parts = lax.optimization_barrier((do_t, wgu_parts, wd_parts))
+        wout_half = D // 2
+        d_wout = d_wout.astype(BF16)
+        wout_mine = my_half(d_wout[:, :wout_half], d_wout[:, wout_half:])
+        wout_theirs = my_half(d_wout[:, wout_half:], d_wout[:, :wout_half])
+        d_mlp = [
+            sum_pair(wgu_parts[0], to_partner(wgu_parts[1])),
+            sum_pair(wd_parts[0], to_partner(wd_parts[1])).reshape(D, HALF),
+            sum_pair(wout_mine, to_partner(wout_theirs)),
+        ]
+        if layer == 0:
+            d_mlp = jnp.concatenate(d_mlp, 1).reshape(FSDP, SHARD, -1)
+            parts = [across(p, d) for d, p in enumerate(dispatch(me, d_mlp))]
+            share = sum_chips(sum(p.astype(F32) for p in parts).astype(BF16))
+            shares += [share, to_partner(share)]
         dq_t, dkv_own, dkv_other = attention_back(scalars, q_t, kv_own, kv_other, o_t, do_t, lse)
         dkv = (dkv_own.astype(F32) + to_partner(dkv_other).astype(F32)).astype(BF16)
         dkv = jnp.sum(over_chips(dkv).astype(F32), 0)
@@ -411,32 +554,31 @@
         d_gain_a = jnp.sum(d_norm * unit_a, 0)
         d_hidden = d_hidden + norm_back(d_norm * gains[layer, 0], unit_a, rms_a)
         gain_grads[layer] = jnp.stack([d_gain_a, d_gain_m])
-        d_proj = jnp.concatenate([d_wqkv, d_wout], 1).astype(BF16)
-        mine, theirs = my_half(d_proj[:, :cut], d_proj[:, cut:]), my_half(d_proj[:, cut:], d_proj[:, :cut])
-        d_proj = sum_pair(mine, to_partner(theirs))
+        d_wqkv = d_wqkv.astype(BF16)
+        half = (Q_ROWS + KV_ROWS) // 2
+        mine = my_half(d_wqkv[:, :half], d_wqkv[:, half:])
+        theirs = my_half(d_wqkv[:, half:], d_wqkv[:, :half])
+        d_wqkv = sum_pair(mine, to_partner(theirs))
         if layer == 0:
             d_gains = jnp.transpose(jnp.stack(gain_grads).reshape(2 * LAYERS, D)).astype(BF16)
-            d_proj = jnp.concatenate([d_proj, d_gains], 1)
-        shares[layer] = sum_chips(mlp_share), sum_chips(scatter_fsdp(d_proj))
+            share = sum_chips(scatter_fsdp(jnp.concatenate([d_wqkv, d_gains], 1)))
+        else:
+            share = jnp.concatenate(d_mlp + [d_wqkv], 1)
+            share = sum_chips(lax.psum_scatter(share, "fsdp", scatter_dimension=0, tiled=True))
+        shares += [share, to_partner(share)]
     input_grad = d_hidden.reshape(1, ROWS, D)
 
-    proj_grads, gate_up_grad, down_grad = [], [], []
-    for layer in range(LAYERS):
-        mlp_share, proj_share = shares[layer]
-        pair = in_order(mlp_share, to_partner(mlp_share))
-        cols = jnp.stack([half[:, :FF].reshape(SHARD, 2, FSDP, -1) for half in pair], 3)
-        gate_up_grad.append(cols.reshape(SHARD, 2 * FF).astype(F32))
-        rows = [half[:, FF:].reshape(FF // FSDP // 2, D) for half in pair]
-        down_grad.append(jnp.concatenate(rows, 0).astype(F32))
-        theirs = to_partner(proj_share)
-        if layer == 0:
-            d_gain = proj_share[:, cut:].astype(F32) + theirs[:, cut:].astype(F32)
-            gain_grad = jnp.transpose(d_gain).reshape(LAYERS, 2, SHARD)
-        pair = in_order(proj_share[:, :cut], theirs[:, :cut])
-        proj_grads.append(jnp.concatenate(pair, 1).astype(F32))
-    qkv_grad = jnp.stack([g[:, : Q_ROWS + KV_ROWS] for g in proj_grads])
-    out_proj_grad = jnp.stack([g[:, Q_ROWS + KV_ROWS :] for g in proj_grads])
-    gate_up_grad, down_grad = jnp.stack(gate_up_grad), jnp.stack(down_grad)
+    all1, all1_p, mlp0, mlp0_p, qkv0, qkv0_p = shares
+    d_gain = qkv0[:, half:].astype(F32) + qkv0_p[:, half:].astype(F32)
+    gain_grad = jnp.transpose(d_gain).reshape(LAYERS, 2, SHARD)
+    qkv_grad, out_proj_grad, gate_up_grad = unpack(
+        core.reshape(1), mlp0, mlp0_p, qkv0, qkv0_p, all1, all1_p
+    )
+    down_grad = []
+    for own, theirs in ((mlp0, mlp0_p), (all1, all1_p)):
+        rows = [x[:, FF : FF + HALF].reshape(UNITS, D) for x in in_order(own, theirs)]
+        down_grad.append(jnp.concatenate(rows, 0))
+    down_grad = jnp.stack(down_grad).astype(F32)
     return (output, input_grad, gain_grad, qkv_grad, out_proj_grad, gate_up_grad, down_grad)
 
 

time: 550 us -> 682 us (1.24)
  Pallas kernels: 77.5 us -> 256 us
  waiting for transfers between devices: 172 us -> 128 us
  blocking collectives: 68.6 us -> 24.6 us
  starting transfers between devices: 53.3 us -> 94 us
    pallas_call x0 -> x3, Pallas kernels: none -> 179 us  [the longest x1 95 us: dispatch(): pl.pallas_call(dispatch_kernel, grid_spec=pltpu.PrefetchScalarGridSpec(nu...]
    ppermute x0 -> x14, waiting for transfers between devices: none -> 66.7 us  [across(): lax.ppermute(x, 'fsdp', [(i, i ^ d) for i in range(FSDP)])]
    all_gather x2 -> x1, waiting for transfers between devices: 49.6 us -> 0.01 us  [local(): pack1 = lax.all_gather(packs[1], 'fsdp', axis=0, tiled=True)]
    ppermute x0 -> x14, starting transfers between devices: none -> 28.2 us  [across(): lax.ppermute(x, 'fsdp', [(i, i ^ d) for i in range(FSDP)])]
    ppermute x12 -> x9, waiting for transfers between devices: 52.8 us -> 25.4 us  [sum_chips(): x = sum_pair(x, lax.ppermute(x, 'ctx', [(i, i ^ bit) for i in range(CTX)]))]
    all_to_all x2 -> x1, blocking collectives: 49.4 us -> 24.6 us  [over_chips(): lax.all_to_all(x, 'ctx', 0, 0, axis_index_groups=SAME_CORE, tiled=True)]
    reduce_scatter x2 -> x1, waiting for transfers between devices: 23.1 us -> 0.01 us  [local(): lax.psum_scatter(share, 'fsdp', scatter_dimension=0, tiled=True)]
    all_to_all x1 -> x0, blocking collectives: 19.2 us -> none  [over_fsdp(): return lax.all_to_all(x, 'fsdp', 0, 0, tiled=True)]
  transfers between devices with their start and end apart: 40 -> 52, of which waited for: 18 -> 18; matrix products, arithmetic and copies ran while one was open for 20% -> 18% of each run, Pallas kernels for 10% -> 34%
where the time goes in v4:
time: 682 us; the launch traced here: 671 us
  Pallas kernels  256 us (38%)
  waiting for transfers between devices  128 us (19%)
  starting transfers between devices  94 us (14%)
  local copies, waits for them, and re-layouts  66.5 us (10%)
  matrix products  44.9 us (7%)
  other arithmetic  38.8 us (6%)
  blocking collectives  24.6 us (4%)
  between operations  18.7 us (3%)
    pallas_call x1, Pallas kernels, dispatch(): pl.pallas_call(dispatch_kernel, grid_spec=pltpu.PrefetchScalarGridSpec(nu...  95 us
    pallas_call x1, Pallas kernels, arrange(): pl.pallas_call(arrange_kernel, grid_spec=pltpu.PrefetchScalarGridSpec(num...  81.7 us
    ppermute x14, waiting for transfers between devices, across(): lax.ppermute(x, 'fsdp', [(i, i ^ d) for i in range(FSDP)])  66.7 us
    pallas_call x2, Pallas kernels, attention_back(): pl.pallas_call(backward_kernel, grid_spec=pltpu.PrefetchScalarGridSpec(nu...  45.5 us
    dot_general x26, matrix products, ein(): return jnp.einsum(spec, a, b, preferred_element_type=F32)  33.2 us
    pallas_call x2, Pallas kernels, attention(): pl.pallas_call(forward_kernel, grid_spec=pltpu.PrefetchScalarGridSpec(num...  32 us
    ppermute x14, starting transfers between devices, across(): lax.ppermute(x, 'fsdp', [(i, i ^ d) for i in range(FSDP)])  28.2 us
    ppermute x9, waiting for transfers between devices, sum_chips(): x = sum_pair(x, lax.ppermute(x, 'ctx', [(i, i ^ bit) for i in range(CTX)]))  25.4 us
  transfers between devices with their start and end apart: 52, of which 18 were waited for; matrix products, arithmetic and copies ran while one was open for 18% of the time, Pallas kernels for 34%

profile of v4, /device:TPU:1, one launch (start us, length us, event | category | flops | bytes accessed | tf_op | source)
XLA Modules:
  0.0 671.5 jit_solution(17096433876697447080)
XLA Ops:
  10.9 8.2 %all-to-all-start = ((bf16[8,72,772]{2,1,0:T(8,128)(2,1)}), bf16[8,72,772]{2,1,0:T(8,128)(2,1)S(1)}, u32[]{:S(2)}, u32[]{:S(2)}) async-start(bf16[8,72,772]{2,1,0:T(8,128)(2,1)} %broadcast_in_dim.16), calls=%async_computation | async-start | bytes 2064384 | tf_op jit(solution)/shard_map/all_to_all | solution.py:45
  20.2 2.6 fusion.78
  27.4 8.8 %all-to-all-done = bf16[8,72,772]{2,1,0:T(8,128)(2,1)S(1)} async-done(((bf16[8,72,772]{2,1,0:T(8,128)(2,1)}), bf16[8,72,772]{2,1,0:T(8,128)(2,1)S(1)}, u32[]{:S(2)}, u32[]{:S(2)}) %all-to-all-start) | async-done | bytes 889376 | tf_op jit(solution)/shard_map/all_to_all | solution.py:45
  44.3 4.8 all-to-all-start.1
  51.6 2.4 collective-permute-start.3
  56.0 2.8 collective-permute-done.1.refs_1_
  60.6 5.3 collective-permute-done.2.refs_2_
  66.0 3.0 collective-permute-start.7
  69.0 26.9 %collective-permute-done.4.refs_4_ = bf16[72,2304]{1,0:T(8,128)(2,1)S(1)} collective-permute-done((bf16[72,2304]{1,0:T(8,128)(2,1)S(1)}, bf16[72,2304]{1,0:T(8,128)(2,1)S(1)}, u32[]{:S(2)}, u32[]{:S(2)}) %collective-permute-start.4) | collective-permute-done | bytes 331808 | tf_op jit(solution)/shard_map/ppermute | solution.py:336
  100.6 4.4 all-to-all-start.2
  112.8 81.7 %arrange.1 = (bf16[8,72,1536]{2,1,0:T(8,128)(2,1)}, bf16[8,72,768]{2,1,0:T(8,128)(2,1)}) custom-call(s32[1]{0:T(128)} %bitcast.17.me, bf16[72,2304]{1,0:T(8,128)(2,1)} %copy-done.69, bf16[72,2304]{1,0:T(8,128)(2,1)} %copy-done.89, bf16[72,2304]{1,0:T(8,128)(2,1)} %copy-done.90, bf16[72,2304]{1,0:T(8,128)(2,1)} %copy-done.91, bf16[72,2304]{1,0:T(8,128)(2,1)} %copy-done.92, ...), custom_call_target="tpu_custom_call" | custom-call | tf_op jit(solution)/shard_map/arrange/pallas_call | solution.py:294
  194.6 3.4 reshape.332
  201.3 15.5 %attention.2 = (f32[9,64,256]{2,1,0:T(8,128)S(1)}, f32[3,2,1,384]{3,2,1,0:T(1,128)S(1)}) custom-call(s32[39]{0:T(128)S(1)} %concatenate.93.sc, bf16[9,64,256]{2,1,0:T(8,128)(2,1)S(1)} %fusion.29.q_ref, bf16[8,2,3,64,256]{4,3,2,1,0:T(8,128)(2,1)S(1)} %all-to-all-done.1.own_ref, bf16[8,2,3,64,256]{4,3,2,1,0:T(8,128)(2,1)S(1)} %collective-permute-done.8.other_ref), custom_call_target="tpu_custom_call" | custom-call | tf_op jit(solution)/shard_map/attention/pallas_call | solution.py:225
  223.0 2.9 fusion.82
  230.3 24.6 %all_to_all.35.own_ref = bf16[8,2,3,64,256]{4,3,2,1,0:T(8,128)(2,1)S(1)} all-to-all(bf16[8,2,3,64,256]{4,3,2,1,0:T(8,128)(2,1)S(1)} %broadcast_in_dim.21), channel_id=1, replica_groups={{0,16,32,48,64,80,96,112},{8,24,40,56,72,88,104,120},{1,17,33,49,65,81,..., dimensions={0} | all-to-all | bytes 3145728 | tf_op jit(solution)/shard_map/all_to_all | solution.py:41
  258.9 3.4 reshape.335
  262.4 2.9 slice.347
  269.1 16.5 %attention.3 = (f32[9,64,256]{2,1,0:T(8,128)S(1)}, f32[3,2,1,384]{3,2,1,0:T(1,128)S(1)}) custom-call(s32[39]{0:T(128)S(1)} %concatenate.93.sc, bf16[9,64,256]{2,1,0:T(8,128)(2,1)S(1)} %fusion.26.q_ref, bf16[8,2,3,64,256]{4,3,2,1,0:T(8,128)(2,1)S(1)} %all_to_all.35.own_ref, bf16[8,2,3,64,256]{4,3,2,1,0:T(8,128)(2,1)} %collective-permute-done.12.other_ref), custom_call_target="tpu_custom_call" | custom-call | tf_op jit(solution)/shard_map/attention/pallas_call | solution.py:225
  294.7 2.7 multiply_reduce_fusion
  298.0 22.9 %attention_back.2 = (f32[9,64,256]{2,1,0:T(8,128)S(1)}, bf16[8,2,3,64,256]{4,3,2,1,0:T(8,128)(2,1)S(1)}, bf16[8,2,3,64,256]{4,3,2,1,0:T(8,128)(2,1)S(1)}) custom-call(s32[39]{0:T(128)S(1)} %concatenate.93.sc, bf16[9,64,256]{2,1,0:T(8,128)(2,1)S(1)} %fusion.26.q_ref, bf16[8,2,3,64,256]{4,3,2,1,0:T(8,128)(2,1)S(1)} %all_to_all.35.own_ref, ...), custom_call_target="tpu_custom_call" | custom-call | tf_op jit(solution)/shard_map/attention_back/pallas_call | solution.py:248
  327.1 4.4 all-to-all-start.4
  335.9 2.5 add_convert_fusion.4
  340.6 3.2 reshape.342
  343.9 12.1 %all-to-all-done.4 = bf16[8,2,3,64,256]{4,3,2,1,0:T(8,128)(2,1)} async-done(((bf16[8,2,3,64,256]{4,3,2,1,0:T(8,128)(2,1)}), bf16[8,2,3,64,256]{4,3,2,1,0:T(8,128)(2,1)}, u32[]{:S(2)}, u32[]{:S(2)}) %all-to-all-start.4) | async-done | bytes 1572896 | tf_op jit(solution)/shard_map/all_to_all | solution.py:41
  379.5 3.5 add_convert_fusion
  383.0 22.7 %attention_back.3 = (f32[9,64,256]{2,1,0:T(8,128)S(1)}, bf16[8,2,3,64,256]{4,3,2,1,0:T(8,128)(2,1)S(1)}, bf16[8,2,3,64,256]{4,3,2,1,0:T(8,128)(2,1)}) custom-call(s32[39]{0:T(128)S(1)} %concatenate.93.sc, bf16[9,64,256]{2,1,0:T(8,128)(2,1)S(1)} %fusion.29.q_ref, bf16[8,2,3,64,256]{4,3,2,1,0:T(8,128)(2,1)S(1)} %all-to-all-done.1.own_ref, ...), custom_call_target="tpu_custom_call" | custom-call | tf_op jit(solution)/shard_map/attention_back/pallas_call | solution.py:248
  410.1 6.1 concatenate.119
  427.4 95.0 %dispatch.1 = (bf16[72,2592]{1,0:T(8,128)(2,1)}, bf16[72,2592]{1,0:T(8,128)(2,1)}, bf16[72,2592]{1,0:T(8,128)(2,1)}, bf16[72,2592]{1,0:T(8,128)(2,1)}, bf16[72,2...) custom-call(s32[1]{0:T(128)} %bitcast.17.me, ...), custom_call_target="tpu_custom_call" | custom-call | tf_op jit(solution)/shard_map/dispatch/pallas_call | solution.py:321
  524.2 2.4 collective-permute-start.26
  526.7 3.7 collective-permute-start.28
  530.5 3.4 collective-permute-done.25
  533.9 5.9 collective-permute-start.30
  539.8 4.5 collective-permute-done.26
  544.3 3.4 collective-permute-start.31
  547.7 3.1 add_convert_fusion.2
  550.9 3.7 all-to-all-start.5
  554.6 2.7 collective-permute-done.29
  557.3 21.0 %collective-permute-done.30 = bf16[72,2592]{1,0:T(8,128)(2,1)} collective-permute-done((bf16[72,2592]{1,0:T(8,128)(2,1)}, bf16[72,2592]{1,0:T(8,128)(2,1)}, u32[]{:S(2)}, u32[]{:S(2)}) %collective-permute-start.30) | collective-permute-done | bytes 373280 | tf_op jit(solution)/shard_map/ppermute | solution.py:336
  580.5 2.9 collective-permute-start.32
  585.1 5.6 collective-permute-done.32
  594.3 2.6 collective-permute-start.17
  603.5 10.7 %all-to-all-start.6 = ((bf16[8,72,484]{2,1,0:T(8,128)(2,1)}), bf16[8,72,484]{2,1,0:T(8,128)(2,1)S(1)}, u32[]{:S(2)}, u32[]{:S(2)}) async-start(bf16[8,72,484]{2,1,0:T(8,128)(2,1)} %bitcast.41), calls=%async_computation.6 | async-start | bytes 1179648 | tf_op jit(solution)/shard_map/all_to_all | solution.py:45
  615.3 11.1 %all-to-all-done.6 = bf16[8,72,484]{2,1,0:T(8,128)(2,1)S(1)} async-done(((bf16[8,72,484]{2,1,0:T(8,128)(2,1)}), bf16[8,72,484]{2,1,0:T(8,128)(2,1)S(1)}, u32[]{:S(2)}, u32[]{:S(2)}) %all-to-all-start.6) | async-done | bytes 557600 | tf_op jit(solution)/shard_map/all_to_all | solution.py:45
  626.7 4.6 collective-permute-done.40
  636.6 4.3 collective-permute-done.41
  641.0 2.6 collective-permute-start.42
  645.2 9.7 %collective-permute-done.42 = bf16[72,3072]{1,0:T(8,128)(2,1)S(1)} collective-permute-done((bf16[72,3072]{1,0:T(8,128)(2,1)S(1)}, bf16[72,3072]{1,0:T(8,128)(2,1)S(1)}, u32[]{:S(2)}, u32[]{:S(2)}) %collective-permute-start.42) | collective-permute-done | bytes 442400 | tf_op jit(solution)/shard_map/ppermute | solution.py:63
  655.0 3.5 collective-permute-start.43
  (453 shorter events, 146.3 us)
Async XLA Ops:
  10.9 25.3 %all-to-all-start = ((bf16[8,72,772]{2,1,0:T(8,128)(2,1)}), bf16[8,72,772]{2,1,0:T(8,128)(2,1)S(1)}, u32[]{:S(2)}, u32[]{:S(2)}) async-start(bf16[8,72,772]{2,1,0:T(8,128)(2,1)} %broadcast_in_dim.16), calls=%async_computation | async-start | bytes 2064384 | tf_op jit(solution)/shard_map/all_to_all | solution.py:45
  44.3 53.1 %all-to-all-start.1 = ((bf16[8,2,3,64,256]{4,3,2,1,0:T(8,128)(2,1)}), bf16[8,2,3,64,256]{4,3,2,1,0:T(8,128)(2,1)S(1)}, u32[]{:S(2)}, u32[]{:S(2)}) async-start(bf16[8,2,3,64,256]{4,3,2,1,0:T(8,128)(2,1)} %broadcast_in_dim.19), calls=%async_computation.1 | async-start | bytes 3145728 | tf_op jit(solution)/shard_map/all_to_all | solution.py:41
  50.1 8.8 %collective-permute-start.1 = (bf16[72,2304]{1,0:T(8,128)(2,1)S(1)}, bf16[72,2304]{1,0:T(8,128)(2,1)S(1)}, u32[]{:S(2)}, u32[]{:S(2)}) collective-permute-start(bf16[72,2304]{1,0:T(8,128)(2,1)S(1)} %constant_dynamic-update-slice_fusion.refs_0_), channel_id=1, source_target_pairs={{0,1},{1,0},{2,3},{3,2},{4,5},{5,4},{6,7},{7,6},{8,9},{9,8},{10,11... | collective-permute-start | bytes 995336 | tf_op jit(solution)/shard_map/ppermute | solution.py:336
  50.7 15.3 %collective-permute-start.2 = (bf16[72,2304]{1,0:T(8,128)(2,1)S(1)}, bf16[72,2304]{1,0:T(8,128)(2,1)S(1)}, u32[]{:S(2)}, u32[]{:S(2)}) collective-permute-start(bf16[72,2304]{1,0:T(8,128)(2,1)S(1)} %constant_dynamic-update-slice_fusion.refs_0_), channel_id=1, source_target_pairs={{0,2},{1,3},{2,0},{3,1},{4,6},{5,7},{6,4},{7,5},{8,10},{9,11},{10,... | collective-permute-start | bytes 995336 | tf_op jit(solution)/shard_map/ppermute | solution.py:336
  51.6 17.4 %collective-permute-start.3 = (bf16[72,2304]{1,0:T(8,128)(2,1)S(1)}, bf16[72,2304]{1,0:T(8,128)(2,1)S(1)}, u32[]{:S(2)}, u32[]{:S(2)}) collective-permute-start(bf16[72,2304]{1,0:T(8,128)(2,1)S(1)} %constant_dynamic-update-slice_fusion.refs_0_), channel_id=1, source_target_pairs={{0,3},{1,2},{2,1},{3,0},{4,7},{5,6},{6,5},{7,4},{8,11},{9,10},{10,... | collective-permute-start | bytes 995336 | tf_op jit(solution)/shard_map/ppermute | solution.py:336
  54.0 41.9 %collective-permute-start.4 = (bf16[72,2304]{1,0:T(8,128)(2,1)S(1)}, bf16[72,2304]{1,0:T(8,128)(2,1)S(1)}, u32[]{:S(2)}, u32[]{:S(2)}) collective-permute-start(bf16[72,2304]{1,0:T(8,128)(2,1)S(1)} %constant_dynamic-update-slice_fusion.refs_0_), channel_id=1, source_target_pairs={{0,4},{1,5},{2,6},{3,7},{4,0},{5,1},{6,2},{7,3},{8,12},{9,13},{10,... | collective-permute-start | bytes 995336 | tf_op jit(solution)/shard_map/ppermute | solution.py:336
  54.9 41.0 %collective-permute-start.5 = (bf16[72,2304]{1,0:T(8,128)(2,1)S(1)}, bf16[72,2304]{1,0:T(8,128)(2,1)S(1)}, u32[]{:S(2)}, u32[]{:S(2)}) collective-permute-start(bf16[72,2304]{1,0:T(8,128)(2,1)S(1)} %constant_dynamic-update-slice_fusion.refs_0_), channel_id=1, source_target_pairs={{0,5},{1,4},{2,7},{3,6},{4,1},{5,0},{6,3},{7,2},{8,13},{9,12},{10,... | collective-permute-start | bytes 995336 | tf_op jit(solution)/shard_map/ppermute | solution.py:336
  58.8 37.1 %collective-permute-start.6 = (bf16[72,2304]{1,0:T(8,128)(2,1)S(1)}, bf16[72,2304]{1,0:T(8,128)(2,1)S(1)}, u32[]{:S(2)}, u32[]{:S(2)}) collective-permute-start(bf16[72,2304]{1,0:T(8,128)(2,1)S(1)} %constant_dynamic-update-slice_fusion.refs_0_), channel_id=1, source_target_pairs={{0,6},{1,7},{2,4},{3,5},{4,2},{5,3},{6,0},{7,1},{8,14},{9,15},{10,... | collective-permute-start | bytes 995336 | tf_op jit(solution)/shard_map/ppermute | solution.py:336
  66.0 31.4 %collective-permute-start.7 = (bf16[72,2304]{1,0:T(8,128)(2,1)S(1)}, bf16[72,2304]{1,0:T(8,128)(2,1)}, u32[]{:S(2)}, u32[]{:S(2)}) collective-permute-start(bf16[72,2304]{1,0:T(8,128)(2,1)S(1)} %constant_dynamic-update-slice_fusion.refs_0_), channel_id=1, source_target_pairs={{0,7},{1,6},{2,5},{3,4},{4,3},{5,2},{6,1},{7,0},{8,15},{9,14},{10,... | collective-permute-start | bytes 995336 | tf_op jit(solution)/shard_map/ppermute | solution.py:336
  97.4 103.9 %collective-permute-start.8 = (bf16[8,2,3,64,256]{4,3,2,1,0:T(8,128)(2,1)S(1)}, bf16[8,2,3,64,256]{4,3,2,1,0:T(8,128)(2,1)S(1)}, u32[]{:S(2)}, u32[]{:S(2)}) collective-permute-start(bf16[8,2,3,64,256]{4,3,2,1,0:T(8,128)(2,1)S(1)} %all-to-all-done.1.own_ref), channel_id=1, source_target_pairs={{0,8},{8,0},{16,24},{24,16},{32,40},{40,32},{48,56},{56,48},{64,72... | collective-permute-start | bytes 4718600 | tf_op jit(solution)/shard_map/ppermute | solution.py:37
  100.6 100.6 %all-to-all-start.2 = ((bf16[8,72,768]{2,1,0:T(8,128)(2,1)}), bf16[8,72,768]{2,1,0:T(8,128)(2,1)}, u32[]{:S(2)}, u32[]{:S(2)}) async-start(bf16[8,72,768]{2,1,0:T(8,128)(2,1)} %broadcast_in_dim.20), calls=%async_computation.2 | async-start | bytes 1769472 | tf_op jit(solution)/shard_map/all_to_all | solution.py:45
  105.0 151.8 %all-gather.2.cloned.1.call-start = ((), (), s32[]{:S(2)}) async-start(), calls=%async_computation.8 | async-start | bytes 2985984 | tf_op jit(solution)/shard_map/all_gather | solution.py:442
  194.5 28.5 %collective-permute-start.9 = (bf16[576,1536]{1,0:T(8,128)(2,1)}, bf16[576,1536]{1,0:T(8,128)(2,1)}, u32[]{:S(2)}, u32[]{:S(2)}) collective-permute-start(bf16[576,1536]{1,0:T(8,128)(2,1)} %bitcast.183), channel_id=1, source_target_pairs={{0,8},{8,0},{16,24},{24,16},{32,40},{40,32},{48,56},{56,48},{64,72... | collective-permute-start | bytes 5308424 | tf_op jit(solution)/shard_map/ppermute | solution.py:37
  200.2 26.0 %collective-permute-start.10 = (bf16[768,576]{0,1:T(8,128)(2,1)}, bf16[768,576]{0,1:T(8,128)(2,1)}, u32[]{:S(2)}, u32[]{:S(2)}) collective-permute-start(bf16[768,576]{0,1:T(8,128)(2,1)} %copy.69), channel_id=1, source_target_pairs={{0,8},{8,0},{16,24},{24,16},{32,40},{40,32},{48,56},{56,48},{64,72... | collective-permute-start | bytes 2654216 | tf_op jit(solution)/shard_map/ppermute | solution.py:37
  201.2 20.5 %collective-permute-start.11 = (bf16[576,768]{1,0:T(8,128)(2,1)}, bf16[576,768]{1,0:T(8,128)(2,1)S(1)}, u32[]{:S(2)}, u32[]{:S(2)}) collective-permute-start(bf16[576,768]{1,0:T(8,128)(2,1)} %bitcast.19), channel_id=1, source_target_pairs={{0,8},{8,0},{16,24},{24,16},{32,40},{40,32},{48,56},{56,48},{64,72... | collective-permute-start | bytes 2654216 | tf_op jit(solution)/shard_map/ppermute | solution.py:37
  254.9 14.3 %collective-permute-start.12 = (bf16[8,2,3,64,256]{4,3,2,1,0:T(8,128)(2,1)S(1)}, bf16[8,2,3,64,256]{4,3,2,1,0:T(8,128)(2,1)}, u32[]{:S(2)}, u32[]{:S(2)}) collective-permute-start(bf16[8,2,3,64,256]{4,3,2,1,0:T(8,128)(2,1)S(1)} %all_to_all.35.own_ref), channel_id=1, source_target_pairs={{0,8},{8,0},{16,24},{24,16},{32,40},{40,32},{48,56},{56,48},{64,72... | collective-permute-start | bytes 4718600 | tf_op jit(solution)/shard_map/ppermute | solution.py:37
  265.3 26.2 %collective-permute-start.13 = (bf16[576,1536]{1,0:T(8,128)(2,1)}, bf16[576,1536]{1,0:T(8,128)(2,1)}, u32[]{:S(2)}, u32[]{:S(2)}) collective-permute-start(bf16[576,1536]{1,0:T(8,128)(2,1)} %slice.347), channel_id=1, source_target_pairs={{0,8},{8,0},{16,24},{24,16},{32,40},{40,32},{48,56},{56,48},{64,72... | collective-permute-start | bytes 5308424 | tf_op jit(solution)/shard_map/ppermute | solution.py:37
  267.5 26.2 %collective-permute-start.14 = (bf16[768,576]{0,1:T(8,128)(2,1)}, bf16[768,576]{0,1:T(8,128)(2,1)S(1)}, u32[]{:S(2)}, u32[]{:S(2)}) collective-permute-start(bf16[768,576]{0,1:T(8,128)(2,1)} %copy.70), channel_id=1, source_target_pairs={{0,8},{8,0},{16,24},{24,16},{32,40},{40,32},{48,56},{56,48},{64,72... | collective-permute-start | bytes 2654216 | tf_op jit(solution)/shard_map/ppermute | solution.py:37
  323.3 12.7 %collective-permute-start.37 = (bf16[768,576]{0,1:T(8,128)(2,1)}, bf16[768,576]{0,1:T(8,128)(2,1)}, u32[]{:S(2)}, u32[]{:S(2)}) collective-permute-start(bf16[768,576]{0,1:T(8,128)(2,1)} %convolution_convert_fusion.6), channel_id=1, source_target_pairs={{0,8},{8,0},{16,24},{24,16},{32,40},{40,32},{48,56},{56,48},{64,72... | collective-permute-start | bytes 2654216 | tf_op jit(solution)/shard_map/ppermute | solution.py:37
  327.1 28.9 %all-to-all-start.4 = ((bf16[8,2,3,64,256]{4,3,2,1,0:T(8,128)(2,1)}), bf16[8,2,3,64,256]{4,3,2,1,0:T(8,128)(2,1)}, u32[]{:S(2)}, u32[]{:S(2)}) async-start(bf16[8,2,3,64,256]{4,3,2,1,0:T(8,128)(2,1)} %add_convert_fusion.3), calls=%async_computation.4 | async-start | bytes 3145728 | tf_op jit(solution)/shard_map/all_to_all | solution.py:41
  331.6 282.6 %reduce-scatter.2.cloned.1.call-start = ((), (), s32[]{:S(2)}) async-start(), calls=%async_computation.9 | async-start | bytes 3981312 | tf_op jit(solution)/shard_map/reduce_scatter | solution.py:567
  334.7 44.8 %collective-permute-start.36 = (bf16[576,1536]{1,0:T(8,128)(2,1)}, bf16[576,1536]{1,0:T(8,128)(2,1)}, u32[]{:S(2)}, u32[]{:S(2)}) collective-permute-start(bf16[576,1536]{1,0:T(8,128)(2,1)} %convolution_convert_fusion), channel_id=1, source_target_pairs={{0,8},{8,0},{16,24},{24,16},{32,40},{40,32},{48,56},{56,48},{64,72... | collective-permute-start | bytes 5308424 | tf_op jit(solution)/shard_map/ppermute | solution.py:37
  376.0 47.5 %collective-permute-start.22 = (bf16[576,1536]{1,0:T(8,128)(2,1)}, bf16[576,1536]{1,0:T(8,128)(2,1)}, u32[]{:S(2)}, u32[]{:S(2)}) collective-permute-start(bf16[576,1536]{1,0:T(8,128)(2,1)} %convolution_convert_fusion.2), channel_id=1, source_target_pairs={{0,8},{8,0},{16,24},{24,16},{32,40},{40,32},{48,56},{56,48},{64,72... | collective-permute-start | bytes 5308424 | tf_op jit(solution)/shard_map/ppermute | solution.py:37
  377.0 39.2 %collective-permute-start.23 = (bf16[768,576]{0,1:T(8,128)(2,1)}, bf16[768,576]{0,1:T(8,128)(2,1)}, u32[]{:S(2)}, u32[]{:S(2)}) collective-permute-start(bf16[768,576]{0,1:T(8,128)(2,1)} %convolution_convert_fusion.8), channel_id=1, source_target_pairs={{0,8},{8,0},{16,24},{24,16},{32,40},{40,32},{48,56},{56,48},{64,72... | collective-permute-start | bytes 2654216 | tf_op jit(solution)/shard_map/ppermute | solution.py:37
  378.0 29.3 %collective-permute-start.24 = (bf16[576,288]{1,0:T(8,128)(2,1)S(1)}, bf16[576,288]{1,0:T(8,128)(2,1)S(1)}, u32[]{:S(2)}, u32[]{:S(2)}) collective-permute-start(bf16[576,288]{1,0:T(8,128)(2,1)S(1)} %broadcast_select_fusion.7), channel_id=1, source_target_pairs={{0,8},{8,0},{16,24},{24,16},{32,40},{40,32},{48,56},{56,48},{64,72... | collective-permute-start | bytes 995336 | tf_op jit(solution)/shard_map/ppermute | solution.py:37
  379.4 29.0 %collective-permute-start.39 = (bf16[576,480]{1,0:T(8,128)(2,1)S(1)}, bf16[576,480]{1,0:T(8,128)(2,1)S(1)}, u32[]{:S(2)}, u32[]{:S(2)}) collective-permute-start(bf16[576,480]{1,0:T(8,128)(2,1)S(1)} %broadcast_select_fusion.4), channel_id=1, source_target_pairs={{0,8},{8,0},{16,24},{24,16},{32,40},{40,32},{48,56},{56,48},{64,72... | collective-permute-start | bytes 1658888 | tf_op jit(solution)/shard_map/ppermute | solution.py:37
  406.9 123.5 %collective-permute-start.16 = (bf16[8,2,3,64,256]{4,3,2,1,0:T(8,128)(2,1)}, bf16[8,2,3,64,256]{4,3,2,1,0:T(8,128)(2,1)}, u32[]{:S(2)}, u32[]{:S(2)}) collective-permute-start(bf16[8,2,3,64,256]{4,3,2,1,0:T(8,128)(2,1)} %get-tuple-element.67), channel_id=1, source_target_pairs={{0,8},{8,0},{16,24},{24,16},{32,40},{40,32},{48,56},{56,48},{64,72... | collective-permute-start | bytes 4718600 | tf_op jit(solution)/shard_map/ppermute | solution.py:37
  522.3 11.5 %collective-permute-start.25 = (bf16[72,2592]{1,0:T(8,128)(2,1)}, bf16[72,2592]{1,0:T(8,128)(2,1)S(1)}, u32[]{:S(2)}, u32[]{:S(2)}) collective-permute-start(bf16[72,2592]{1,0:T(8,128)(2,1)} %get-tuple-element.73), channel_id=1, source_target_pairs={{0,1},{1,0},{2,3},{3,2},{4,5},{5,4},{6,7},{7,6},{8,9},{9,8},{10,11... | collective-permute-start | bytes 1119752 | tf_op jit(solution)/shard_map/ppermute | solution.py:336
  524.2 20.1 %collective-permute-start.26 = (bf16[72,2592]{1,0:T(8,128)(2,1)}, bf16[72,2592]{1,0:T(8,128)(2,1)S(1)}, u32[]{:S(2)}, u32[]{:S(2)}) collective-permute-start(bf16[72,2592]{1,0:T(8,128)(2,1)} %get-tuple-element.74), channel_id=1, source_target_pairs={{0,2},{1,3},{2,0},{3,1},{4,6},{5,7},{6,4},{7,5},{8,10},{9,11},{10,... | collective-permute-start | bytes 1119752 | tf_op jit(solution)/shard_map/ppermute | solution.py:336
  526.6 28.0 %collective-permute-start.27 = (bf16[72,2592]{1,0:T(8,128)(2,1)}, bf16[72,2592]{1,0:T(8,128)(2,1)}, u32[]{:S(2)}, u32[]{:S(2)}) collective-permute-start(bf16[72,2592]{1,0:T(8,128)(2,1)} %get-tuple-element.75), channel_id=1, source_target_pairs={{0,3},{1,2},{2,1},{3,0},{4,7},{5,6},{6,5},{7,4},{8,11},{9,10},{10,... | collective-permute-start | bytes 1119752 | tf_op jit(solution)/shard_map/ppermute | solution.py:336
  526.7 27.9 %collective-permute-start.28 = (bf16[72,2592]{1,0:T(8,128)(2,1)}, bf16[72,2592]{1,0:T(8,128)(2,1)}, u32[]{:S(2)}, u32[]{:S(2)}) collective-permute-start(bf16[72,2592]{1,0:T(8,128)(2,1)} %get-tuple-element.76), channel_id=1, source_target_pairs={{0,4},{1,5},{2,6},{3,7},{4,0},{5,1},{6,2},{7,3},{8,12},{9,13},{10,... | collective-permute-start | bytes 1119752 | tf_op jit(solution)/shard_map/ppermute | solution.py:336
  530.5 26.8 %collective-permute-start.29 = (bf16[72,2592]{1,0:T(8,128)(2,1)}, bf16[72,2592]{1,0:T(8,128)(2,1)}, u32[]{:S(2)}, u32[]{:S(2)}) collective-permute-start(bf16[72,2592]{1,0:T(8,128)(2,1)} %get-tuple-element.77), channel_id=1, source_target_pairs={{0,5},{1,4},{2,7},{3,6},{4,1},{5,0},{6,3},{7,2},{8,13},{9,12},{10,... | collective-permute-start | bytes 1119752 | tf_op jit(solution)/shard_map/ppermute | solution.py:336
  533.9 44.5 %collective-permute-start.30 = (bf16[72,2592]{1,0:T(8,128)(2,1)}, bf16[72,2592]{1,0:T(8,128)(2,1)}, u32[]{:S(2)}, u32[]{:S(2)}) collective-permute-start(bf16[72,2592]{1,0:T(8,128)(2,1)} %get-tuple-element.78), channel_id=1, source_target_pairs={{0,6},{1,7},{2,4},{3,5},{4,2},{5,3},{6,0},{7,1},{8,14},{9,15},{10,... | collective-permute-start | bytes 1119752 | tf_op jit(solution)/shard_map/ppermute | solution.py:336
  544.3 34.0 %collective-permute-start.31 = (bf16[72,2592]{1,0:T(8,128)(2,1)}, bf16[72,2592]{1,0:T(8,128)(2,1)}, u32[]{:S(2)}, u32[]{:S(2)}) collective-permute-start(bf16[72,2592]{1,0:T(8,128)(2,1)} %get-tuple-element.79), channel_id=1, source_target_pairs={{0,7},{1,6},{2,5},{3,4},{4,3},{5,2},{6,1},{7,0},{8,15},{9,14},{10,... | collective-permute-start | bytes 1119752 | tf_op jit(solution)/shard_map/ppermute | solution.py:336
  550.9 40.6 %all-to-all-start.5 = ((bf16[8,2,3,64,256]{4,3,2,1,0:T(8,128)(2,1)}), bf16[8,2,3,64,256]{4,3,2,1,0:T(8,128)(2,1)S(1)}, u32[]{:S(2)}, u32[]{:S(2)}) async-start(bf16[8,2,3,64,256]{4,3,2,1,0:T(8,128)(2,1)} %add_convert_fusion.2), calls=%async_computation.5 | async-start | bytes 3145728 | tf_op jit(solution)/shard_map/all_to_all | solution.py:41
  580.5 10.1 %collective-permute-start.32 = (bf16[72,2592]{1,0:T(8,128)(2,1)S(1)}, bf16[72,2592]{1,0:T(8,128)(2,1)S(1)}, u32[]{:S(2)}, u32[]{:S(2)}) collective-permute-start(bf16[72,2592]{1,0:T(8,128)(2,1)S(1)} %add_convert_fusion.16), channel_id=1, source_target_pairs={{0,16},{8,24},{16,0},{24,8},{32,48},{40,56},{48,32},{56,40},{64,80... | collective-permute-start | bytes 1119752 | tf_op jit(solution)/shard_map/ppermute | solution.py:63
  590.7 7.4 %collective-permute-start.33 = (bf16[72,2592]{1,0:T(8,128)(2,1)S(1)}, bf16[72,2592]{1,0:T(8,128)(2,1)}, u32[]{:S(2)}, u32[]{:S(2)}) collective-permute-start(bf16[72,2592]{1,0:T(8,128)(2,1)S(1)} %add_convert_fusion.15), channel_id=1, source_target_pairs={{0,32},{8,40},{16,48},{24,56},{32,0},{40,8},{48,16},{56,24},{64,96... | collective-permute-start | bytes 1119752 | tf_op jit(solution)/shard_map/ppermute | solution.py:63
  594.3 7.8 %collective-permute-start.17 = (bf16[576,480]{1,0:T(8,128)(2,1)}, bf16[576,480]{1,0:T(8,128)(2,1)S(1)}, u32[]{:S(2)}, u32[]{:S(2)}) collective-permute-start(bf16[576,480]{1,0:T(8,128)(2,1)} %broadcast_select_fusion.5), channel_id=1, source_target_pairs={{0,8},{8,0},{16,24},{24,16},{32,40},{40,32},{48,56},{56,48},{64,72... | collective-permute-start | bytes 1658888 | tf_op jit(solution)/shard_map/ppermute | solution.py:37
  599.2 32.7 %collective-permute-start.34 = (bf16[72,2592]{1,0:T(8,128)(2,1)S(1)}, bf16[72,2592]{1,0:T(8,128)(2,1)}, u32[]{:S(2)}, u32[]{:S(2)}) collective-permute-start(bf16[72,2592]{1,0:T(8,128)(2,1)S(1)} %add_convert_fusion.14), channel_id=1, source_target_pairs={{0,64},{8,72},{16,80},{24,88},{32,96},{40,104},{48,112},{56,120},{... | collective-permute-start | bytes 1119752 | tf_op jit(solution)/shard_map/ppermute | solution.py:63
  603.5 23.0 %all-to-all-start.6 = ((bf16[8,72,484]{2,1,0:T(8,128)(2,1)}), bf16[8,72,484]{2,1,0:T(8,128)(2,1)S(1)}, u32[]{:S(2)}, u32[]{:S(2)}) async-start(bf16[8,72,484]{2,1,0:T(8,128)(2,1)} %bitcast.41), calls=%async_computation.6 | async-start | bytes 1179648 | tf_op jit(solution)/shard_map/all_to_all | solution.py:45
  614.2 17.0 %collective-permute-start.40 = (bf16[72,3072]{1,0:T(8,128)(2,1)}, bf16[72,3072]{1,0:T(8,128)(2,1)S(1)}, u32[]{:S(2)}, u32[]{:S(2)}) collective-permute-start(bf16[72,3072]{1,0:T(8,128)(2,1)} %reduce-scatter.2.cloned.1.call-done), channel_id=1, source_target_pairs={{0,16},{8,24},{16,0},{24,8},{32,48},{40,56},{48,32},{56,40},{64,80... | collective-permute-start | bytes 1327112 | tf_op jit(solution)/shard_map/ppermute | solution.py:63
  626.6 8.7 %collective-permute-start.18 = (bf16[72,484]{1,0:T(8,128)(2,1)S(1)}, bf16[72,484]{1,0:T(8,128)(2,1)S(1)}, u32[]{:S(2)}, u32[]{:S(2)}) collective-permute-start(bf16[72,484]{1,0:T(8,128)(2,1)S(1)} %reduce_sum.162), channel_id=1, source_target_pairs={{0,16},{8,24},{16,0},{24,8},{32,48},{40,56},{48,32},{56,40},{64,80... | collective-permute-start | bytes 209096 | tf_op jit(solution)/shard_map/ppermute | solution.py:63
  631.4 9.6 %collective-permute-start.41 = (bf16[72,3072]{1,0:T(8,128)(2,1)S(1)}, bf16[72,3072]{1,0:T(8,128)(2,1)S(1)}, u32[]{:S(2)}, u32[]{:S(2)}) collective-permute-start(bf16[72,3072]{1,0:T(8,128)(2,1)S(1)} %add_convert_fusion.10), channel_id=1, source_target_pairs={{0,32},{8,40},{16,48},{24,56},{32,0},{40,8},{48,16},{56,24},{64,96... | collective-permute-start | bytes 1327112 | tf_op jit(solution)/shard_map/ppermute | solution.py:63
  633.0 10.6 %collective-permute-start.35 = (bf16[72,2592]{1,0:T(8,128)(2,1)S(1)}, bf16[72,2592]{1,0:T(8,128)(2,1)S(1)}, u32[]{:S(2)}, u32[]{:S(2)}) collective-permute-start(bf16[72,2592]{1,0:T(8,128)(2,1)S(1)} %add_convert_fusion.13.refs_0_), channel_id=1, source_target_pairs={{0,8},{8,0},{16,24},{24,16},{32,40},{40,32},{48,56},{56,48},{64,72... | collective-permute-start | bytes 1119752 | tf_op jit(solution)/shard_map/ppermute | solution.py:37
  635.3 8.9 %collective-permute-start.19 = (bf16[72,484]{1,0:T(8,128)(2,1)S(1)}, bf16[72,484]{1,0:T(8,128)(2,1)S(1)}, u32[]{:S(2)}, u32[]{:S(2)}) collective-permute-start(bf16[72,484]{1,0:T(8,128)(2,1)S(1)} %add_convert_fusion.21), channel_id=1, source_target_pairs={{0,32},{8,40},{16,48},{24,56},{32,0},{40,8},{48,16},{56,24},{64,96... | collective-permute-start | bytes 209096 | tf_op jit(solution)/shard_map/ppermute | solution.py:63
  641.0 13.8 %collective-permute-start.42 = (bf16[72,3072]{1,0:T(8,128)(2,1)S(1)}, bf16[72,3072]{1,0:T(8,128)(2,1)S(1)}, u32[]{:S(2)}, u32[]{:S(2)}) collective-permute-start(bf16[72,3072]{1,0:T(8,128)(2,1)S(1)} %add_convert_fusion.9), channel_id=1, source_target_pairs={{0,64},{8,72},{16,80},{24,88},{32,96},{40,104},{48,112},{56,120},{... | collective-permute-start | bytes 1327112 | tf_op jit(solution)/shard_map/ppermute | solution.py:63
  644.2 14.3 %collective-permute-start.20 = (bf16[72,484]{1,0:T(8,128)(2,1)S(1)}, bf16[72,484]{1,0:T(8,128)(2,1)S(1)}, u32[]{:S(2)}, u32[]{:S(2)}) collective-permute-start(bf16[72,484]{1,0:T(8,128)(2,1)S(1)} %add_convert_fusion.20), channel_id=1, source_target_pairs={{0,64},{8,72},{16,80},{24,88},{32,96},{40,104},{48,112},{56,120},{... | collective-permute-start | bytes 209096 | tf_op jit(solution)/shard_map/ppermute | solution.py:63
  655.0 5.9 collective-permute-start.43
  (114 other events, 761.3 us)
Sparse Core Ops, SparseCore 0:
  108.9 59.8 all-gather.1
  416.3 79.9 reduce-scatter.1
